TPU v7x, 128 devices: a whole 4x4x4 slice. The times are simulated.
128 devices in a mesh: queue: 8 (over z_lo, y), seq: 16 (over z_hi, x, core).
Axes of the slice: x: 4, y: 4, z: 4 (z_hi: 2, z_lo: 2; z = z_hi * 2 + z_lo), core: 2. Of those that a mesh axis runs over, the one named last changes fastest.
Arguments:
- latents: bfloat16 [8, 4, 128, 5120], P('queue', None, 'seq'), may hold values from -6 to 6
- steps: int32 [8], P('queue'), may hold values from 0 to 49
- leaving: int32 [8], P('queue'), may hold values from 0 to 3
- fresh: bfloat16 [128, 5120], P('seq'), may hold values from -6 to 6
- mod_table: float32 [50, 15360], replicated, may hold values from -4 to 4
- w_qkv: bfloat16 [5120, 3, 4096], P(None, None, 'seq'), may hold values from -0.078125 to 0.078125
- q_gain: float32 [4096], P('seq'), may hold values from 0.5 to 16
- k_gain: float32 [4096], P('seq'), may hold values from 0.5 to 16
- w_out: bfloat16 [4096, 5120], P('seq'), may hold values from -0.09375 to 0.09375
Outputs:
- queue_next: bfloat16 [8, 4, 128, 5120], P('queue', None, 'seq')
All inputs are finite; a program needn't handle non-finite values.
Results may differ from a plain program's by a relative error of at most 0.017.
Values may be sent and summed in bfloat16 or wider, within the bound.
No kernel may reach another device: no remote copies, remote signals or barrier semaphores. Data moves between devices by JAX's collectives and lax.ppermute only.
A program may use at most 128 MiB of HBM per device.

v0:
```python
import jax
import jax.numpy as jnp
from jax import lax
from jax.sharding import PartitionSpec as P

HEAD_DIM = 128


def from_behind(x, axis, by):
    count = lax.axis_size(axis)
    pairs = [(i, i + by) for i in range(count) if 0 <= i + by < count]
    return lax.ppermute(x, axis, pairs)


def layer_norm_mod(rows, shift, scale):
    values = rows.astype(jnp.float32)
    mean = jnp.mean(values, axis=-1, keepdims=True)
    centred = values - mean
    var = jnp.mean(centred * centred, axis=-1, keepdims=True)
    return (centred * lax.rsqrt(var + 1e-06) * (1.0 + scale) + shift).astype(jnp.bfloat16)


def head_norm(values, gain):
    power = jnp.mean(values * values, axis=-1, keepdims=True)
    return values * lax.rsqrt(power + 1e-06) * gain


def body(latents, steps, leaving, fresh, mod_table, w_qkv, q_gain, k_gain, w_out):
    parts_here, frames, local_rows, width = latents.shape
    seq_count = lax.axis_size("seq")
    frame_tok = local_rows * seq_count
    length = frames * frame_tok
    local_width = w_qkv.shape[2]
    local_heads = local_width // HEAD_DIM
    levels = mod_table.shape[0]
    onehot = (steps[:, None] == jnp.arange(levels)[None, :]).astype(jnp.float32)
    modrows = jnp.dot(onehot, mod_table, precision=lax.Precision.HIGHEST)
    shift = modrows[:, None, None, :width]
    scale = modrows[:, None, None, width : 2 * width]
    gate = modrows[:, None, None, 2 * width :]
    w_flat = w_qkv.reshape(width, 3 * local_width)
    q_scale = q_gain.reshape(local_heads, HEAD_DIM)
    k_scale = k_gain.reshape(local_heads, HEAD_DIM)
    normed = layer_norm_mod(lax.all_gather(latents, "seq", axis=2, tiled=True), shift, scale)
    count = normed.shape[2]
    qkv = jnp.dot(normed.reshape(-1, width), w_flat, preferred_element_type=jnp.float32)
    qkv = qkv.reshape(-1, 3, local_heads, HEAD_DIM)
    query = head_norm(qkv[:, 0], q_scale).astype(jnp.bfloat16)
    project_keys = head_norm(qkv[:, 1], k_scale).astype(jnp.bfloat16)
    project_values = qkv[:, 2].astype(jnp.bfloat16)
    joined = jnp.concatenate(
        [
            query.reshape(-1, local_width),
            project_keys.reshape(-1, local_width),
            project_values.reshape(-1, local_width),
        ],
        axis=1,
    )
    qkv_all = joined.reshape(parts_here, frames, count, 3 * local_width)
    qkv_all = qkv_all.reshape(parts_here, length, 3, local_heads, HEAD_DIM)
    block = min(512, length)
    blocks = length // block
    keys = qkv_all[0, :, 1]
    values = qkv_all[0, :, 2]
    queries = qkv_all[0, :, 0].reshape(blocks, block, local_heads, HEAD_DIM)

    def attend(query):
        scores = jnp.einsum(
            "qhd,khd->hqk", query, keys, preferred_element_type=jnp.float32
        ) * HEAD_DIM ** (-0.5)
        top = jnp.max(scores, axis=-1, keepdims=True)
        expo = jnp.exp(scores - top)
        total = jnp.sum(expo, axis=-1, keepdims=True)
        prob = (expo / total).astype(jnp.bfloat16)
        return jnp.einsum("hqk,khd->qhd", prob, values, preferred_element_type=jnp.float32).astype(
            jnp.bfloat16
        )

    outputs = [lax.map(attend, queries).reshape(frames, frame_tok, local_width)]
    attn = jnp.stack(outputs, axis=0)
    arranged = attn.transpose(2, 0, 1, 3).reshape(frame_tok, parts_here * frames, local_width)
    product = jnp.dot(arranged.reshape(-1, local_width), w_out, preferred_element_type=jnp.float32)
    proj = lax.psum_scatter(
        product.reshape(local_rows * lax.axis_size("seq"), parts_here * frames, width).astype(
            jnp.bfloat16
        ),
        "seq",
        scatter_dimension=0,
        tiled=True,
    ).astype(jnp.float32)
    proj = proj.reshape(local_rows, parts_here, frames, width).transpose(1, 2, 0, 3)
    updated = (latents.astype(jnp.float32) + gate * proj).astype(jnp.bfloat16)
    select = jnp.arange(frames)[None, :] == leaving[:, None]
    handed = jnp.sum(
        jnp.where(select[:, :, None, None], updated.astype(jnp.float32), 0.0), axis=1
    ).astype(jnp.bfloat16)
    arriving = from_behind(handed[parts_here - 1], "queue", 1)
    first = jnp.where(lax.axis_index("queue") == 0, fresh, arriving)
    incoming = jnp.concatenate([first[None], handed[:-1]], axis=0)
    return jnp.where(select[:, :, None, None], incoming[:, None], updated)


def solution(mesh):
    return jax.shard_map(
        body,
        mesh=mesh,
        in_specs=(
            P("queue", None, "seq", None),
            P("queue"),
            P("queue"),
            P("seq", None),
            P(),
            P(None, None, "seq"),
            P("seq"),
            P("seq"),
            P("seq", None),
        ),
        out_specs=P("queue", None, "seq", None),
        check_vma=False,
    )
```

profile of v0, /device:TPU:96, one launch (start us, length us, event | category | flops | bytes accessed | tf_op | source)
XLA Modules:
  0.0 202.3 jit_solution(11046667841524267325)
XLA Ops:
  6.5 0.0 copy-start
  6.5 0.0 all-gather.2.cloned.1.call-start
  6.5 0.7 all-gather.2.cloned.1.call-update
  7.3 0.0 reduce-scatter.4.cloned.1.call-start
  8.2 10.8 %copy.18 = bf16[5120,3,256]{0,2,1:T(8,128)(2,1)} copy(bf16[5120,3,256]{2,0,1:T(8,128)(2,1)} %param.14) | data formatting | bytes 15728640 | tf_op args[5]
  19.0 0.0 copy-done
  19.0 1.2 fusion.25
  20.3 49.0 %all-gather.2.cloned.1.call-done = bf16[1,4,128,5120]{3,2,1,0:T(8,128)(2,1)} async-done(((bf16[1,4,8,5120]{3,2,1,0:T(8,128)(2,1)}), bf16[1,4,128,5120]{3,2,1,0:T(8,128)(2,1)}) %all-gather.2.cloned.1.call-update) | async-done | bytes 5242896 | tf_op jit(solution)/shard_map/all_gather | solution.py:44
  69.3 0.0 copy-start.1
  69.3 3.4 %convert_reduce_fusion = f32[4,128]{1,0:T(4,128)S(1)} fusion(bf16[1,4,128,5120]{3,2,1,0:T(8,128)(2,1)} %all-gather.2.cloned.1.call-done), kind=kLoop, calls=%fused_computation.2 | loop fusion | flops 5242368 | bytes 5244928 | tf_op jit(solution)/shard_map/reduce_sum | solution.py:17
  72.7 0.6 copy-done.1
  73.3 0.0 slice-start
  73.3 1.5 fusion.3
  74.8 0.0 slice-start.1
  74.8 3.0 %fusion.6 = bf16[1,4,128,5120]{3,2,1,0:T(8,128)(2,1)S(1)} fusion(bf16[1,4,128,5120]{3,2,1,0:T(8,128)(2,1)S(1)} %copy-done.1, f32[5120]{0:T(1024)S(1)} %bitcast.120, f32[5120]{0:T(1024)S(1)} %bitcast.119, f32[4,128]{1,0:T(4,128)S(1)} %add_rsqrt_fusion.2, f32[4,128]{1,0:T(4,128)S(1)} %broadcast_multiply_fusion), kind=kLoop, calls=%fused_computation.8 | loop fusion | flops 15728640 | bytes 10530816 | tf_op jit(solution)/shard_map/convert_element_type | solution.py:20
  77.9 0.0 slice-done
  77.9 0.0 slice-done.1
  77.9 0.0 copy-start.3
  77.9 0.0 copy-start.4
  77.9 4.2 %fusion.36 = f32[512,3,2,128]{0,3,2,1:T(8,128)S(1)} fusion(bf16[512,5120,1,1]{1,0,3,2:T(8,128)(2,1)S(1)} %bitcast.111, bf16[3,2,128,5120]{3,2,1,0:T(8,128)(2,1)S(1)} %bitcast.110), kind=kOutput, calls=%fused_computation.57 | convolution fusion | flops 4026531840 | bytes 14680064 | tf_op jit(solution)/shard_map/dot_general | solution.py:46
  82.2 0.2 multiply_reduce_fusion.2
  82.4 0.0 copy-done.3
  82.4 0.0 copy-done.4
  82.4 0.1 fusion.16
  82.6 0.9 pad_maximum_fusion
  83.5 1.9 fusion.35
  85.4 3.1 %fusion.10 = bf16[512,2,128]{0,2,1:T(8,128)(2,1)} fusion(f32[2,512]{1,0:T(2,128)S(1)} %fusion.35, bf16[1,512,3,2,128]{1,4,3,2,0:T(8,128)(2,1)} %bitcast.116), kind=kOutput, calls=%fused_computation.17 | convolution fusion | flops 270665216 | bytes 1052672 | tf_op jit(solution)/shard_map/while/body/eval_jaxpr/hqk,khd->qhd/dot_general | solution.py:75
  88.5 1.7 stack_reshape.3
  90.2 1.8 copy.22
  92.0 3.4 %fusion.7 = bf16[4,16,8,5120]{3,2,1,0:T(8,128)(2,1)S(1)} fusion(bf16[256,5120]{1,0:T(8,128)(2,1)} %param.17, bf16[1,4,128,256]{3,2,1,0:T(8,128)(2,1)} %copy.22), kind=kOutput, calls=%fused_computation.10 | convolution fusion | flops 1344798720 | bytes 8126464 | tf_op jit(solution)/shard_map/dot_general | solution.py:82
  95.4 2.8 %copy.29 = bf16[4,16,8,5120]{3,2,0,1:T(8,128)(2,1)} copy(bf16[4,16,8,5120]{3,2,1,0:T(8,128)(2,1)S(1)} %fusion.7) | data formatting | bytes 10485760
  98.2 0.0 copy-start.2
  98.2 0.0 reduce-scatter.4.cloned.1.call-update
  98.9 83.1 %reduce-scatter.4.cloned.1.call-done = bf16[8,20480]{1,0:T(8,128)(2,1)} async-done(((bf16[128,20480]{1,0:T(8,128)(2,1)}), bf16[8,20480]{1,0:T(8,128)(2,1)}) %reduce-scatter.4.cloned.1.call-update) | async-done | bytes 327696
  182.0 1.9 select_reduce_fusion
  183.9 3.4 %collective-permute-start = (bf16[8,5120]{1,0:T(8,128)(2,1)}, bf16[8,5120]{1,0:T(8,128)(2,1)}, u32[]{:S(2)}, u32[]{:S(2)}) collective-permute-start(bf16[8,5120]{1,0:T(8,128)(2,1)} %select_reduce_fusion), channel_id=1, source_target_pairs={{0,16},{16,32},{32,48},{48,64},{64,80},{80,96},{96,112},{1,17},{17... | collective-permute-start | bytes 245768 | tf_op jit(solution)/shard_map/ppermute | solution.py:12
  187.3 5.4 %collective-permute-done = bf16[8,5120]{1,0:T(8,128)(2,1)} collective-permute-done((bf16[8,5120]{1,0:T(8,128)(2,1)}, bf16[8,5120]{1,0:T(8,128)(2,1)}, u32[]{:S(2)}, u32[]{:S(2)}) %collective-permute-start) | collective-permute-done | bytes 81952 | tf_op jit(solution)/shard_map/ppermute | solution.py:12
  192.6 0.0 copy-done.2
  192.6 0.9 broadcast_select_fusion.1
  193.5 1.9 broadcast_select_fusion
  (8 shorter events, 0.1 us)
Async XLA Ops:
  6.5 12.5 %copy-start = (f32[50,15360]{1,0:T(8,128)S(1)}, f32[50,15360]{1,0:T(8,128)}, u32[]{:S(2)}) copy-start(f32[50,15360]{1,0:T(8,128)} %param.13) | copy-start | bytes 9216004
  6.5 62.7 %all-gather.2.cloned.1.call-start = ((), (), s32[]{:S(2)}) async-start(), calls=%async_computation.1 | async-start | bytes 5570560 | tf_op jit(solution)/shard_map/all_gather | solution.py:44
  7.3 174.7 %reduce-scatter.4.cloned.1.call-start = ((), (), s32[]{:S(2)}) async-start(), calls=%async_computation.2 | async-start | bytes 5570560
  69.3 4.0 %copy-start.1 = (bf16[1,4,128,5120]{3,2,1,0:T(8,128)(2,1)S(1)}, bf16[1,4,128,5120]{3,2,1,0:T(8,128)(2,1)}, u32[]{:S(2)}) copy-start(bf16[1,4,128,5120]{3,2,1,0:T(8,128)(2,1)} %all-gather.2.cloned.1.call-done) | copy-start | bytes 15728644
  73.3 4.6 %slice-start = ((s8[7864320]{0:T(1024)(128)(4,1)}), s8[4194304]{0:T(1024)(128)(4,1)S(1)}, s32[]{:S(2)}) async-start(s8[7864320]{0:T(1024)(128)(4,1)} %bitcast.108), calls=%async_computation.3 | async-start | bytes 8388608
  74.8 3.1 %slice-start.1 = ((s8[7864320]{0:T(1024)(128)(4,1)}), s8[3670016]{0:T(1024)(128)(4,1)S(1)}, s32[]{:S(2)}) async-start(s8[7864320]{0:T(1024)(128)(4,1)} %bitcast.108), calls=%async_computation.4 | async-start | bytes 7340032
  77.9 4.5 %copy-start.3 = (f32[256]{0:T(256)S(1)}, f32[256]{0:T(256)}, u32[]{:S(2)}) copy-start(f32[256]{0:T(256)} %param.16) | copy-start | bytes 3076
  77.9 4.5 %copy-start.4 = (f32[256]{0:T(256)S(1)}, f32[256]{0:T(256)}, u32[]{:S(2)}) copy-start(f32[256]{0:T(256)} %param.15) | copy-start | bytes 3076
  98.2 94.4 %copy-start.2 = (bf16[8,5120]{1,0:T(8,128)(2,1)S(1)}, bf16[8,5120]{1,0:T(8,128)(2,1)}, u32[]{:S(2)}) copy-start(bf16[8,5120]{1,0:T(8,128)(2,1)} %param.12) | copy-start | bytes 245764
  183.9 8.7 %collective-permute-start = (bf16[8,5120]{1,0:T(8,128)(2,1)}, bf16[8,5120]{1,0:T(8,128)(2,1)}, u32[]{:S(2)}, u32[]{:S(2)}) collective-permute-start(bf16[8,5120]{1,0:T(8,128)(2,1)} %select_reduce_fusion), channel_id=1, source_target_pairs={{0,16},{16,32},{32,48},{48,64},{64,80},{80,96},{96,112},{1,17},{17... | collective-permute-start | bytes 245768 | tf_op jit(solution)/shard_map/ppermute | solution.py:12
Sparse Core Ops, SparseCore 0:
  9.8 59.3 all-gather.1
  98.3 83.6 reduce-scatter.3
where the time goes:
time: 205 us; the launch traced here: 202 us
  waiting for transfers between devices  138 us (67%)
  local copies, waits for them, and re-layouts  17.8 us (9%)
  between operations  15.2 us (7%)
  matrix products  13.9 us (7%)
  other arithmetic  13.9 us (7%)
  starting transfers between devices  3.42 us (2%)
    unnamed x3, waiting for transfers between devices  83.8 us
    all_gather x1, waiting for transfers between devices, body(): lax.all_gather(latents, 'seq', axis=2, tiled=True)  49 us
    unnamed x16, local copies, waits for them, and re-layouts  14.2 us
    ppermute x1, waiting for transfers between devices, from_behind(): return lax.ppermute(x, axis, pairs)  5.35 us
    dot_general x1, matrix products, body(): jnp.dot(normed.reshape(-1, width), w_flat, preferred_element_type=jnp.flo...  4.24 us
  transfers between devices with their start and end apart: 3, of which 3 were waited for; matrix products, arithmetic and copies ran while one was open for 6% of the time, Pallas kernels for 0%

commit v1 on v0

v1 whole, which is shorter than its diff:
```python
import functools

import jax
import jax.numpy as jnp
from jax import lax
from jax.experimental import pallas as pl
from jax.experimental.pallas import tpu as pltpu
from jax.sharding import PartitionSpec as P

HEAD_DIM = 128
Z_CHIPS, X_CHIPS, CORES = 2, 4, 2
MIB = 1 << 20


def hop(value, dz=0, dx=0, dc=0):
    pairs = []
    for z in range(Z_CHIPS):
        for x in range(X_CHIPS):
            for c in range(CORES):
                to_z, to_x, to_c = (z + dz) % Z_CHIPS, (x + dx) % X_CHIPS, (c + dc) % CORES
                pairs.append(((z * X_CHIPS + x) * CORES + c, (to_z * X_CHIPS + to_x) * CORES + to_c))
    return lax.ppermute(value, "seq", pairs)


def from_behind(x, axis, by):
    count = lax.axis_size(axis)
    pairs = [(i, i + by) for i in range(count) if 0 <= i + by < count]
    return lax.ppermute(x, axis, pairs)


def layer_norm_mod(rows, shift, scale):
    values = rows.astype(jnp.float32)
    mean = jnp.mean(values, axis=-1, keepdims=True)
    centred = values - mean
    var = jnp.mean(centred * centred, axis=-1, keepdims=True)
    return (centred * lax.rsqrt(var + 1e-06) * (1.0 + scale) + shift).astype(jnp.bfloat16)


def qkv_kernel(pieces, *refs):
    xs, (w_mine, w_other, gains, q_ref, kv_ref, rows_ref) = refs[:pieces], refs[pieces:]
    step = pl.program_id(0)
    rows = xs[0].shape[0]

    @pl.when(step == 0)
    def _():
        for i, x in enumerate(xs):
            rows_ref[i * rows : (i + 1) * rows, :] = x[...]

    def project(w):
        return jnp.dot(rows_ref[...], w[0], preferred_element_type=jnp.float32)

    def normed(values, gain):
        out = []
        for head in range(values.shape[1] // HEAD_DIM):
            part = values[:, head * HEAD_DIM : (head + 1) * HEAD_DIM]
            power = jnp.mean(part * part, axis=-1, keepdims=True)
            out.append(part * lax.rsqrt(power + 1e-06) * gain[:, head * HEAD_DIM : (head + 1) * HEAD_DIM])
        return jnp.concatenate(out, axis=1).astype(jnp.bfloat16)

    for owner, w in enumerate((w_mine, w_other)):
        @pl.when(step == 3 * owner)
        def _(owner=owner, w=w):
            q_ref[owner] = normed(project(w), gains[2 * owner : 2 * owner + 1, :])

        @pl.when(step == 3 * owner + 1)
        def _(owner=owner, w=w):
            kv_ref[2 * owner] = normed(project(w), gains[2 * owner + 1 : 2 * owner + 2, :])

        @pl.when(step == 3 * owner + 2)
        def _(owner=owner, w=w):
            kv_ref[2 * owner + 1] = project(w).astype(jnp.bfloat16)


def qkv_call(xs, w_mine, w_other, gains):
    pieces = len(xs)
    rows, width = xs[0].shape
    cols = w_mine.shape[2]
    total = rows * pieces
    whole = lambda shape: pl.BlockSpec(shape, lambda i: (0,) * len(shape))
    return pl.pallas_call(
        functools.partial(qkv_kernel, pieces),
        grid=(6,),
        in_specs=[whole((rows, width))] * pieces
        + [
            pl.BlockSpec((1, width, cols), lambda i: (jnp.minimum(i, 2), 0, 0)),
            pl.BlockSpec((1, width, cols), lambda i: (jnp.maximum(i - 3, 0), 0, 0)),
            whole(gains.shape),
        ],
        out_specs=[whole((2, total, cols)), whole((4, total, cols))],
        out_shape=[
            jax.ShapeDtypeStruct((2, total, cols), jnp.bfloat16),
            jax.ShapeDtypeStruct((4, total, cols), jnp.bfloat16),
        ],
        scratch_shapes=[pltpu.VMEM((total, width), jnp.bfloat16)],
        compiler_params=pltpu.CompilerParams(vmem_limit_bytes=40 * MIB),
        cost_estimate=pl.CostEstimate(
            flops=2 * total * width * cols * 6, bytes_accessed=12 * width * cols, transcendentals=0
        ),
    )(*xs, w_mine, w_other, gains)


def attend_kernel(pieces, q_ref, kv_ref, kv_far, w_mine, w_other, *refs):
    outs, attn_ref = refs[:pieces], refs[pieces]
    rows = outs[0].shape[0]
    contract = (((1,), (1,)), ((), ()))

    @pl.when(pl.program_id(0) == 0)
    def _():
        cols = q_ref.shape[2]
        for owner in range(2):
            for head in range(cols // HEAD_DIM):
                span = slice(head * HEAD_DIM, (head + 1) * HEAD_DIM)
                query = q_ref[owner, :, span]
                near, far = 2 * owner, 2 * (1 - owner)
                scores = jnp.concatenate(
                    [
                        lax.dot_general(query, kv_ref[near, :, span], contract, preferred_element_type=jnp.float32),
                        lax.dot_general(query, kv_far[far, :, span], contract, preferred_element_type=jnp.float32),
                    ],
                    axis=1,
                ) * HEAD_DIM ** (-0.5)
                top = jnp.max(scores, axis=-1, keepdims=True)
                expo = jnp.exp(scores - top)
                total = jnp.sum(expo, axis=-1, keepdims=True)
                prob = (expo / total).astype(jnp.bfloat16)
                half = kv_ref.shape[1]
                value = jnp.dot(prob[:, :half], kv_ref[near + 1, :, span], preferred_element_type=jnp.float32)
                value += jnp.dot(prob[:, half:], kv_far[far + 1, :, span], preferred_element_type=jnp.float32)
                at = owner * cols + head * HEAD_DIM
                attn_ref[:, at : at + HEAD_DIM] = value.astype(jnp.bfloat16)

    cols = w_mine.shape[0]
    part = jnp.dot(attn_ref[:, :cols], w_mine[...], preferred_element_type=jnp.float32)
    part += jnp.dot(attn_ref[:, cols:], w_other[...], preferred_element_type=jnp.float32)
    part = part.astype(jnp.bfloat16)
    for i, out in enumerate(outs):
        out[...] = part[i * rows : (i + 1) * rows, :]


def attend_call(q, kv, kv_far, w_mine, w_other, pieces):
    total = q.shape[1]
    rows = total // pieces
    cols, width = w_mine.shape
    block = 1024
    whole = lambda shape: pl.BlockSpec(shape, lambda i: (0,) * len(shape))
    return pl.pallas_call(
        functools.partial(attend_kernel, pieces),
        grid=(width // block,),
        in_specs=[
            whole(q.shape),
            whole(kv.shape),
            whole(kv_far.shape),
            pl.BlockSpec((cols, block), lambda i: (0, i)),
            pl.BlockSpec((cols, block), lambda i: (0, i)),
        ],
        out_specs=[pl.BlockSpec((rows, block), lambda i: (0, i))] * pieces,
        out_shape=[jax.ShapeDtypeStruct((rows, width), jnp.bfloat16)] * pieces,
        scratch_shapes=[pltpu.VMEM((total, 2 * cols), jnp.bfloat16)],
        compiler_params=pltpu.CompilerParams(vmem_limit_bytes=32 * MIB),
        cost_estimate=pl.CostEstimate(
            flops=4 * total * cols * width + 16 * total * total * cols,
            bytes_accessed=4 * cols * width,
            transcendentals=8 * total * total,
        ),
    )(q, kv, kv_far, w_mine, w_other)


def body(latents, steps, leaving, fresh, mod_table, w_qkv, q_gain, k_gain, w_out):
    _, frames, local_rows, width = latents.shape
    rows = frames * local_rows
    modrow = lax.dynamic_slice_in_dim(mod_table, steps[0], 1, axis=0)
    shift, scale, gate = modrow[:, :width], modrow[:, width : 2 * width], modrow[:, 2 * width :]
    own = latents.reshape(rows, width)
    normed = layer_norm_mod(own, shift, scale)

    w_mine = w_qkv.transpose(1, 0, 2)
    w_other = hop(w_mine, dc=1)
    gain_mine = jnp.stack([q_gain, k_gain])
    gains = jnp.concatenate([gain_mine, hop(gain_mine, dc=1)], axis=0)
    out_other = hop(w_out, dc=1)

    left = hop(normed, dx=1)
    right = hop(normed, dx=-1)
    far = hop(normed, dz=1)
    across = hop(normed, dx=2)
    far_left = hop(left, dz=1)
    far_right = hop(right, dz=1)
    far_across = hop(far, dx=2)
    xs = [normed, left, right, far, across, far_left, far_right, far_across]

    q, kv = qkv_call(xs, w_mine, w_other, gains)
    kv_far = hop(kv, dc=1)
    parts = attend_call(q, kv, kv_far, w_out, out_other, len(xs))
    p_own, p_left, p_right, p_far, p_across, p_far_left, p_far_right, p_far_across = parts

    def add(a, b):
        return (a.astype(jnp.float32) + b.astype(jnp.float32)).astype(jnp.bfloat16)

    s_left = add(p_left, hop(p_far_left, dz=1))
    s_right = add(p_right, hop(p_far_right, dz=1))
    s_far = add(p_far, hop(p_far_across, dx=2))
    arrived = [hop(p_across, dx=2), hop(s_left, dx=-1), hop(s_right, dx=1), hop(s_far, dz=1)]
    proj = p_own.astype(jnp.float32)
    for piece in arrived:
        proj = proj + piece.astype(jnp.float32)

    updated = (own.astype(jnp.float32) + gate * proj).astype(jnp.bfloat16).reshape(frames, local_rows, width)
    handed = lax.dynamic_slice_in_dim(updated, leaving[0], 1, axis=0)[0]
    arriving = from_behind(handed, "queue", 1)
    first = jnp.where(lax.axis_index("queue") == 0, fresh, arriving)
    select = jnp.arange(frames) == leaving[0]
    return jnp.where(select[:, None, None], first[None], updated)[None]


def solution(mesh):
    return jax.shard_map(
        body,
        mesh=mesh,
        in_specs=(
            P("queue", None, "seq", None),
            P("queue"),
            P("queue"),
            P("seq", None),
            P(),
            P(None, None, "seq"),
            P("seq"),
            P("seq"),
            P("seq", None),
        ),
        out_specs=P("queue", None, "seq", None),
        check_vma=False,
    )
```

time: 205 us -> 101 us (0.49); the launches traced: 202 us -> 101 us
  waiting for transfers between devices: 138 us -> 47.4 us
  starting transfers between devices: 3.42 us -> 26.9 us
  local copies, waits for them, and re-layouts: 17.8 us -> 3.43 us
  matrix products: 13.9 us -> 0 us
  between operations: 15.2 us -> 1.43 us
  Pallas kernels: 0 us -> 13.4 us
  other arithmetic: 13.9 us -> 8.5 us
    unnamed x3 -> x0, waiting for transfers between devices: 83.8 us -> none
    all_gather x1 -> x0, waiting for transfers between devices: 49 us -> none  [body(): lax.all_gather(latents, 'seq', axis=2, tiled=True)]
    ppermute x0 -> x18, waiting for transfers between devices: none -> 42.4 us  [hop(): return lax.ppermute(value, 'seq', pairs)]
    ppermute x0 -> x18, starting transfers between devices: none -> 23.4 us  [hop(): return lax.ppermute(value, 'seq', pairs)]
    pallas_call x0 -> x2, Pallas kernels: none -> 13.4 us  [the longest x1 8.62 us: qkv_call(): pl.pallas_call(functools.partial(qkv_kernel, pieces), grid=(6,), in_specs...]
    dot_general x4 -> x0, matrix products: 12 us -> none  [the longest x1 4.24 us: body(): jnp.dot(normed.reshape(-1, width), w_flat, preferred_element_type=jnp.flo...]
    unnamed x16 -> x6, local copies, waits for them, and re-layouts: 14.2 us -> 3.24 us
    another operation x2 -> x0, local copies, waits for them, and re-layouts: 3.51 us -> none  [body(): attn = jnp.stack(outputs, axis=0)]
  transfers between devices with their start and end apart: 3 -> 19, of which waited for: 3 -> 12; matrix products, arithmetic and copies ran while one was open for 6% -> 6% of each run, Pallas kernels for 0% -> 9%
where the time goes in v1:
time: 101 us
  waiting for transfers between devices  47.4 us (47%)
  starting transfers between devices  26.9 us (27%)
  Pallas kernels  13.4 us (13%)
  other arithmetic  8.5 us (8%)
  local copies, waits for them, and re-layouts  3.43 us (3%)
  between operations  1.43 us (1%)
    ppermute x18, waiting for transfers between devices, hop(): return lax.ppermute(value, 'seq', pairs)  42.4 us
    ppermute x18, starting transfers between devices, hop(): return lax.ppermute(value, 'seq', pairs)  23.4 us
    pallas_call x1, Pallas kernels, qkv_call(): pl.pallas_call(functools.partial(qkv_kernel, pieces), grid=(6,), in_specs...  8.62 us
    ppermute x1, waiting for transfers between devices, from_behind(): return lax.ppermute(x, axis, pairs)  4.95 us
    pallas_call x1, Pallas kernels, attend_call(): pl.pallas_call(functools.partial(attend_kernel, pieces), grid=(width // b...  4.82 us
    ppermute x1, starting transfers between devices, from_behind(): return lax.ppermute(x, axis, pairs)  3.47 us
    unnamed x6, local copies, waits for them, and re-layouts  3.24 us
  transfers between devices with their start and end apart: 19, of which 12 were waited for; matrix products, arithmetic and copies ran while one was open for 6% of the time, Pallas kernels for 9%

profile of v1, /device:TPU:96, one launch (start us, length us, event | category | flops | bytes accessed | tf_op | source)
XLA Modules:
  0.0 101.1 jit_solution(13733098009169449854)
XLA Ops:
  0.0 0.0 collective-permute-start.7
  0.0 0.5 collective-permute-start.10
  1.2 1.1 %convert_reduce_fusion = f32[4,8]{1,0:T(4,128)S(1)} fusion(bf16[1,4,8,5120]{3,2,1,0:T(8,128)(2,1)} %param.9), kind=kLoop, calls=%fused_computation.1 | loop fusion | flops 327648 | bytes 327808 | tf_op jit(solution)/shard_map/reduce_sum | solution.py:33
  2.3 0.1 div.9
  2.4 1.2 %fusion.8 = f32[4,8]{1,0:T(4,128)S(1)} fusion(bf16[1,4,8,5120]{3,2,1,0:T(8,128)(2,1)} %param.9, f32[4,8]{1,0:T(4,128)S(1)} %broadcast_multiply_fusion), kind=kLoop, calls=%fused_computation.11 | loop fusion | flops 655328 | bytes 327936 | tf_op jit(solution)/shard_map/reduce_sum | solution.py:35
  3.6 0.1 rsqrt.12
  3.7 1.2 %fusion.9 = (f32[1,5120]{1,0:T(1,128)S(1)}, f32[1,5120]{1,0:T(1,128)S(1)}, f32[1,5120]{1,0:T(1,128)S(1)}) fusion(f32[50,15360]{1,0:T(8,128)} %param.13, s32[]{:T(128)S(6)} %select_n.26, s32[]{:T(128)S(6)} %add.75, s32[]{:T(128)S(6)} %add.76), kind=kLoop, calls=%fused_computation.25 | loop fusion | flops 5120 | bytes 122892 | tf_op jit(solution)/shard_map/slice | solution.py:172
  4.9 1.2 %fusion.5.refs_0_ = bf16[32,5120]{1,0:T(8,128)(2,1)S(1)} fusion(bf16[1,4,8,5120]{3,2,1,0:T(8,128)(2,1)} %param.9, f32[5120]{0:T(1024)S(1)} %bitcast.41, f32[5120]{0:T(1024)S(1)} %bitcast.40, f32[32]{0:T(128)S(1)} %rsqrt.12, f32[32]{0:T(128)S(1)} %div.9), kind=kLoop, calls=%fused_computation.8 | loop fusion | flops 983040 | bytes 696576 | tf_op jit(solution)/shard_map/convert_element_type | solution.py:36
  6.1 1.6 %collective-permute-start = (bf16[32,5120]{1,0:T(8,128)(2,1)S(1)}, bf16[32,5120]{1,0:T(8,128)(2,1)S(1)}, u32[]{:S(2)}, u32[]{:S(2)}) collective-permute-start(bf16[32,5120]{1,0:T(8,128)(2,1)S(1)} %fusion.5.refs_0_), channel_id=1, source_target_pairs={{0,2},{1,3},{2,4},{3,5},{4,6},{5,7},{6,0},{7,1},{8,10},{9,11},{10,... | collective-permute-start | bytes 983048 | tf_op jit(solution)/shard_map/ppermute | solution.py:22
  7.6 0.7 pad_maximum_fusion.1
  8.3 0.0 collective-permute-start.8
  8.4 1.8 %collective-permute-start.1 = (bf16[32,5120]{1,0:T(8,128)(2,1)S(1)}, bf16[32,5120]{1,0:T(8,128)(2,1)S(1)}, u32[]{:S(2)}, u32[]{:S(2)}) collective-permute-start(bf16[32,5120]{1,0:T(8,128)(2,1)S(1)} %fusion.5.refs_0_), channel_id=1, source_target_pairs={{0,6},{1,7},{2,0},{3,1},{4,2},{5,3},{6,4},{7,5},{8,14},{9,15},{10,... | collective-permute-start | bytes 983048 | tf_op jit(solution)/shard_map/ppermute | solution.py:22
  10.2 6.0 %collective-permute-done.8 = f32[2,256]{1,0:T(2,128)S(1)} collective-permute-done((f32[2,256]{1,0:T(2,128)S(1)}, f32[2,256]{1,0:T(2,128)S(1)}, u32[]{:S(2)}, u32[]{:S(2)}) %collective-permute-start.8) | collective-permute-done | bytes 2080 | tf_op jit(solution)/shard_map/ppermute | solution.py:22
  16.2 0.6 collective-permute-start.2
  16.7 0.3 collective-permute-done.refs_1_
  17.0 2.8 %collective-permute-start.3 = (bf16[32,5120]{1,0:T(8,128)(2,1)S(1)}, bf16[32,5120]{1,0:T(8,128)(2,1)S(1)}, u32[]{:S(2)}, u32[]{:S(2)}) collective-permute-start(bf16[32,5120]{1,0:T(8,128)(2,1)S(1)} %fusion.5.refs_0_), channel_id=1, source_target_pairs={{0,4},{1,5},{2,6},{3,7},{4,0},{5,1},{6,2},{7,3},{8,12},{9,13},{10,... | collective-permute-start | bytes 983048 | tf_op jit(solution)/shard_map/ppermute | solution.py:22
  19.7 0.0 collective-permute-done.1.refs_2_
  19.7 3.0 %collective-permute-start.4 = (bf16[32,5120]{1,0:T(8,128)(2,1)S(1)}, bf16[32,5120]{1,0:T(8,128)(2,1)S(1)}, u32[]{:S(2)}, u32[]{:S(2)}) collective-permute-start(bf16[32,5120]{1,0:T(8,128)(2,1)S(1)} %collective-permute-done.refs_1_), channel_id=1, source_target_pairs={{0,8},{1,9},{2,10},{3,11},{4,12},{5,13},{6,14},{7,15},{8,0},{9,1},... | collective-permute-start | bytes 983048 | tf_op jit(solution)/shard_map/ppermute | solution.py:22
  22.7 5.5 %collective-permute-done.2.refs_3_ = bf16[32,5120]{1,0:T(8,128)(2,1)S(1)} collective-permute-done((bf16[32,5120]{1,0:T(8,128)(2,1)S(1)}, bf16[32,5120]{1,0:T(8,128)(2,1)S(1)}, u32[]{:S(2)}, u32[]{:S(2)}) %collective-permute-start.2) | collective-permute-done | bytes 327712 | tf_op jit(solution)/shard_map/ppermute | solution.py:22
  28.2 0.6 collective-permute-start.5
  28.8 0.0 collective-permute-done.3.refs_4_
  28.8 3.0 %collective-permute-start.6 = (bf16[32,5120]{1,0:T(8,128)(2,1)S(1)}, bf16[32,5120]{1,0:T(8,128)(2,1)S(1)}, u32[]{:S(2)}, u32[]{:S(2)}) collective-permute-start(bf16[32,5120]{1,0:T(8,128)(2,1)S(1)} %collective-permute-done.2.refs_3_), channel_id=1, source_target_pairs={{0,4},{1,5},{2,6},{3,7},{4,0},{5,1},{6,2},{7,3},{8,12},{9,13},{10,... | collective-permute-start | bytes 983048 | tf_op jit(solution)/shard_map/ppermute | solution.py:22
  31.8 0.7 pad_maximum_fusion.refs_10_
  32.5 2.7 %collective-permute-done.4.refs_5_ = bf16[32,5120]{1,0:T(8,128)(2,1)S(1)} collective-permute-done((bf16[32,5120]{1,0:T(8,128)(2,1)S(1)}, bf16[32,5120]{1,0:T(8,128)(2,1)S(1)}, u32[]{:S(2)}, u32[]{:S(2)}) %collective-permute-start.4) | collective-permute-done | bytes 327712 | tf_op jit(solution)/shard_map/ppermute | solution.py:22
  35.2 6.2 %collective-permute-done.5.refs_6_ = bf16[32,5120]{1,0:T(8,128)(2,1)S(1)} collective-permute-done((bf16[32,5120]{1,0:T(8,128)(2,1)S(1)}, bf16[32,5120]{1,0:T(8,128)(2,1)S(1)}, u32[]{:S(2)}, u32[]{:S(2)}) %collective-permute-start.5) | collective-permute-done | bytes 327712 | tf_op jit(solution)/shard_map/ppermute | solution.py:22
  41.5 0.0 collective-permute-done.6.refs_7_
  41.5 0.0 collective-permute-done.7.refs_9_
  41.5 0.0 copy-start
  41.5 3.2 %copy-done = bf16[5120,3,256]{2,0,1:T(8,128)(2,1)S(1)} copy-done((bf16[5120,3,256]{2,0,1:T(8,128)(2,1)S(1)}, bf16[5120,3,256]{2,0,1:T(8,128)(2,1)}, u32[]{:S(2)}) %copy-start) | copy-done | bytes 7864344
  44.7 0.0 copy-start.1
  44.7 8.6 %shard_map.91 = (bf16[2,256,256]{2,1,0:T(8,128)(2,1)S(1)}, bf16[4,256,256]{2,1,0:T(8,128)(2,1)S(1)}) custom-call(bf16[32,5120]{1,0:T(8,128)(2,1)S(1)} %fusion.5.refs_0_, bf16[32,5120]{1,0:T(8,128)(2,1)S(1)} %collective-permute-done.refs_1_, bf16[32,5120]{1,0:T(8,128)(2,1)S(1)} %collective-permute-done.1.refs_2_, ...), custom_call_target="tpu_custom_call" | custom-call | flops 4026531840 | bytes 15728640 | tf_op jit(solution)/shard_map/pallas_call | solution.py:80
  53.3 0.1 collective-permute-start.9
  53.4 0.0 collective-permute-done.10.w_other
  53.4 1.9 %collective-permute-done.9.kv_far = bf16[4,256,256]{2,1,0:T(8,128)(2,1)S(1)} collective-permute-done((bf16[4,256,256]{2,1,0:T(8,128)(2,1)S(1)}, bf16[4,256,256]{2,1,0:T(8,128)(2,1)S(1)}, u32[]{:S(2)}, u32[]{:S(2)}) %collective-permute-start.9) | collective-permute-done | bytes 524320 | tf_op jit(solution)/shard_map/ppermute | solution.py:22
  55.3 0.0 copy-done.1
  55.3 4.8 %shard_map.92 = (bf16[32,5120]{1,0:T(8,128)(2,1)S(1)}, bf16[32,5120]{1,0:T(8,128)(2,1)S(1)}, bf16[32,5120]{1,0:T(8,128)(2,1)S(1)}, bf16[32,5120]{1,0:T(8,128)(2,...) custom-call(bf16[2,256,256]{2,1,0:T(8,128)(2,1)S(1)} %get-tuple-elem, ...), custom_call_target="tpu_custom_call" | custom-call | flops 1610612736 | bytes 5242880 | tf_op jit(solution)/shard_map/pallas_call | solution.py:146
  60.2 0.0 copy-start.2
  60.2 0.6 collective-permute-start.12
  60.8 3.0 %collective-permute-start.14 = (bf16[32,5120]{1,0:T(8,128)(2,1)S(1)}, bf16[32,5120]{1,0:T(8,128)(2,1)S(1)}, u32[]{:S(2)}, u32[]{:S(2)}) collective-permute-start(bf16[32,5120]{1,0:T(8,128)(2,1)S(1)} %get-tuple-element.22), channel_id=1, source_target_pairs={{0,8},{1,9},{2,10},{3,11},{4,12},{5,13},{6,14},{7,15},{8,0},{9,1},... | collective-permute-start | bytes 983048 | tf_op jit(solution)/shard_map/ppermute | solution.py:22
  63.8 3.0 %collective-permute-start.16 = (bf16[32,5120]{1,0:T(8,128)(2,1)S(1)}, bf16[32,5120]{1,0:T(8,128)(2,1)S(1)}, u32[]{:S(2)}, u32[]{:S(2)}) collective-permute-start(bf16[32,5120]{1,0:T(8,128)(2,1)S(1)} %get-tuple-element.24), channel_id=1, source_target_pairs={{0,4},{1,5},{2,6},{3,7},{4,0},{5,1},{6,2},{7,3},{8,12},{9,13},{10,... | collective-permute-start | bytes 983048 | tf_op jit(solution)/shard_map/ppermute | solution.py:22
  66.8 0.5 collective-permute-start.11
  67.3 5.0 %collective-permute-done.12 = bf16[32,5120]{1,0:T(8,128)(2,1)S(1)} collective-permute-done((bf16[32,5120]{1,0:T(8,128)(2,1)S(1)}, bf16[32,5120]{1,0:T(8,128)(2,1)S(1)}, u32[]{:S(2)}, u32[]{:S(2)}) %collective-permute-start.12) | collective-permute-done | bytes 327712 | tf_op jit(solution)/shard_map/ppermute | solution.py:22
  72.3 0.1 add_convert_fusion.2
  72.4 0.3 collective-permute-start.13
  72.7 5.9 %collective-permute-done.14 = bf16[32,5120]{1,0:T(8,128)(2,1)S(1)} collective-permute-done((bf16[32,5120]{1,0:T(8,128)(2,1)S(1)}, bf16[32,5120]{1,0:T(8,128)(2,1)S(1)}, u32[]{:S(2)}, u32[]{:S(2)}) %collective-permute-start.14) | collective-permute-done | bytes 327712 | tf_op jit(solution)/shard_map/ppermute | solution.py:22
  78.5 0.1 add_convert_fusion.1
  78.6 1.6 %collective-permute-start.15 = (bf16[32,5120]{1,0:T(8,128)(2,1)S(1)}, bf16[32,5120]{1,0:T(8,128)(2,1)S(1)}, u32[]{:S(2)}, u32[]{:S(2)}) collective-permute-start(bf16[32,5120]{1,0:T(8,128)(2,1)S(1)} %add_convert_fusion.1), channel_id=1, source_target_pairs={{0,2},{1,3},{2,4},{3,5},{4,6},{5,7},{6,0},{7,1},{8,10},{9,11},{10,... | collective-permute-start | bytes 983048 | tf_op jit(solution)/shard_map/ppermute | solution.py:22
  80.2 0.0 collective-permute-done.16
  80.2 0.1 add_convert_fusion
  80.2 0.6 collective-permute-start.17
  81.5 0.0 collective-permute-done.11
  81.6 5.3 %collective-permute-done.13 = bf16[32,5120]{1,0:T(8,128)(2,1)S(1)} collective-permute-done((bf16[32,5120]{1,0:T(8,128)(2,1)S(1)}, bf16[32,5120]{1,0:T(8,128)(2,1)S(1)}, u32[]{:S(2)}, u32[]{:S(2)}) %collective-permute-start.13) | collective-permute-done | bytes 327712 | tf_op jit(solution)/shard_map/ppermute | solution.py:22
  86.8 2.0 %collective-permute-done.15 = bf16[32,5120]{1,0:T(8,128)(2,1)S(1)} collective-permute-done((bf16[32,5120]{1,0:T(8,128)(2,1)S(1)}, bf16[32,5120]{1,0:T(8,128)(2,1)S(1)}, u32[]{:S(2)}, u32[]{:S(2)}) %collective-permute-start.15) | collective-permute-done | bytes 327712 | tf_op jit(solution)/shard_map/ppermute | solution.py:22
  88.8 1.7 %collective-permute-done.17 = bf16[32,5120]{1,0:T(8,128)(2,1)S(1)} collective-permute-done((bf16[32,5120]{1,0:T(8,128)(2,1)S(1)}, bf16[32,5120]{1,0:T(8,128)(2,1)S(1)}, u32[]{:S(2)}, u32[]{:S(2)}) %collective-permute-start.17) | collective-permute-done | bytes 327712 | tf_op jit(solution)/shard_map/ppermute | solution.py:22
  90.5 1.3 %fusion.6 = bf16[32,5120]{1,0:T(8,128)(2,1)S(1)} fusion(bf16[1,4,8,5120]{3,2,1,0:T(8,128)(2,1)} %param.9, bf16[32,5120]{1,0:T(8,128)(2,1)S(1)} %collective-permute-done.17, bf16[32,5120]{1,0:T(8,128)(2,1)S(1)} %collective-permute-done.15, bf16[32,5120]{1,0:T(8,128)(2,1)S(1)} %collective-permute-done.13, bf16[32,5120]{1,0:T(8,128)(2,1)S(1)} %collective-permute-done.11, ...), kind=kLoop, calls=%fused_computation.9 | loop fusion | flops 2129920 | bytes 2314240 | tf_op jit(solution)/shard_map/convert_element_type | solution.py:207
  91.8 3.5 %collective-permute-start.18 = (bf16[8,5120]{1,0:T(8,128)(2,1)S(1)}, bf16[8,5120]{1,0:T(8,128)(2,1)S(1)}, u32[]{:S(2)}, u32[]{:S(2)}) collective-permute-start(bf16[8,5120]{1,0:T(8,128)(2,1)S(1)} %dynamic-slice_bitcast_fusion), channel_id=1, source_target_pairs={{0,16},{16,32},{32,48},{48,64},{64,80},{80,96},{96,112},{1,17},{17... | collective-permute-start | bytes 245768 | tf_op jit(solution)/shard_map/ppermute | solution.py:28
  95.3 4.9 %collective-permute-done.18 = bf16[8,5120]{1,0:T(8,128)(2,1)S(1)} collective-permute-done((bf16[8,5120]{1,0:T(8,128)(2,1)S(1)}, bf16[8,5120]{1,0:T(8,128)(2,1)S(1)}, u32[]{:S(2)}, u32[]{:S(2)}) %collective-permute-start.18) | collective-permute-done | bytes 81952 | tf_op jit(solution)/shard_map/ppermute | solution.py:28
  100.2 0.0 copy-done.2
  100.3 0.8 bitcast_select_fusion
  (5 shorter events, 0.0 us)
Async XLA Ops:
  0.0 41.5 %collective-permute-start.7 = (bf16[3,5120,256]{2,1,0:T(8,128)(2,1)}, bf16[3,5120,256]{2,1,0:T(8,128)(2,1)}, u32[]{:S(2)}, u32[]{:S(2)}) collective-permute-start(bf16[3,5120,256]{2,1,0:T(8,128)(2,1)} %bitcast.36), channel_id=1, source_target_pairs={{0,1},{1,0},{2,3},{3,2},{4,5},{5,4},{6,7},{7,6},{8,9},{9,8},{10,11... | collective-permute-start | bytes 23592968 | tf_op jit(solution)/shard_map/ppermute | solution.py:22
  0.0 53.4 %collective-permute-start.10 = (bf16[256,5120]{1,0:T(8,128)(2,1)}, bf16[256,5120]{1,0:T(8,128)(2,1)S(1)}, u32[]{:S(2)}, u32[]{:S(2)}) collective-permute-start(bf16[256,5120]{1,0:T(8,128)(2,1)} %w_mine.1), channel_id=1, source_target_pairs={{0,1},{1,0},{2,3},{3,2},{4,5},{5,4},{6,7},{7,6},{8,9},{9,8},{10,11... | collective-permute-start | bytes 7864328 | tf_op jit(solution)/shard_map/ppermute | solution.py:22
  6.1 10.9 %collective-permute-start = (bf16[32,5120]{1,0:T(8,128)(2,1)S(1)}, bf16[32,5120]{1,0:T(8,128)(2,1)S(1)}, u32[]{:S(2)}, u32[]{:S(2)}) collective-permute-start(bf16[32,5120]{1,0:T(8,128)(2,1)S(1)} %fusion.5.refs_0_), channel_id=1, source_target_pairs={{0,2},{1,3},{2,4},{3,5},{4,6},{5,7},{6,0},{7,1},{8,10},{9,11},{10,... | collective-permute-start | bytes 983048 | tf_op jit(solution)/shard_map/ppermute | solution.py:22
  8.3 7.8 %collective-permute-start.8 = (f32[2,256]{1,0:T(2,128)S(1)}, f32[2,256]{1,0:T(2,128)S(1)}, u32[]{:S(2)}, u32[]{:S(2)}) collective-permute-start(f32[2,256]{1,0:T(2,128)S(1)} %pad_maximum_fusion.1), channel_id=1, source_target_pairs={{0,1},{1,0},{2,3},{3,2},{4,5},{5,4},{6,7},{7,6},{8,9},{9,8},{10,11... | collective-permute-start | bytes 6152 | tf_op jit(solution)/shard_map/ppermute | solution.py:22
  8.4 11.4 %collective-permute-start.1 = (bf16[32,5120]{1,0:T(8,128)(2,1)S(1)}, bf16[32,5120]{1,0:T(8,128)(2,1)S(1)}, u32[]{:S(2)}, u32[]{:S(2)}) collective-permute-start(bf16[32,5120]{1,0:T(8,128)(2,1)S(1)} %fusion.5.refs_0_), channel_id=1, source_target_pairs={{0,6},{1,7},{2,0},{3,1},{4,2},{5,3},{6,4},{7,5},{8,14},{9,15},{10,... | collective-permute-start | bytes 983048 | tf_op jit(solution)/shard_map/ppermute | solution.py:22
  16.2 12.1 %collective-permute-start.2 = (bf16[32,5120]{1,0:T(8,128)(2,1)S(1)}, bf16[32,5120]{1,0:T(8,128)(2,1)S(1)}, u32[]{:S(2)}, u32[]{:S(2)}) collective-permute-start(bf16[32,5120]{1,0:T(8,128)(2,1)S(1)} %fusion.5.refs_0_), channel_id=1, source_target_pairs={{0,8},{1,9},{2,10},{3,11},{4,12},{5,13},{6,14},{7,15},{8,0},{9,1},... | collective-permute-start | bytes 983048 | tf_op jit(solution)/shard_map/ppermute | solution.py:22
  17.0 11.8 %collective-permute-start.3 = (bf16[32,5120]{1,0:T(8,128)(2,1)S(1)}, bf16[32,5120]{1,0:T(8,128)(2,1)S(1)}, u32[]{:S(2)}, u32[]{:S(2)}) collective-permute-start(bf16[32,5120]{1,0:T(8,128)(2,1)S(1)} %fusion.5.refs_0_), channel_id=1, source_target_pairs={{0,4},{1,5},{2,6},{3,7},{4,0},{5,1},{6,2},{7,3},{8,12},{9,13},{10,... | collective-permute-start | bytes 983048 | tf_op jit(solution)/shard_map/ppermute | solution.py:22
  19.7 15.5 %collective-permute-start.4 = (bf16[32,5120]{1,0:T(8,128)(2,1)S(1)}, bf16[32,5120]{1,0:T(8,128)(2,1)S(1)}, u32[]{:S(2)}, u32[]{:S(2)}) collective-permute-start(bf16[32,5120]{1,0:T(8,128)(2,1)S(1)} %collective-permute-done.refs_1_), channel_id=1, source_target_pairs={{0,8},{1,9},{2,10},{3,11},{4,12},{5,13},{6,14},{7,15},{8,0},{9,1},... | collective-permute-start | bytes 983048 | tf_op jit(solution)/shard_map/ppermute | solution.py:22
  28.2 13.2 %collective-permute-start.5 = (bf16[32,5120]{1,0:T(8,128)(2,1)S(1)}, bf16[32,5120]{1,0:T(8,128)(2,1)S(1)}, u32[]{:S(2)}, u32[]{:S(2)}) collective-permute-start(bf16[32,5120]{1,0:T(8,128)(2,1)S(1)} %collective-permute-done.1.refs_2_), channel_id=1, source_target_pairs={{0,8},{1,9},{2,10},{3,11},{4,12},{5,13},{6,14},{7,15},{8,0},{9,1},... | collective-permute-start | bytes 983048 | tf_op jit(solution)/shard_map/ppermute | solution.py:22
  28.8 12.7 %collective-permute-start.6 = (bf16[32,5120]{1,0:T(8,128)(2,1)S(1)}, bf16[32,5120]{1,0:T(8,128)(2,1)S(1)}, u32[]{:S(2)}, u32[]{:S(2)}) collective-permute-start(bf16[32,5120]{1,0:T(8,128)(2,1)S(1)} %collective-permute-done.2.refs_3_), channel_id=1, source_target_pairs={{0,4},{1,5},{2,6},{3,7},{4,0},{5,1},{6,2},{7,3},{8,12},{9,13},{10,... | collective-permute-start | bytes 983048 | tf_op jit(solution)/shard_map/ppermute | solution.py:22
  41.5 3.2 %copy-start = (bf16[5120,3,256]{2,0,1:T(8,128)(2,1)S(1)}, bf16[5120,3,256]{2,0,1:T(8,128)(2,1)}, u32[]{:S(2)}) copy-start(bf16[5120,3,256]{2,0,1:T(8,128)(2,1)} %param.14) | copy-start | bytes 23592964
  44.7 10.6 %copy-start.1 = (bf16[256,5120]{1,0:T(8,128)(2,1)S(1)}, bf16[256,5120]{1,0:T(8,128)(2,1)}, u32[]{:S(2)}) copy-start(bf16[256,5120]{1,0:T(8,128)(2,1)} %w_mine.1) | copy-start | bytes 7864324
  53.3 2.0 %collective-permute-start.9 = (bf16[4,256,256]{2,1,0:T(8,128)(2,1)S(1)}, bf16[4,256,256]{2,1,0:T(8,128)(2,1)S(1)}, u32[]{:S(2)}, u32[]{:S(2)}) collective-permute-start(bf16[4,256,256]{2,1,0:T(8,128)(2,1)S(1)} %get-tuple-element.16.kv_ref), channel_id=1, source_target_pairs={{0,1},{1,0},{2,3},{3,2},{4,5},{5,4},{6,7},{7,6},{8,9},{9,8},{10,11... | collective-permute-start | bytes 1572872 | tf_op jit(solution)/shard_map/ppermute | solution.py:22
  60.2 40.1 %copy-start.2 = (bf16[8,5120]{1,0:T(8,128)(2,1)S(1)}, bf16[8,5120]{1,0:T(8,128)(2,1)}, u32[]{:S(2)}) copy-start(bf16[8,5120]{1,0:T(8,128)(2,1)} %param.12) | copy-start | bytes 245764
  60.2 12.1 %collective-permute-start.12 = (bf16[32,5120]{1,0:T(8,128)(2,1)S(1)}, bf16[32,5120]{1,0:T(8,128)(2,1)S(1)}, u32[]{:S(2)}, u32[]{:S(2)}) collective-permute-start(bf16[32,5120]{1,0:T(8,128)(2,1)S(1)} %get-tuple-element.20), channel_id=1, source_target_pairs={{0,8},{1,9},{2,10},{3,11},{4,12},{5,13},{6,14},{7,15},{8,0},{9,1},... | collective-permute-start | bytes 983048 | tf_op jit(solution)/shard_map/ppermute | solution.py:22
  60.8 17.7 %collective-permute-start.14 = (bf16[32,5120]{1,0:T(8,128)(2,1)S(1)}, bf16[32,5120]{1,0:T(8,128)(2,1)S(1)}, u32[]{:S(2)}, u32[]{:S(2)}) collective-permute-start(bf16[32,5120]{1,0:T(8,128)(2,1)S(1)} %get-tuple-element.22), channel_id=1, source_target_pairs={{0,8},{1,9},{2,10},{3,11},{4,12},{5,13},{6,14},{7,15},{8,0},{9,1},... | collective-permute-start | bytes 983048 | tf_op jit(solution)/shard_map/ppermute | solution.py:22
  63.8 16.4 %collective-permute-start.16 = (bf16[32,5120]{1,0:T(8,128)(2,1)S(1)}, bf16[32,5120]{1,0:T(8,128)(2,1)S(1)}, u32[]{:S(2)}, u32[]{:S(2)}) collective-permute-start(bf16[32,5120]{1,0:T(8,128)(2,1)S(1)} %get-tuple-element.24), channel_id=1, source_target_pairs={{0,4},{1,5},{2,6},{3,7},{4,0},{5,1},{6,2},{7,3},{8,12},{9,13},{10,... | collective-permute-start | bytes 983048 | tf_op jit(solution)/shard_map/ppermute | solution.py:22
  66.8 14.7 %collective-permute-start.11 = (bf16[32,5120]{1,0:T(8,128)(2,1)S(1)}, bf16[32,5120]{1,0:T(8,128)(2,1)S(1)}, u32[]{:S(2)}, u32[]{:S(2)}) collective-permute-start(bf16[32,5120]{1,0:T(8,128)(2,1)S(1)} %get-tuple-element.18), channel_id=1, source_target_pairs={{0,4},{1,5},{2,6},{3,7},{4,0},{5,1},{6,2},{7,3},{8,12},{9,13},{10,... | collective-permute-start | bytes 983048 | tf_op jit(solution)/shard_map/ppermute | solution.py:22
  72.4 14.4 %collective-permute-start.13 = (bf16[32,5120]{1,0:T(8,128)(2,1)S(1)}, bf16[32,5120]{1,0:T(8,128)(2,1)S(1)}, u32[]{:S(2)}, u32[]{:S(2)}) collective-permute-start(bf16[32,5120]{1,0:T(8,128)(2,1)S(1)} %add_convert_fusion.2), channel_id=1, source_target_pairs={{0,6},{1,7},{2,0},{3,1},{4,2},{5,3},{6,4},{7,5},{8,14},{9,15},{10,... | collective-permute-start | bytes 983048 | tf_op jit(solution)/shard_map/ppermute | solution.py:22
  78.6 10.2 %collective-permute-start.15 = (bf16[32,5120]{1,0:T(8,128)(2,1)S(1)}, bf16[32,5120]{1,0:T(8,128)(2,1)S(1)}, u32[]{:S(2)}, u32[]{:S(2)}) collective-permute-start(bf16[32,5120]{1,0:T(8,128)(2,1)S(1)} %add_convert_fusion.1), channel_id=1, source_target_pairs={{0,2},{1,3},{2,4},{3,5},{4,6},{5,7},{6,0},{7,1},{8,10},{9,11},{10,... | collective-permute-start | bytes 983048 | tf_op jit(solution)/shard_map/ppermute | solution.py:22
  80.2 10.2 %collective-permute-start.17 = (bf16[32,5120]{1,0:T(8,128)(2,1)S(1)}, bf16[32,5120]{1,0:T(8,128)(2,1)S(1)}, u32[]{:S(2)}, u32[]{:S(2)}) collective-permute-start(bf16[32,5120]{1,0:T(8,128)(2,1)S(1)} %add_convert_fusion), channel_id=1, source_target_pairs={{0,8},{1,9},{2,10},{3,11},{4,12},{5,13},{6,14},{7,15},{8,0},{9,1},... | collective-permute-start | bytes 983048 | tf_op jit(solution)/shard_map/ppermute | solution.py:22
  91.8 8.4 %collective-permute-start.18 = (bf16[8,5120]{1,0:T(8,128)(2,1)S(1)}, bf16[8,5120]{1,0:T(8,128)(2,1)S(1)}, u32[]{:S(2)}, u32[]{:S(2)}) collective-permute-start(bf16[8,5120]{1,0:T(8,128)(2,1)S(1)} %dynamic-slice_bitcast_fusion), channel_id=1, source_target_pairs={{0,16},{16,32},{32,48},{48,64},{64,80},{80,96},{96,112},{1,17},{17... | collective-permute-start | bytes 245768 | tf_op jit(solution)/shard_map/ppermute | solution.py:28

commit v2 on v1

v2 whole, which is shorter than its diff:
```python
import functools

import jax
import jax.numpy as jnp
from jax import lax
from jax.experimental import pallas as pl
from jax.experimental.pallas import tpu as pltpu
from jax.sharding import PartitionSpec as P

HEAD_DIM = 128
Z_CHIPS, X_CHIPS, CORES = 2, 4, 2
MIB = 1 << 20
ANY = pl.BlockSpec(memory_space=pl.ANY)
VMEM = pl.BlockSpec(memory_space=pltpu.VMEM)
SMEM = pl.BlockSpec(memory_space=pltpu.SMEM)


def hop(value, dz=0, dx=0, dc=0):
    pairs = []
    for z in range(Z_CHIPS):
        for x in range(X_CHIPS):
            for c in range(CORES):
                to_z, to_x, to_c = (z + dz) % Z_CHIPS, (x + dx) % X_CHIPS, (c + dc) % CORES
                pairs.append(((z * X_CHIPS + x) * CORES + c, (to_z * X_CHIPS + to_x) * CORES + to_c))
    return lax.ppermute(value, "seq", pairs)


def from_behind(x, axis, by):
    count = lax.axis_size(axis)
    pairs = [(i, i + by) for i in range(count) if 0 <= i + by < count]
    return lax.ppermute(x, axis, pairs)


def norm_kernel(step, x_ref, table, out_ref, gate_ref, row, sem):
    width = x_ref.shape[-1]
    copy = pltpu.make_async_copy(table.at[pl.ds(step[0], 1), :], row, sem)
    copy.start()
    values = x_ref[...].astype(jnp.float32)
    mean = jnp.mean(values, axis=-1, keepdims=True)
    centred = values - mean
    var = jnp.mean(centred * centred, axis=-1, keepdims=True)
    scaled = centred * lax.rsqrt(var + 1e-06)
    copy.wait()
    shift, scale = row[:, :width], row[:, width : 2 * width]
    out_ref[...] = (scaled * (1.0 + scale) + shift).astype(jnp.bfloat16)
    gate_ref[...] = row[:, 2 * width :]


def norm_call(step, x, table):
    rows, width = x.shape
    return pl.pallas_call(
        norm_kernel,
        in_specs=[SMEM, VMEM, ANY],
        out_specs=[VMEM, VMEM],
        out_shape=[
            jax.ShapeDtypeStruct((rows, width), jnp.bfloat16),
            jax.ShapeDtypeStruct((1, width), jnp.float32),
        ],
        scratch_shapes=[pltpu.VMEM((1, 3 * width), jnp.float32), pltpu.SemaphoreType.DMA],
        compiler_params=pltpu.CompilerParams(vmem_limit_bytes=8 * MIB),
        cost_estimate=pl.CostEstimate(flops=10 * rows * width, bytes_accessed=4 * rows * width, transcendentals=0),
    )(step, x, pltpu.with_memory_space_constraint(table, pltpu.HBM))


def head_norm(values, gain):
    out = []
    for at in range(0, values.shape[1], HEAD_DIM):
        part = values[:, at : at + HEAD_DIM]
        power = jnp.mean(part * part, axis=-1, keepdims=True)
        out.append(part * lax.rsqrt(power + 1e-06) * gain[:, at : at + HEAD_DIM])
    return jnp.concatenate(out, axis=1)


def project(i, rows_ref, weights, gains, q_ref, kv_ref):
    owner, kind = divmod(i, 3)
    acc = jnp.dot(rows_ref[...], weights[i], preferred_element_type=jnp.float32)
    if kind < 2:
        acc = head_norm(acc, gains[2 * owner + kind][...])
    if kind == 0:
        q_ref[owner] = acc.astype(jnp.bfloat16)
    else:
        kv_ref[2 * owner + kind - 1] = acc.astype(jnp.bfloat16)


def gather_rows(xs, rows_ref):
    rows = xs[0].shape[0]
    for i, x in enumerate(xs):
        rows_ref[i * rows : (i + 1) * rows, :] = x[...]


def first_kernel(pieces, *refs):
    xs, gains = refs[:pieces], refs[pieces : pieces + 4]
    w_mine, w_other, q_ref, kv_ref, held, rows_ref, sems = refs[pieces + 4 :]
    copies = []
    for i in range(6):
        copies.append(pltpu.make_async_copy((w_mine, w_other)[i // 3].at[i % 3], held.at[i], sems.at[i]))
        copies[i].start()
    gather_rows(xs, rows_ref)
    for i in range(6):
        copies[i].wait()
        project(i, rows_ref, held, gains, q_ref, kv_ref)


def rest_kernel(pieces, *refs):
    xs, gains = refs[:pieces], refs[pieces : pieces + 4]
    held, q_ref, kv_ref, rows_ref = refs[pieces + 4 :]
    gather_rows(xs, rows_ref)
    for i in range(6):
        project(i, rows_ref, held, gains, q_ref, kv_ref)


def qkv_shapes(total, cols):
    return [
        jax.ShapeDtypeStruct((2, total, cols), jnp.bfloat16),
        jax.ShapeDtypeStruct((4, total, cols), jnp.bfloat16),
    ]


def first_call(xs, gains, w_mine, w_other):
    pieces = len(xs)
    rows, width = xs[0].shape
    total, cols = rows * pieces, w_mine.shape[2]
    return pl.pallas_call(
        functools.partial(first_kernel, pieces),
        in_specs=[VMEM] * (pieces + 4) + [ANY, ANY],
        out_specs=[VMEM] * 3,
        out_shape=qkv_shapes(total, cols) + [pltpu.VMEM((6, width, cols), jnp.bfloat16)],
        scratch_shapes=[pltpu.VMEM((total, width), jnp.bfloat16), pltpu.SemaphoreType.DMA((6,))],
        compiler_params=pltpu.CompilerParams(vmem_limit_bytes=24 * MIB),
        cost_estimate=pl.CostEstimate(
            flops=12 * total * width * cols, bytes_accessed=12 * width * cols, transcendentals=0
        ),
    )(
        *xs,
        *gains,
        pltpu.with_memory_space_constraint(w_mine, pltpu.HBM),
        pltpu.with_memory_space_constraint(w_other, pltpu.HBM),
    )


def rest_call(xs, gains, held):
    pieces = len(xs)
    rows, width = xs[0].shape
    total, cols = rows * pieces, held.shape[2]
    return pl.pallas_call(
        functools.partial(rest_kernel, pieces),
        in_specs=[VMEM] * (pieces + 5),
        out_specs=[VMEM] * 2,
        out_shape=qkv_shapes(total, cols),
        scratch_shapes=[pltpu.VMEM((total, width), jnp.bfloat16)],
        compiler_params=pltpu.CompilerParams(vmem_limit_bytes=24 * MIB),
        cost_estimate=pl.CostEstimate(
            flops=12 * total * width * cols, bytes_accessed=12 * width * cols, transcendentals=0
        ),
    )(*xs, *gains, pltpu.with_memory_space_constraint(held, pltpu.VMEM))


def attend_kernel(pieces, q_a, q_b, kv_a, kv_b, far_a, far_b, w_mine, w_other, *refs):
    outs, (q_ref, kv_ref, attn_ref) = refs[:pieces], refs[pieces:]
    rows = outs[0].shape[0]
    cols = q_a.shape[2]
    contract = (((1,), (1,)), ((), ()))

    @pl.when(pl.program_id(0) == 0)
    def _():
        cut, half = q_a.shape[1], q_ref.shape[1]
        for owner in range(2):
            q_ref[owner, :cut, :] = q_a[owner]
            q_ref[owner, cut:, :] = q_b[owner]
            for kind in range(2):
                near, far = 2 * owner + kind, 2 * (1 - owner) + kind
                kv_ref[near, :cut, :] = kv_a[near]
                kv_ref[near, cut:half, :] = kv_b[near]
                kv_ref[near, half : half + cut, :] = far_a[far]
                kv_ref[near, half + cut :, :] = far_b[far]
        for owner in range(2):
            for at in range(0, cols, HEAD_DIM):
                span = slice(at, at + HEAD_DIM)
                scores = lax.dot_general(
                    q_ref[owner, :, span], kv_ref[2 * owner, :, span], contract, preferred_element_type=jnp.float32
                ) * HEAD_DIM ** (-0.5)
                top = jnp.max(scores, axis=-1, keepdims=True)
                expo = jnp.exp(scores - top)
                total = jnp.sum(expo, axis=-1, keepdims=True)
                prob = (expo * (1.0 / total)).astype(jnp.bfloat16)
                value = jnp.dot(prob, kv_ref[2 * owner + 1, :, span], preferred_element_type=jnp.float32)
                attn_ref[:, owner * cols + at : owner * cols + at + HEAD_DIM] = value.astype(jnp.bfloat16)

    part = jnp.dot(attn_ref[:, :cols], w_mine[...], preferred_element_type=jnp.float32)
    part += jnp.dot(attn_ref[:, cols:], w_other[...], preferred_element_type=jnp.float32)
    part = part.astype(jnp.bfloat16)
    for i, out in enumerate(outs):
        out[...] = part[i * rows : (i + 1) * rows, :]


def attend_call(q_a, q_b, kv_a, kv_b, far_a, far_b, w_mine, w_other, pieces):
    total = q_a.shape[1] + q_b.shape[1]
    rows = total // pieces
    cols, width = w_mine.shape
    block = 1024
    whole = lambda x: pl.BlockSpec(x.shape, lambda i: (0,) * x.ndim)
    operands = (q_a, q_b, kv_a, kv_b, far_a, far_b)
    return pl.pallas_call(
        functools.partial(attend_kernel, pieces),
        grid=(width // block,),
        in_specs=[whole(x) for x in operands] + [pl.BlockSpec((cols, block), lambda i: (0, i))] * 2,
        out_specs=[pl.BlockSpec((rows, block), lambda i: (0, i))] * pieces,
        out_shape=[jax.ShapeDtypeStruct((rows, width), jnp.bfloat16)] * pieces,
        scratch_shapes=[
            pltpu.VMEM((2, total, cols), jnp.bfloat16),
            pltpu.VMEM((4, 2 * total, cols), jnp.bfloat16),
            pltpu.VMEM((total, 2 * cols), jnp.bfloat16),
        ],
        compiler_params=pltpu.CompilerParams(vmem_limit_bytes=32 * MIB),
        cost_estimate=pl.CostEstimate(
            flops=4 * total * cols * width + 16 * total * total * cols,
            bytes_accessed=4 * cols * width,
            transcendentals=8 * total * total,
        ),
    )(*operands, w_mine, w_other)


def body(latents, steps, leaving, fresh, mod_table, w_qkv, q_gain, k_gain, w_out):
    _, frames, local_rows, width = latents.shape
    rows = frames * local_rows
    own = latents.reshape(rows, width)
    normed, gate = norm_call(steps, own, mod_table)

    w_mine = w_qkv.transpose(1, 0, 2)
    q_gain, k_gain = q_gain[None], k_gain[None]
    q_other, k_other = hop(q_gain, dc=1), hop(k_gain, dc=1)
    gains = [q_gain, k_gain, q_other, k_other]
    w_send, out_send, _, _ = lax.optimization_barrier((w_mine, w_out, q_other, k_other))
    w_other = hop(w_send, dc=1)
    out_other = hop(out_send, dc=1)

    left = hop(normed, dx=1)
    right = hop(normed, dx=-1)
    far = hop(normed, dz=1)
    across = hop(normed, dx=2)
    far_left = hop(left, dz=1)
    far_right = hop(right, dz=1)
    far_across = hop(far, dx=2)

    q_a, kv_a, held = first_call([normed, left, right, far, across], gains, w_mine, w_other)
    far_a = hop(kv_a, dc=1)
    q_b, kv_b = rest_call([far_left, far_right, far_across], gains, held)
    far_b = hop(kv_b, dc=1)
    parts = attend_call(q_a, q_b, kv_a, kv_b, far_a, far_b, w_out, out_other, 8)
    p_own, p_left, p_right, p_far, p_across, p_far_left, p_far_right, p_far_across = parts

    def add(a, b):
        return (a.astype(jnp.float32) + b.astype(jnp.float32)).astype(jnp.bfloat16)

    s_left = add(p_left, hop(p_far_left, dz=1))
    s_right = add(p_right, hop(p_far_right, dz=1))
    s_far = add(p_far, hop(p_far_across, dx=2))
    arrived = [hop(p_across, dx=2), hop(s_left, dx=-1), hop(s_right, dx=1), hop(s_far, dz=1)]
    proj = p_own.astype(jnp.float32)
    for piece in arrived:
        proj = proj + piece.astype(jnp.float32)

    updated = (own.astype(jnp.float32) + gate * proj).astype(jnp.bfloat16).reshape(frames, local_rows, width)
    handed = lax.dynamic_slice_in_dim(updated, leaving[0], 1, axis=0)[0]
    arriving = from_behind(handed, "queue", 1)
    first = jnp.where(lax.axis_index("queue") == 0, fresh, arriving)
    select = jnp.arange(frames) == leaving[0]
    return jnp.where(select[:, None, None], first[None], updated)[None]


def solution(mesh):
    return jax.shard_map(
        body,
        mesh=mesh,
        in_specs=(
            P("queue", None, "seq", None),
            P("queue"),
            P("queue"),
            P("seq", None),
            P(),
            P(None, None, "seq"),
            P("seq"),
            P("seq"),
            P("seq", None),
        ),
        out_specs=P("queue", None, "seq", None),
        check_vma=False,
    )
```

time: 101 us -> 87.1 us (0.86)
  waiting for transfers between devices: 47.4 us -> 39.6 us
  other arithmetic: 8.5 us -> 1.35 us
  Pallas kernels: 13.4 us -> 16.6 us
  starting transfers between devices: 26.9 us -> 25.4 us
  local copies, waits for them, and re-layouts: 3.43 us -> 2.37 us
    ppermute x18 -> x20, waiting for transfers between devices: 42.4 us -> 34.7 us  [hop(): return lax.ppermute(value, 'seq', pairs)]
    pallas_call x1 -> x3, Pallas kernels: 8.62 us -> 11.7 us  [the longest x1 8.1 us: first_call(): pl.pallas_call(functools.partial(first_kernel, pieces), in_specs=[VMEM] *...]
    reduce_sum x2 -> x0, other arithmetic: 2.34 us -> none  [the longest x1 1.22 us: layer_norm_mod(): var = jnp.mean(centred * centred, axis=-1, keepdims=True)]
    ppermute x18 -> x20, starting transfers between devices: 23.4 us -> 21.9 us  [hop(): return lax.ppermute(value, 'seq', pairs)]
    slice x1 -> x0, other arithmetic: 1.23 us -> none  [body(): modrow[:, 2 * width:]]
    convert_element_type x1 -> x0, other arithmetic: 1.16 us -> none  [layer_norm_mod(): (centred * lax.rsqrt(var + 1e-06) * (1.0 + scale) + shift).astype(jnp.bfl...]
    unnamed x6 -> x16, local copies, waits for them, and re-layouts: 3.24 us -> 2.35 us
  transfers between devices with their start and end apart: 19 -> 21, of which waited for: 12 -> 13; matrix products, arithmetic and copies ran while one was open for 6% -> 0% of each run, Pallas kernels for 9% -> 14%
where the time goes in v2:
time: 87.1 us; the launch traced here: 86.8 us
  waiting for transfers between devices  39.6 us (45%)
  starting transfers between devices  25.4 us (29%)
  Pallas kernels  16.6 us (19%)
  local copies, waits for them, and re-layouts  2.37 us (3%)
  between operations  1.5 us (2%)
  other arithmetic  1.35 us (2%)
    ppermute x20, waiting for transfers between devices, hop(): return lax.ppermute(value, 'seq', pairs)  34.7 us
    ppermute x20, starting transfers between devices, hop(): return lax.ppermute(value, 'seq', pairs)  21.9 us
    pallas_call x1, Pallas kernels, first_call(): pl.pallas_call(functools.partial(first_kernel, pieces), in_specs=[VMEM] *...  8.1 us
    ppermute x1, waiting for transfers between devices, from_behind(): return lax.ppermute(x, axis, pairs)  4.95 us
    pallas_call x1, Pallas kernels, attend_call(): pl.pallas_call(functools.partial(attend_kernel, pieces), grid=(width // b...  4.86 us
    ppermute x1, starting transfers between devices, from_behind(): return lax.ppermute(x, axis, pairs)  3.48 us
    pallas_call x1, Pallas kernels, rest_call(): pl.pallas_call(functools.partial(rest_kernel, pieces), in_specs=[VMEM] *...  2.7 us
    unnamed x16, local copies, waits for them, and re-layouts  2.35 us
  transfers between devices with their start and end apart: 21, of which 13 were waited for; matrix products, arithmetic and copies ran while one was open for 0% of the time, Pallas kernels for 14%

profile of v2, /device:TPU:96, one launch (start us, length us, event | category | flops | bytes accessed | tf_op | source)
XLA Modules:
  0.0 86.8 jit_solution(14290281956726723923)
XLA Ops:
  0.0 0.0 collective-permute-start.4
  0.0 0.5 collective-permute-start.5
  0.5 0.8 collective-permute-done.4.refs_7_.refs_5_
  1.4 0.2 collective-permute-done.5.refs_8_.refs_6_
  1.5 0.3 collective-permute-start.6
  1.9 0.2 collective-permute-start.12
  2.7 0.0 copy-start.1
  2.7 1.0 %copy-done.1 = bf16[1,4,8,5120]{3,2,1,0:T(8,128)(2,1)S(1)} copy-done((bf16[1,4,8,5120]{3,2,1,0:T(8,128)(2,1)S(1)}, bf16[1,4,8,5120]{3,2,1,0:T(8,128)(2,1)}, u32[]{:S(2)}) %copy-start.1) | copy-done | bytes 327704
  3.7 0.9 %shard_map.91 = (bf16[32,5120]{1,0:T(8,128)(2,1)S(1)}, f32[1,5120]{1,0:T(1,128)S(1)}) custom-call(s32[1]{0:T(128)S(6)} %copy.10.step, bf16[32,5120]{1,0:T(8,128)(2,1)S(1)} %bitcast.16, f32[50,15360]{1,0:T(8,128)} %table.1), custom_call_target="tpu_custom_call" | custom-call | flops 1638400 | bytes 655360 | tf_op jit(solution)/shard_map/pallas_call | solution.py:51
  4.6 0.0 copy-start.4
  4.6 1.6 %collective-permute-start = (bf16[32,5120]{1,0:T(8,128)(2,1)S(1)}, bf16[32,5120]{1,0:T(8,128)(2,1)S(1)}, u32[]{:S(2)}, u32[]{:S(2)}) collective-permute-start(bf16[32,5120]{1,0:T(8,128)(2,1)S(1)} %get-tuple-element.23.refs_0_), channel_id=1, source_target_pairs={{0,2},{1,3},{2,4},{3,5},{4,6},{5,7},{6,0},{7,1},{8,10},{9,11},{10,... | collective-permute-start | bytes 983048 | tf_op jit(solution)/shard_map/ppermute | solution.py:25
  6.2 1.7 %collective-permute-start.1 = (bf16[32,5120]{1,0:T(8,128)(2,1)S(1)}, bf16[32,5120]{1,0:T(8,128)(2,1)S(1)}, u32[]{:S(2)}, u32[]{:S(2)}) collective-permute-start(bf16[32,5120]{1,0:T(8,128)(2,1)S(1)} %get-tuple-element.23.refs_0_), channel_id=1, source_target_pairs={{0,6},{1,7},{2,0},{3,1},{4,2},{5,3},{6,4},{7,5},{8,14},{9,15},{10,... | collective-permute-start | bytes 983048 | tf_op jit(solution)/shard_map/ppermute | solution.py:25
  7.9 0.6 collective-permute-start.2
  8.5 7.4 %collective-permute-done.refs_1_ = bf16[32,5120]{1,0:T(8,128)(2,1)S(1)} collective-permute-done((bf16[32,5120]{1,0:T(8,128)(2,1)S(1)}, bf16[32,5120]{1,0:T(8,128)(2,1)S(1)}, u32[]{:S(2)}, u32[]{:S(2)}) %collective-permute-start) | collective-permute-done | bytes 327712 | tf_op jit(solution)/shard_map/ppermute | solution.py:25
  15.8 1.8 %collective-permute-start.3 = (bf16[32,5120]{1,0:T(8,128)(2,1)S(1)}, bf16[32,5120]{1,0:T(8,128)(2,1)S(1)}, u32[]{:S(2)}, u32[]{:S(2)}) collective-permute-start(bf16[32,5120]{1,0:T(8,128)(2,1)S(1)} %get-tuple-element.23.refs_0_), channel_id=1, source_target_pairs={{0,4},{1,5},{2,6},{3,7},{4,0},{5,1},{6,2},{7,3},{8,12},{9,13},{10,... | collective-permute-start | bytes 983048 | tf_op jit(solution)/shard_map/ppermute | solution.py:25
  17.7 0.0 collective-permute-done.1.refs_2_
  17.7 0.6 collective-permute-start.7
  18.2 0.6 collective-permute-done.2.refs_3_
  18.8 2.4 %collective-permute-start.8 = (bf16[32,5120]{1,0:T(8,128)(2,1)S(1)}, bf16[32,5120]{1,0:T(8,128)(2,1)S(1)}, u32[]{:S(2)}, u32[]{:S(2)}) collective-permute-start(bf16[32,5120]{1,0:T(8,128)(2,1)S(1)} %collective-permute-done.1.refs_2_), channel_id=1, source_target_pairs={{0,8},{1,9},{2,10},{3,11},{4,12},{5,13},{6,14},{7,15},{8,0},{9,1},... | collective-permute-start | bytes 983048 | tf_op jit(solution)/shard_map/ppermute | solution.py:25
  21.2 5.3 %collective-permute-done.3.refs_4_ = bf16[32,5120]{1,0:T(8,128)(2,1)S(1)} collective-permute-done((bf16[32,5120]{1,0:T(8,128)(2,1)S(1)}, bf16[32,5120]{1,0:T(8,128)(2,1)S(1)}, u32[]{:S(2)}, u32[]{:S(2)}) %collective-permute-start.3) | collective-permute-done | bytes 327712 | tf_op jit(solution)/shard_map/ppermute | solution.py:25
  26.5 1.8 %collective-permute-start.9 = (bf16[32,5120]{1,0:T(8,128)(2,1)S(1)}, bf16[32,5120]{1,0:T(8,128)(2,1)S(1)}, u32[]{:S(2)}, u32[]{:S(2)}) collective-permute-start(bf16[32,5120]{1,0:T(8,128)(2,1)S(1)} %collective-permute-done.2.refs_3_), channel_id=1, source_target_pairs={{0,4},{1,5},{2,6},{3,7},{4,0},{5,1},{6,2},{7,3},{8,12},{9,13},{10,... | collective-permute-start | bytes 983048 | tf_op jit(solution)/shard_map/ppermute | solution.py:25
  28.3 0.0 collective-permute-done.6.refs_10_
  28.3 0.7 copy-done.3
  29.0 0.7 copy-done.5
  29.7 8.1 %shard_map.92 = (bf16[2,160,256]{2,1,0:T(8,128)(2,1)S(1)}, bf16[4,160,256]{2,1,0:T(8,128)(2,1)S(1)}, bf16[6,5120,256]{2,1,0:T(8,128)(2,1)S(1)}) custom-call(bf16[32,5120]{1,0:T(8,128)(2,1)S(1)} %get-tuple-element.23.refs_0_, bf16[32,5120]{1,0:T(8,128)(2,1)S(1)} %collective-permute-done.refs_1_, bf16[32,5120]{1,0:T(8,128)(2,1)S(1)} %collective-permute-done.1.refs_2_, ...), custom_call_target="tpu_custom_call" | custom-call | flops 2516582400 | bytes 15728640 | tf_op jit(solution)/shard_map/pallas_call | solution.py:123
  37.8 0.1 collective-permute-start.10
  37.9 0.0 collective-permute-done.7.refs_0_
  37.9 0.0 collective-permute-done.8.refs_1_
  37.9 0.0 collective-permute-done.9.refs_2_
  37.9 0.0 copy-done.6
  37.9 0.0 copy-done.4
  37.9 0.0 copy-start
  37.9 2.7 %shard_map.93 = (bf16[2,96,256]{2,1,0:T(8,128)(2,1)S(1)}, bf16[4,96,256]{2,1,0:T(8,128)(2,1)S(1)}) custom-call(bf16[32,5120]{1,0:T(8,128)(2,1)S(1)} %collective-permute-done.7.refs_0_, bf16[32,5120]{1,0:T(8,128)(2,1)S(1)} %collective-permute-done.8.refs_1_, bf16[32,5120]{1,0:T(8,128)(2,1)S(1)} %collective-permute-done.9.refs_2_, f32[1,256]{1,0:T(1,128)S(1)} %bitcast.20, ...), custom_call_target="tpu_custom_call" | custom-call | flops 1509949440 | bytes 15728640 | tf_op jit(solution)/shard_map/pallas_call | solution.py:145
  40.6 0.0 copy-start.2
  40.6 0.0 copy-start.7
  40.6 0.7 collective-permute-start.11
  41.4 0.0 collective-permute-done.12.w_other
  41.4 1.1 %collective-permute-done.11.far_b = bf16[4,96,256]{2,1,0:T(8,128)(2,1)S(1)} collective-permute-done((bf16[4,96,256]{2,1,0:T(8,128)(2,1)S(1)}, bf16[4,96,256]{2,1,0:T(8,128)(2,1)S(1)}, u32[]{:S(2)}, u32[]{:S(2)}) %collective-permute-start.11) | collective-permute-done | bytes 196640 | tf_op jit(solution)/shard_map/ppermute | solution.py:25
  42.5 0.0 collective-permute-done.10.far_a
  42.5 0.0 copy-done
  42.5 4.9 %shard_map.94 = (bf16[32,5120]{1,0:T(8,128)(2,1)S(1)}, bf16[32,5120]{1,0:T(8,128)(2,1)S(1)}, bf16[32,5120]{1,0:T(8,128)(2,1)S(1)}, bf16[32,5120]{1,0:T(8,128)(2,...) custom-call(bf16[2,160,256]{2,1,0:T(8,128)(2,1)S(1)} %get-tuple-elem, ...), custom_call_target="tpu_custom_call" | custom-call | flops 1610612736 | bytes 5242880 | tf_op jit(solution)/shard_map/pallas_call | solution.py:203
  47.3 0.7 collective-permute-start.14
  48.0 3.0 %collective-permute-start.16 = (bf16[32,5120]{1,0:T(8,128)(2,1)S(1)}, bf16[32,5120]{1,0:T(8,128)(2,1)S(1)}, u32[]{:S(2)}, u32[]{:S(2)}) collective-permute-start(bf16[32,5120]{1,0:T(8,128)(2,1)S(1)} %get-tuple-element.36), channel_id=1, source_target_pairs={{0,8},{1,9},{2,10},{3,11},{4,12},{5,13},{6,14},{7,15},{8,0},{9,1},... | collective-permute-start | bytes 983048 | tf_op jit(solution)/shard_map/ppermute | solution.py:25
  51.0 1.7 %collective-permute-start.18 = (bf16[32,5120]{1,0:T(8,128)(2,1)S(1)}, bf16[32,5120]{1,0:T(8,128)(2,1)S(1)}, u32[]{:S(2)}, u32[]{:S(2)}) collective-permute-start(bf16[32,5120]{1,0:T(8,128)(2,1)S(1)} %get-tuple-element.38), channel_id=1, source_target_pairs={{0,4},{1,5},{2,6},{3,7},{4,0},{5,1},{6,2},{7,3},{8,12},{9,13},{10,... | collective-permute-start | bytes 983048 | tf_op jit(solution)/shard_map/ppermute | solution.py:25
  52.7 1.8 %collective-permute-start.13 = (bf16[32,5120]{1,0:T(8,128)(2,1)S(1)}, bf16[32,5120]{1,0:T(8,128)(2,1)S(1)}, u32[]{:S(2)}, u32[]{:S(2)}) collective-permute-start(bf16[32,5120]{1,0:T(8,128)(2,1)S(1)} %get-tuple-element.32), channel_id=1, source_target_pairs={{0,4},{1,5},{2,6},{3,7},{4,0},{5,1},{6,2},{7,3},{8,12},{9,13},{10,... | collective-permute-start | bytes 983048 | tf_op jit(solution)/shard_map/ppermute | solution.py:25
  54.5 5.0 %collective-permute-done.14 = bf16[32,5120]{1,0:T(8,128)(2,1)S(1)} collective-permute-done((bf16[32,5120]{1,0:T(8,128)(2,1)S(1)}, bf16[32,5120]{1,0:T(8,128)(2,1)S(1)}, u32[]{:S(2)}, u32[]{:S(2)}) %collective-permute-start.14) | collective-permute-done | bytes 327712 | tf_op jit(solution)/shard_map/ppermute | solution.py:25
  59.5 0.1 add_convert_fusion.3
  59.5 1.2 %collective-permute-start.15 = (bf16[32,5120]{1,0:T(8,128)(2,1)S(1)}, bf16[32,5120]{1,0:T(8,128)(2,1)S(1)}, u32[]{:S(2)}, u32[]{:S(2)}) collective-permute-start(bf16[32,5120]{1,0:T(8,128)(2,1)S(1)} %add_convert_fusion.3), channel_id=1, source_target_pairs={{0,6},{1,7},{2,0},{3,1},{4,2},{5,3},{6,4},{7,5},{8,14},{9,15},{10,... | collective-permute-start | bytes 983048 | tf_op jit(solution)/shard_map/ppermute | solution.py:25
  60.8 5.2 %collective-permute-done.16 = bf16[32,5120]{1,0:T(8,128)(2,1)S(1)} collective-permute-done((bf16[32,5120]{1,0:T(8,128)(2,1)S(1)}, bf16[32,5120]{1,0:T(8,128)(2,1)S(1)}, u32[]{:S(2)}, u32[]{:S(2)}) %collective-permute-start.16) | collective-permute-done | bytes 327712 | tf_op jit(solution)/shard_map/ppermute | solution.py:25
  65.9 0.1 add_convert_fusion.2
  66.0 0.7 collective-permute-start.17
  66.7 0.0 collective-permute-done.18
  66.7 0.1 add_convert_fusion.1
  66.8 0.6 collective-permute-start.19
  68.1 0.9 collective-permute-done.13
  68.9 5.5 %collective-permute-done.15 = bf16[32,5120]{1,0:T(8,128)(2,1)S(1)} collective-permute-done((bf16[32,5120]{1,0:T(8,128)(2,1)S(1)}, bf16[32,5120]{1,0:T(8,128)(2,1)S(1)}, u32[]{:S(2)}, u32[]{:S(2)}) %collective-permute-start.15) | collective-permute-done | bytes 327712 | tf_op jit(solution)/shard_map/ppermute | solution.py:25
  74.4 2.0 %collective-permute-done.17 = bf16[32,5120]{1,0:T(8,128)(2,1)S(1)} collective-permute-done((bf16[32,5120]{1,0:T(8,128)(2,1)S(1)}, bf16[32,5120]{1,0:T(8,128)(2,1)S(1)}, u32[]{:S(2)}, u32[]{:S(2)}) %collective-permute-start.17) | collective-permute-done | bytes 327712 | tf_op jit(solution)/shard_map/ppermute | solution.py:25
  76.5 0.8 collective-permute-done.19
  77.2 0.0 copy-done.2
  77.2 0.3 add_convert_fusion
  77.6 3.5 %collective-permute-start.20 = (bf16[8,5120]{1,0:T(8,128)(2,1)S(1)}, bf16[8,5120]{1,0:T(8,128)(2,1)S(1)}, u32[]{:S(2)}, u32[]{:S(2)}) collective-permute-start(bf16[8,5120]{1,0:T(8,128)(2,1)S(1)} %dynamic-slice_bitcast_fusion), channel_id=1, source_target_pairs={{0,16},{16,32},{32,48},{48,64},{64,80},{80,96},{96,112},{1,17},{17... | collective-permute-start | bytes 245768 | tf_op jit(solution)/shard_map/ppermute | solution.py:31
  81.1 4.9 %collective-permute-done.20 = bf16[8,5120]{1,0:T(8,128)(2,1)S(1)} collective-permute-done((bf16[8,5120]{1,0:T(8,128)(2,1)S(1)}, bf16[8,5120]{1,0:T(8,128)(2,1)S(1)}, u32[]{:S(2)}, u32[]{:S(2)}) %collective-permute-start.20) | collective-permute-done | bytes 81952 | tf_op jit(solution)/shard_map/ppermute | solution.py:31
  86.0 0.0 copy-done.7
  86.0 0.8 bitcast_select_fusion
  (6 shorter events, 0.0 us)
Async XLA Ops:
  0.0 1.4 %collective-permute-start.4 = (f32[1,256]{1,0:T(1,128)}, f32[1,256]{1,0:T(1,128)S(1)}, u32[]{:S(2)}, u32[]{:S(2)}) collective-permute-start(f32[1,256]{1,0:T(1,128)} %bitcast.18), channel_id=1, source_target_pairs={{0,1},{1,0},{2,3},{3,2},{4,5},{5,4},{6,7},{7,6},{8,9},{9,8},{10,11... | collective-permute-start | bytes 3080 | tf_op jit(solution)/shard_map/ppermute | solution.py:25
  0.0 1.5 %collective-permute-start.5 = (f32[1,256]{1,0:T(1,128)}, f32[1,256]{1,0:T(1,128)S(1)}, u32[]{:S(2)}, u32[]{:S(2)}) collective-permute-start(f32[1,256]{1,0:T(1,128)} %bitcast.21), channel_id=1, source_target_pairs={{0,1},{1,0},{2,3},{3,2},{4,5},{5,4},{6,7},{7,6},{8,9},{9,8},{10,11... | collective-permute-start | bytes 3080 | tf_op jit(solution)/shard_map/ppermute | solution.py:25
  1.5 26.7 %collective-permute-start.6 = (bf16[3,5120,256]{2,1,0:T(8,128)(2,1)}, bf16[3,5120,256]{2,1,0:T(8,128)(2,1)}, u32[]{:S(2)}, u32[]{:S(2)}) collective-permute-start(bf16[3,5120,256]{2,1,0:T(8,128)(2,1)} %bitcast.24), channel_id=1, source_target_pairs={{0,1},{1,0},{2,3},{3,2},{4,5},{5,4},{6,7},{7,6},{8,9},{9,8},{10,11... | collective-permute-start | bytes 23592968 | tf_op jit(solution)/shard_map/ppermute | solution.py:25
  1.9 39.5 %collective-permute-start.12 = (bf16[256,5120]{1,0:T(8,128)(2,1)}, bf16[256,5120]{1,0:T(8,128)(2,1)S(1)}, u32[]{:S(2)}, u32[]{:S(2)}) collective-permute-start(bf16[256,5120]{1,0:T(8,128)(2,1)} %w_mine.1), channel_id=1, source_target_pairs={{0,1},{1,0},{2,3},{3,2},{4,5},{5,4},{6,7},{7,6},{8,9},{9,8},{10,11... | collective-permute-start | bytes 7864328 | tf_op jit(solution)/shard_map/ppermute | solution.py:25
  2.7 1.0 %copy-start.1 = (bf16[1,4,8,5120]{3,2,1,0:T(8,128)(2,1)S(1)}, bf16[1,4,8,5120]{3,2,1,0:T(8,128)(2,1)}, u32[]{:S(2)}) copy-start(bf16[1,4,8,5120]{3,2,1,0:T(8,128)(2,1)} %param.9) | copy-start | bytes 983044
  3.7 34.2 %copy-start.6 = (f32[256]{0:T(256)S(1)}, f32[256]{0:T(256)}, u32[]{:S(2)}) copy-start(f32[256]{0:T(256)} %param.16) | copy-start | bytes 3076
  4.6 33.3 %copy-start.4 = (f32[256]{0:T(256)S(1)}, f32[256]{0:T(256)}, u32[]{:S(2)}) copy-start(f32[256]{0:T(256)} %param.15) | copy-start | bytes 3076
  4.6 11.2 %collective-permute-start = (bf16[32,5120]{1,0:T(8,128)(2,1)S(1)}, bf16[32,5120]{1,0:T(8,128)(2,1)S(1)}, u32[]{:S(2)}, u32[]{:S(2)}) collective-permute-start(bf16[32,5120]{1,0:T(8,128)(2,1)S(1)} %get-tuple-element.23.refs_0_), channel_id=1, source_target_pairs={{0,2},{1,3},{2,4},{3,5},{4,6},{5,7},{6,0},{7,1},{8,10},{9,11},{10,... | collective-permute-start | bytes 983048 | tf_op jit(solution)/shard_map/ppermute | solution.py:25
  6.2 11.5 %collective-permute-start.1 = (bf16[32,5120]{1,0:T(8,128)(2,1)S(1)}, bf16[32,5120]{1,0:T(8,128)(2,1)S(1)}, u32[]{:S(2)}, u32[]{:S(2)}) collective-permute-start(bf16[32,5120]{1,0:T(8,128)(2,1)S(1)} %get-tuple-element.23.refs_0_), channel_id=1, source_target_pairs={{0,6},{1,7},{2,0},{3,1},{4,2},{5,3},{6,4},{7,5},{8,14},{9,15},{10,... | collective-permute-start | bytes 983048 | tf_op jit(solution)/shard_map/ppermute | solution.py:25
  7.9 10.9 %collective-permute-start.2 = (bf16[32,5120]{1,0:T(8,128)(2,1)S(1)}, bf16[32,5120]{1,0:T(8,128)(2,1)S(1)}, u32[]{:S(2)}, u32[]{:S(2)}) collective-permute-start(bf16[32,5120]{1,0:T(8,128)(2,1)S(1)} %get-tuple-element.23.refs_0_), channel_id=1, source_target_pairs={{0,8},{1,9},{2,10},{3,11},{4,12},{5,13},{6,14},{7,15},{8,0},{9,1},... | collective-permute-start | bytes 983048 | tf_op jit(solution)/shard_map/ppermute | solution.py:25
  15.8 10.6 %collective-permute-start.3 = (bf16[32,5120]{1,0:T(8,128)(2,1)S(1)}, bf16[32,5120]{1,0:T(8,128)(2,1)S(1)}, u32[]{:S(2)}, u32[]{:S(2)}) collective-permute-start(bf16[32,5120]{1,0:T(8,128)(2,1)S(1)} %get-tuple-element.23.refs_0_), channel_id=1, source_target_pairs={{0,4},{1,5},{2,6},{3,7},{4,0},{5,1},{6,2},{7,3},{8,12},{9,13},{10,... | collective-permute-start | bytes 983048 | tf_op jit(solution)/shard_map/ppermute | solution.py:25
  17.7 20.2 %collective-permute-start.7 = (bf16[32,5120]{1,0:T(8,128)(2,1)S(1)}, bf16[32,5120]{1,0:T(8,128)(2,1)S(1)}, u32[]{:S(2)}, u32[]{:S(2)}) collective-permute-start(bf16[32,5120]{1,0:T(8,128)(2,1)S(1)} %collective-permute-done.refs_1_), channel_id=1, source_target_pairs={{0,8},{1,9},{2,10},{3,11},{4,12},{5,13},{6,14},{7,15},{8,0},{9,1},... | collective-permute-start | bytes 983048 | tf_op jit(solution)/shard_map/ppermute | solution.py:25
  18.8 19.1 %collective-permute-start.8 = (bf16[32,5120]{1,0:T(8,128)(2,1)S(1)}, bf16[32,5120]{1,0:T(8,128)(2,1)S(1)}, u32[]{:S(2)}, u32[]{:S(2)}) collective-permute-start(bf16[32,5120]{1,0:T(8,128)(2,1)S(1)} %collective-permute-done.1.refs_2_), channel_id=1, source_target_pairs={{0,8},{1,9},{2,10},{3,11},{4,12},{5,13},{6,14},{7,15},{8,0},{9,1},... | collective-permute-start | bytes 983048 | tf_op jit(solution)/shard_map/ppermute | solution.py:25
  26.5 11.4 %collective-permute-start.9 = (bf16[32,5120]{1,0:T(8,128)(2,1)S(1)}, bf16[32,5120]{1,0:T(8,128)(2,1)S(1)}, u32[]{:S(2)}, u32[]{:S(2)}) collective-permute-start(bf16[32,5120]{1,0:T(8,128)(2,1)S(1)} %collective-permute-done.2.refs_3_), channel_id=1, source_target_pairs={{0,4},{1,5},{2,6},{3,7},{4,0},{5,1},{6,2},{7,3},{8,12},{9,13},{10,... | collective-permute-start | bytes 983048 | tf_op jit(solution)/shard_map/ppermute | solution.py:25
  28.3 0.7 copy-start.3
  29.0 0.7 copy-start.5
  37.8 4.7 %collective-permute-start.10 = (bf16[4,160,256]{2,1,0:T(8,128)(2,1)S(1)}, bf16[4,160,256]{2,1,0:T(8,128)(2,1)S(1)}, u32[]{:S(2)}, u32[]{:S(2)}) collective-permute-start(bf16[4,160,256]{2,1,0:T(8,128)(2,1)S(1)} %get-tuple-element.28.kv_a), channel_id=1, source_target_pairs={{0,1},{1,0},{2,3},{3,2},{4,5},{5,4},{6,7},{7,6},{8,9},{9,8},{10,11... | collective-permute-start | bytes 983048 | tf_op jit(solution)/shard_map/ppermute | solution.py:25
  37.9 4.6 %copy-start = (bf16[256,5120]{1,0:T(8,128)(2,1)S(1)}, bf16[256,5120]{1,0:T(8,128)(2,1)}, u32[]{:S(2)}) copy-start(bf16[256,5120]{1,0:T(8,128)(2,1)} %w_mine.1) | copy-start | bytes 7864324
  40.6 36.6 %copy-start.2 = (bf16[1,4,8,5120]{3,2,1,0:T(8,128)(2,1)S(1)}, bf16[1,4,8,5120]{3,2,1,0:T(8,128)(2,1)}, u32[]{:S(2)}) copy-start(bf16[1,4,8,5120]{3,2,1,0:T(8,128)(2,1)} %param.9) | copy-start | bytes 983044
  40.6 45.4 %copy-start.7 = (bf16[8,5120]{1,0:T(8,128)(2,1)S(1)}, bf16[8,5120]{1,0:T(8,128)(2,1)}, u32[]{:S(2)}) copy-start(bf16[8,5120]{1,0:T(8,128)(2,1)} %param.12) | copy-start | bytes 245764
  40.6 1.8 %collective-permute-start.11 = (bf16[4,96,256]{2,1,0:T(8,128)(2,1)S(1)}, bf16[4,96,256]{2,1,0:T(8,128)(2,1)S(1)}, u32[]{:S(2)}, u32[]{:S(2)}) collective-permute-start(bf16[4,96,256]{2,1,0:T(8,128)(2,1)S(1)} %get-tuple-element.29.kv_b), channel_id=1, source_target_pairs={{0,1},{1,0},{2,3},{3,2},{4,5},{5,4},{6,7},{7,6},{8,9},{9,8},{10,11... | collective-permute-start | bytes 589832 | tf_op jit(solution)/shard_map/ppermute | solution.py:25
  47.3 12.1 %collective-permute-start.14 = (bf16[32,5120]{1,0:T(8,128)(2,1)S(1)}, bf16[32,5120]{1,0:T(8,128)(2,1)S(1)}, u32[]{:S(2)}, u32[]{:S(2)}) collective-permute-start(bf16[32,5120]{1,0:T(8,128)(2,1)S(1)} %get-tuple-element.34), channel_id=1, source_target_pairs={{0,8},{1,9},{2,10},{3,11},{4,12},{5,13},{6,14},{7,15},{8,0},{9,1},... | collective-permute-start | bytes 983048 | tf_op jit(solution)/shard_map/ppermute | solution.py:25
  48.0 18.0 %collective-permute-start.16 = (bf16[32,5120]{1,0:T(8,128)(2,1)S(1)}, bf16[32,5120]{1,0:T(8,128)(2,1)S(1)}, u32[]{:S(2)}, u32[]{:S(2)}) collective-permute-start(bf16[32,5120]{1,0:T(8,128)(2,1)S(1)} %get-tuple-element.36), channel_id=1, source_target_pairs={{0,8},{1,9},{2,10},{3,11},{4,12},{5,13},{6,14},{7,15},{8,0},{9,1},... | collective-permute-start | bytes 983048 | tf_op jit(solution)/shard_map/ppermute | solution.py:25
  51.0 15.7 %collective-permute-start.18 = (bf16[32,5120]{1,0:T(8,128)(2,1)S(1)}, bf16[32,5120]{1,0:T(8,128)(2,1)S(1)}, u32[]{:S(2)}, u32[]{:S(2)}) collective-permute-start(bf16[32,5120]{1,0:T(8,128)(2,1)S(1)} %get-tuple-element.38), channel_id=1, source_target_pairs={{0,4},{1,5},{2,6},{3,7},{4,0},{5,1},{6,2},{7,3},{8,12},{9,13},{10,... | collective-permute-start | bytes 983048 | tf_op jit(solution)/shard_map/ppermute | solution.py:25
  52.7 16.2 %collective-permute-start.13 = (bf16[32,5120]{1,0:T(8,128)(2,1)S(1)}, bf16[32,5120]{1,0:T(8,128)(2,1)S(1)}, u32[]{:S(2)}, u32[]{:S(2)}) collective-permute-start(bf16[32,5120]{1,0:T(8,128)(2,1)S(1)} %get-tuple-element.32), channel_id=1, source_target_pairs={{0,4},{1,5},{2,6},{3,7},{4,0},{5,1},{6,2},{7,3},{8,12},{9,13},{10,... | collective-permute-start | bytes 983048 | tf_op jit(solution)/shard_map/ppermute | solution.py:25
  59.5 14.9 %collective-permute-start.15 = (bf16[32,5120]{1,0:T(8,128)(2,1)S(1)}, bf16[32,5120]{1,0:T(8,128)(2,1)S(1)}, u32[]{:S(2)}, u32[]{:S(2)}) collective-permute-start(bf16[32,5120]{1,0:T(8,128)(2,1)S(1)} %add_convert_fusion.3), channel_id=1, source_target_pairs={{0,6},{1,7},{2,0},{3,1},{4,2},{5,3},{6,4},{7,5},{8,14},{9,15},{10,... | collective-permute-start | bytes 983048 | tf_op jit(solution)/shard_map/ppermute | solution.py:25
  66.0 10.5 %collective-permute-start.17 = (bf16[32,5120]{1,0:T(8,128)(2,1)S(1)}, bf16[32,5120]{1,0:T(8,128)(2,1)S(1)}, u32[]{:S(2)}, u32[]{:S(2)}) collective-permute-start(bf16[32,5120]{1,0:T(8,128)(2,1)S(1)} %add_convert_fusion.2), channel_id=1, source_target_pairs={{0,2},{1,3},{2,4},{3,5},{4,6},{5,7},{6,0},{7,1},{8,10},{9,11},{10,... | collective-permute-start | bytes 983048 | tf_op jit(solution)/shard_map/ppermute | solution.py:25
  66.8 10.5 %collective-permute-start.19 = (bf16[32,5120]{1,0:T(8,128)(2,1)S(1)}, bf16[32,5120]{1,0:T(8,128)(2,1)S(1)}, u32[]{:S(2)}, u32[]{:S(2)}) collective-permute-start(bf16[32,5120]{1,0:T(8,128)(2,1)S(1)} %add_convert_fusion.1), channel_id=1, source_target_pairs={{0,8},{1,9},{2,10},{3,11},{4,12},{5,13},{6,14},{7,15},{8,0},{9,1},... | collective-permute-start | bytes 983048 | tf_op jit(solution)/shard_map/ppermute | solution.py:25
  77.6 8.4 %collective-permute-start.20 = (bf16[8,5120]{1,0:T(8,128)(2,1)S(1)}, bf16[8,5120]{1,0:T(8,128)(2,1)S(1)}, u32[]{:S(2)}, u32[]{:S(2)}) collective-permute-start(bf16[8,5120]{1,0:T(8,128)(2,1)S(1)} %dynamic-slice_bitcast_fusion), channel_id=1, source_target_pairs={{0,16},{16,32},{32,48},{48,64},{64,80},{80,96},{96,112},{1,17},{17... | collective-permute-start | bytes 245768 | tf_op jit(solution)/shard_map/ppermute | solution.py:31

commit v3 on v2

v3 whole, which is shorter than its diff:
```python
import functools

import jax
import jax.numpy as jnp
from jax import lax
from jax.experimental import pallas as pl
from jax.experimental.pallas import tpu as pltpu
from jax.sharding import PartitionSpec as P

HEAD_DIM = 128
Z_CHIPS, X_CHIPS, CORES = 2, 4, 2
MIB = 1 << 20
ANY = pl.BlockSpec(memory_space=pl.ANY)
VMEM = pl.BlockSpec(memory_space=pltpu.VMEM)
SMEM = pl.BlockSpec(memory_space=pltpu.SMEM)


def hop(value, dz=0, dx=0, dc=0):
    pairs = []
    for z in range(Z_CHIPS):
        for x in range(X_CHIPS):
            for c in range(CORES):
                to_z, to_x, to_c = (z + dz) % Z_CHIPS, (x + dx) % X_CHIPS, (c + dc) % CORES
                pairs.append(((z * X_CHIPS + x) * CORES + c, (to_z * X_CHIPS + to_x) * CORES + to_c))
    return lax.ppermute(value, "seq", pairs)


def from_behind(x, axis, by):
    count = lax.axis_size(axis)
    pairs = [(i, i + by) for i in range(count) if 0 <= i + by < count]
    return lax.ppermute(x, axis, pairs)


def norm_kernel(step, x_hbm, table, q_hbm, k_hbm, out_ref, gate_ref, gain_ref, x_ref, row, q_ref, k_ref, sems):
    width = x_hbm.shape[-1]
    moves = [(x_hbm, x_ref), (table.at[pl.ds(step[0], 1), :], row), (q_hbm, q_ref), (k_hbm, k_ref)]
    copies = [pltpu.make_async_copy(src, dst, sems.at[i]) for i, (src, dst) in enumerate(moves)]
    for copy in copies:
        copy.start()
    copies[0].wait()
    values = x_ref[...].astype(jnp.float32)
    mean = jnp.mean(values, axis=-1, keepdims=True)
    centred = values - mean
    var = jnp.mean(centred * centred, axis=-1, keepdims=True)
    scaled = centred * lax.rsqrt(var + 1e-06)
    for copy in copies[1:]:
        copy.wait()
    shift, scale = row[:, :width], row[:, width : 2 * width]
    out_ref[...] = (scaled * (1.0 + scale) + shift).astype(jnp.bfloat16)
    gate_ref[...] = row[:, 2 * width :]
    gain_ref[0:1, :] = q_ref[...]
    gain_ref[1:2, :] = k_ref[...]


def norm_call(step, x, table, q_gain, k_gain):
    rows, width = x.shape
    cols = q_gain.shape[1]
    in_hbm = lambda array: pltpu.with_memory_space_constraint(array, pltpu.HBM)
    return pl.pallas_call(
        norm_kernel,
        in_specs=[SMEM] + [ANY] * 4,
        out_specs=[VMEM] * 3,
        out_shape=[
            jax.ShapeDtypeStruct((rows, width), jnp.bfloat16),
            jax.ShapeDtypeStruct((1, width), jnp.float32),
            jax.ShapeDtypeStruct((2, cols), jnp.float32),
        ],
        scratch_shapes=[
            pltpu.VMEM((rows, width), jnp.bfloat16),
            pltpu.VMEM((1, 3 * width), jnp.float32),
            pltpu.VMEM((1, cols), jnp.float32),
            pltpu.VMEM((1, cols), jnp.float32),
            pltpu.SemaphoreType.DMA((4,)),
        ],
        compiler_params=pltpu.CompilerParams(vmem_limit_bytes=8 * MIB),
        cost_estimate=pl.CostEstimate(flops=10 * rows * width, bytes_accessed=4 * rows * width, transcendentals=0),
    )(step, in_hbm(x), in_hbm(table), in_hbm(q_gain), in_hbm(k_gain))


def head_norm(values, gain):
    out = []
    for at in range(0, values.shape[1], HEAD_DIM):
        part = values[:, at : at + HEAD_DIM]
        power = jnp.mean(part * part, axis=-1, keepdims=True)
        out.append(part * lax.rsqrt(power + 1e-06) * gain[:, at : at + HEAD_DIM])
    return jnp.concatenate(out, axis=1)


def project(i, rows_ref, weights, gains, q_ref, kv_ref):
    owner, kind = divmod(i, 3)
    acc = jnp.dot(rows_ref[...], weights[i], preferred_element_type=jnp.float32)
    if kind < 2:
        acc = head_norm(acc, gains[owner][kind : kind + 1, :])
    if kind == 0:
        q_ref[owner] = acc.astype(jnp.bfloat16)
    else:
        kv_ref[2 * owner + kind - 1] = acc.astype(jnp.bfloat16)


def gather_rows(xs, rows_ref):
    rows = xs[0].shape[0]
    for i, x in enumerate(xs):
        rows_ref[i * rows : (i + 1) * rows, :] = x[...]


def first_kernel(pieces, *refs):
    xs, gains = refs[:pieces], refs[pieces : pieces + 2]
    w_mine, w_other, q_ref, kv_ref, held, rows_ref, sems = refs[pieces + 2 :]
    copies = []
    for i in range(6):
        copies.append(pltpu.make_async_copy((w_mine, w_other)[i // 3].at[i % 3], held.at[i], sems.at[i]))
        copies[i].start()
    gather_rows(xs, rows_ref)
    for i in range(6):
        copies[i].wait()
        project(i, rows_ref, held, gains, q_ref, kv_ref)


def rest_kernel(pieces, *refs):
    xs, gains = refs[:pieces], refs[pieces : pieces + 2]
    held, q_ref, kv_ref, rows_ref = refs[pieces + 2 :]
    gather_rows(xs, rows_ref)
    for i in range(6):
        project(i, rows_ref, held, gains, q_ref, kv_ref)


def qkv_shapes(total, cols):
    return [
        jax.ShapeDtypeStruct((2, total, cols), jnp.bfloat16),
        jax.ShapeDtypeStruct((4, total, cols), jnp.bfloat16),
    ]


def first_call(xs, gains, w_mine, w_other):
    pieces = len(xs)
    rows, width = xs[0].shape
    total, cols = rows * pieces, w_mine.shape[2]
    return pl.pallas_call(
        functools.partial(first_kernel, pieces),
        in_specs=[VMEM] * (pieces + 2) + [ANY, ANY],
        out_specs=[VMEM] * 3,
        out_shape=qkv_shapes(total, cols) + [pltpu.VMEM((6, width, cols), jnp.bfloat16)],
        scratch_shapes=[pltpu.VMEM((total, width), jnp.bfloat16), pltpu.SemaphoreType.DMA((6,))],
        compiler_params=pltpu.CompilerParams(vmem_limit_bytes=24 * MIB),
        cost_estimate=pl.CostEstimate(
            flops=40 * 12 * total * width * cols, bytes_accessed=12 * width * cols, transcendentals=0
        ),
    )(
        *xs,
        *gains,
        pltpu.with_memory_space_constraint(w_mine, pltpu.HBM),
        w_other,
    )


def rest_call(xs, gains, held):
    pieces = len(xs)
    rows, width = xs[0].shape
    total, cols = rows * pieces, held.shape[2]
    return pl.pallas_call(
        functools.partial(rest_kernel, pieces),
        in_specs=[VMEM] * (pieces + 3),
        out_specs=[VMEM] * 2,
        out_shape=qkv_shapes(total, cols),
        scratch_shapes=[pltpu.VMEM((total, width), jnp.bfloat16)],
        compiler_params=pltpu.CompilerParams(vmem_limit_bytes=24 * MIB),
        cost_estimate=pl.CostEstimate(
            flops=12 * total * width * cols, bytes_accessed=12 * width * cols, transcendentals=0
        ),
    )(*xs, *gains, pltpu.with_memory_space_constraint(held, pltpu.VMEM))


def attend(q_ref, kv_ref, attn_ref):
    cols = q_ref.shape[2]
    contract = (((1,), (1,)), ((), ()))
    for owner in range(2):
        for at in range(0, cols, HEAD_DIM):
            span = slice(at, at + HEAD_DIM)
            scores = lax.dot_general(
                q_ref[owner, :, span], kv_ref[2 * owner, :, span], contract, preferred_element_type=jnp.float32
            ) * HEAD_DIM ** (-0.5)
            top = jnp.max(scores, axis=-1, keepdims=True)
            expo = jnp.exp(scores - top)
            total = jnp.sum(expo, axis=-1, keepdims=True)
            prob = (expo * (1.0 / total)).astype(jnp.bfloat16)
            value = jnp.dot(prob, kv_ref[2 * owner + 1, :, span], preferred_element_type=jnp.float32)
            attn_ref[:, owner * cols + at : owner * cols + at + HEAD_DIM] = value.astype(jnp.bfloat16)


def out_project(attn_ref, w_mine, w_other, outs):
    rows, cols = outs[0].shape[0], w_mine.shape[0]
    part = jnp.dot(attn_ref[:, :cols], w_mine[...], preferred_element_type=jnp.float32)
    part += jnp.dot(attn_ref[:, cols:], w_other[...], preferred_element_type=jnp.float32)
    part = part.astype(jnp.bfloat16)
    for i, out in enumerate(outs):
        out[...] = part[i * rows : (i + 1) * rows, :]


def far_kernel(pieces, q_a, q_b, kv_a, kv_b, far_a, far_b, w_mine, w_other, *refs):
    outs, (kv_ref, q_ref, attn_ref) = refs[:pieces], refs[pieces:]

    @pl.when(pl.program_id(0) == 0)
    def _():
        cut, most = q_a.shape[1], q_b.shape[1]
        half, tail = cut + most, q_ref.shape[1] - most
        for owner in range(2):
            q_ref[owner, :most, :] = q_b[owner]
            q_ref[owner, most:, :] = q_a[owner, cut - tail :, :]
            for kind in range(2):
                near, far = 2 * owner + kind, 2 * (1 - owner) + kind
                kv_ref[near, :cut, :] = kv_a[near]
                kv_ref[near, cut:half, :] = kv_b[near]
                kv_ref[near, half : half + cut, :] = far_a[far]
                kv_ref[near, half + cut :, :] = far_b[far]
        attend(q_ref, kv_ref, attn_ref)

    out_project(attn_ref, w_mine, w_other, outs)


def near_kernel(pieces, q_a, kv_ref, w_mine, w_other, *refs):
    outs, (q_ref, attn_ref) = refs[:pieces], refs[pieces:]

    @pl.when(pl.program_id(0) == 0)
    def _():
        q_ref[...] = q_a[:, : q_ref.shape[1], :]
        attend(q_ref, kv_ref, attn_ref)

    out_project(attn_ref, w_mine, w_other, outs)


def attend_call(kernel, operands, w_mine, w_other, rows, pieces, keys=None):
    cols, width = w_mine.shape
    total, block = rows * pieces, 1024
    whole = lambda shape: pl.BlockSpec(shape, lambda i: (0,) * len(shape))
    length = 2 * 8 * rows
    out_shape = [jax.ShapeDtypeStruct((rows, width), jnp.bfloat16)] * pieces
    out_specs = [pl.BlockSpec((rows, block), lambda i: (0, i))] * pieces
    if keys is not None:
        out_shape = out_shape + [jax.ShapeDtypeStruct(keys, jnp.bfloat16)]
        out_specs = out_specs + [whole(keys)]
    return pl.pallas_call(
        functools.partial(kernel, pieces),
        grid=(width // block,),
        in_specs=[whole(x.shape) for x in operands] + [pl.BlockSpec((cols, block), lambda i: (0, i))] * 2,
        out_specs=out_specs,
        out_shape=out_shape,
        scratch_shapes=[
            pltpu.VMEM((2, total, cols), jnp.bfloat16),
            pltpu.VMEM((total, 2 * cols), jnp.bfloat16),
        ],
        compiler_params=pltpu.CompilerParams(vmem_limit_bytes=24 * MIB),
        cost_estimate=pl.CostEstimate(
            flops=4 * total * cols * width + 8 * total * length * cols,
            bytes_accessed=4 * cols * width,
            transcendentals=4 * total * length,
        ),
    )(*operands, w_mine, w_other)


def body(latents, steps, leaving, fresh, mod_table, w_qkv, q_gain, k_gain, w_out):
    _, frames, local_rows, width = latents.shape
    rows = frames * local_rows
    own = latents.reshape(rows, width)
    normed, gate, gain = norm_call(steps, own, mod_table, q_gain[None], k_gain[None])

    w_mine = w_qkv.transpose(1, 0, 2)
    gains = [gain, hop(gain, dc=1)]
    w_send, _ = lax.optimization_barrier((w_mine, gains[1]))
    w_other = hop(w_send, dc=1)

    left = hop(normed, dx=1)
    right = hop(normed, dx=-1)
    far = hop(normed, dz=1)
    across = hop(normed, dx=2)
    far_left = hop(left, dz=1)
    right_send, out_send, _ = lax.optimization_barrier((right, w_out, w_other))
    far_right = hop(right_send, dz=1)
    far_across = hop(far, dx=2)

    out_other = hop(out_send, dc=1)

    q_a, kv_a, held = first_call([normed, left, right, far, across], gains, w_mine, w_other)
    far_a = hop(kv_a, dc=1)
    q_b, kv_b = rest_call([far_left, far_right, far_across], gains, held)
    far_b = hop(kv_b, dc=1)
    keys = (4, 16 * rows, kv_a.shape[2])
    operands = (q_a, q_b, kv_a, kv_b, far_a, far_b)
    p_far_left, p_far_right, p_far_across, p_across, kv = attend_call(
        far_kernel, operands, w_out, out_other, rows, 4, keys
    )
    p_own, p_left, p_right, p_far = attend_call(near_kernel, (q_a, kv), w_out, out_other, rows, 4)

    def add(a, b):
        return (a.astype(jnp.float32) + b.astype(jnp.float32)).astype(jnp.bfloat16)

    s_left = add(p_left, hop(p_far_left, dz=1))
    s_right = add(p_right, hop(p_far_right, dz=1))
    s_far = add(p_far, hop(p_far_across, dx=2))
    arrived = [hop(p_across, dx=2), hop(s_left, dx=-1), hop(s_right, dx=1), hop(s_far, dz=1)]
    proj = p_own.astype(jnp.float32)
    for piece in arrived:
        proj = proj + piece.astype(jnp.float32)

    updated = (own.astype(jnp.float32) + gate * proj).astype(jnp.bfloat16).reshape(frames, local_rows, width)
    handed = lax.dynamic_slice_in_dim(updated, leaving[0], 1, axis=0)[0]
    arriving = from_behind(handed, "queue", 1)
    first = jnp.where(lax.axis_index("queue") == 0, fresh, arriving)
    select = jnp.arange(frames) == leaving[0]
    return jnp.where(select[:, None, None], first[None], updated)[None]


def solution(mesh):
    return jax.shard_map(
        body,
        mesh=mesh,
        in_specs=(
            P("queue", None, "seq", None),
            P("queue"),
            P("queue"),
            P("seq", None),
            P(),
            P(None, None, "seq"),
            P("seq"),
            P("seq"),
            P("seq", None),
        ),
        out_specs=P("queue", None, "seq", None),
        check_vma=False,
    )
```

time: 87.1 us -> 95 us (1.091); the launches traced: 86.8 us -> 93.3 us
  local copies, waits for them, and re-layouts: 2.37 us -> 6.32 us
  Pallas kernels: 16.6 us -> 19.7 us
  waiting for transfers between devices: 39.6 us -> 36.6 us
  starting transfers between devices: 25.4 us -> 27.9 us
    unnamed x16 -> x10, local copies, waits for them, and re-layouts: 2.35 us -> 6.3 us
    ppermute x20 -> x19, waiting for transfers between devices: 34.7 us -> 31.7 us  [hop(): return lax.ppermute(value, 'seq', pairs)]
    pallas_call x2 -> x3, Pallas kernels: 5.79 us -> 8.77 us  [the longest x2 7.36 us: attend_call(): pl.pallas_call(functools.partial(kernel, pieces), grid=(width // block,),...]
    ppermute x20 -> x19, starting transfers between devices: 21.9 us -> 24.4 us  [hop(): return lax.ppermute(value, 'seq', pairs)]
  transfers between devices with their start and end apart: 21 -> 20, of which waited for: 13 -> 10; matrix products, arithmetic and copies ran while one was open for 0% -> 0% of each run, Pallas kernels for 14% -> 16%
where the time goes in v3:
time: 95 us; the launch traced here: 93.3 us
  waiting for transfers between devices  36.6 us (39%)
  starting transfers between devices  27.9 us (29%)
  Pallas kernels  19.7 us (21%)
  local copies, waits for them, and re-layouts  6.32 us (7%)
  between operations  1.47 us (2%)
  other arithmetic  1.35 us (1%)
    ppermute x19, waiting for transfers between devices, hop(): return lax.ppermute(value, 'seq', pairs)  31.7 us
    ppermute x19, starting transfers between devices, hop(): return lax.ppermute(value, 'seq', pairs)  24.4 us
    pallas_call x1, Pallas kernels, first_call(): pl.pallas_call(functools.partial(first_kernel, pieces), in_specs=[VMEM] *...  8.13 us
    pallas_call x2, Pallas kernels, attend_call(): pl.pallas_call(functools.partial(kernel, pieces), grid=(width // block,),...  7.36 us
    unnamed x10, local copies, waits for them, and re-layouts  6.3 us
    ppermute x1, waiting for transfers between devices, from_behind(): return lax.ppermute(x, axis, pairs)  4.94 us
    ppermute x1, starting transfers between devices, from_behind(): return lax.ppermute(x, axis, pairs)  3.49 us
    pallas_call x1, Pallas kernels, rest_call(): pl.pallas_call(functools.partial(rest_kernel, pieces), in_specs=[VMEM] *...  2.76 us
  transfers between devices with their start and end apart: 20, of which 10 were waited for; matrix products, arithmetic and copies ran while one was open for 0% of the time, Pallas kernels for 16%

profile of v3, /device:TPU:96, one launch (start us, length us, event | category | flops | bytes accessed | tf_op | source)
XLA Modules:
  0.0 93.3 jit_solution(13127093811937096850)
XLA Ops:
  0.7 1.4 %shard_map.91 = (bf16[32,5120]{1,0:T(8,128)(2,1)S(1)}, f32[1,5120]{1,0:T(1,128)S(1)}, f32[2,256]{1,0:T(2,128)S(1)}) custom-call(s32[1]{0:T(128)S(6)} %copy.10.step, bf16[32,5120]{1,0:T(8,128)(2,1)} %bitcast.18, f32[50,15360]{1,0:T(8,128)} %table.1, f32[1,256]{1,0:T(1,128)} %bitcast.19, f32[1,256]{1,0:T(1,128)} %bitcast.20), custom_call_target="tpu_custom_call" | custom-call | flops 1638400 | bytes 655360 | tf_op jit(solution)/shard_map/pallas_call | solution.py:59
  2.1 0.1 collective-permute-start.4
  2.2 1.1 %collective-permute-done.4.refs_6_.refs_4_ = f32[2,256]{1,0:T(2,128)S(1)} collective-permute-done((f32[2,256]{1,0:T(2,128)S(1)}, f32[2,256]{1,0:T(2,128)S(1)}, u32[]{:S(2)}, u32[]{:S(2)}) %collective-permute-start.4) | collective-permute-done | bytes 2080 | tf_op jit(solution)/shard_map/ppermute | solution.py:25
  3.3 0.2 collective-permute-start.5
  3.5 1.5 %collective-permute-start = (bf16[32,5120]{1,0:T(8,128)(2,1)S(1)}, bf16[32,5120]{1,0:T(8,128)(2,1)S(1)}, u32[]{:S(2)}, u32[]{:S(2)}) collective-permute-start(bf16[32,5120]{1,0:T(8,128)(2,1)S(1)} %get-tuple-element.26.refs_0_), channel_id=1, source_target_pairs={{0,2},{1,3},{2,4},{3,5},{4,6},{5,7},{6,0},{7,1},{8,10},{9,11},{10,... | collective-permute-start | bytes 983048 | tf_op jit(solution)/shard_map/ppermute | solution.py:25
  5.0 0.6 collective-permute-start.2
  5.5 1.7 %collective-permute-start.1 = (bf16[32,5120]{1,0:T(8,128)(2,1)S(1)}, bf16[32,5120]{1,0:T(8,128)(2,1)S(1)}, u32[]{:S(2)}, u32[]{:S(2)}) collective-permute-start(bf16[32,5120]{1,0:T(8,128)(2,1)S(1)} %get-tuple-element.26.refs_0_), channel_id=1, source_target_pairs={{0,6},{1,7},{2,0},{3,1},{4,2},{5,3},{6,4},{7,5},{8,14},{9,15},{10,... | collective-permute-start | bytes 983048 | tf_op jit(solution)/shard_map/ppermute | solution.py:25
  7.3 1.8 %collective-permute-start.3 = (bf16[32,5120]{1,0:T(8,128)(2,1)S(1)}, bf16[32,5120]{1,0:T(8,128)(2,1)S(1)}, u32[]{:S(2)}, u32[]{:S(2)}) collective-permute-start(bf16[32,5120]{1,0:T(8,128)(2,1)S(1)} %get-tuple-element.26.refs_0_), channel_id=1, source_target_pairs={{0,4},{1,5},{2,6},{3,7},{4,0},{5,1},{6,2},{7,3},{8,12},{9,13},{10,... | collective-permute-start | bytes 983048 | tf_op jit(solution)/shard_map/ppermute | solution.py:25
  9.1 5.6 %collective-permute-done.refs_1_ = bf16[32,5120]{1,0:T(8,128)(2,1)S(1)} collective-permute-done((bf16[32,5120]{1,0:T(8,128)(2,1)S(1)}, bf16[32,5120]{1,0:T(8,128)(2,1)S(1)}, u32[]{:S(2)}, u32[]{:S(2)}) %collective-permute-start) | collective-permute-done | bytes 327712 | tf_op jit(solution)/shard_map/ppermute | solution.py:25
  14.6 0.6 collective-permute-start.6
  15.2 1.0 %collective-permute-done.2.refs_3_ = bf16[32,5120]{1,0:T(8,128)(2,1)S(1)} collective-permute-done((bf16[32,5120]{1,0:T(8,128)(2,1)S(1)}, bf16[32,5120]{1,0:T(8,128)(2,1)S(1)}, u32[]{:S(2)}, u32[]{:S(2)}) %collective-permute-start.2) | collective-permute-done | bytes 327712 | tf_op jit(solution)/shard_map/ppermute | solution.py:25
  16.1 2.7 %collective-permute-start.8 = (bf16[32,5120]{1,0:T(8,128)(2,1)S(1)}, bf16[32,5120]{1,0:T(8,128)(2,1)S(1)}, u32[]{:S(2)}, u32[]{:S(2)}) collective-permute-start(bf16[32,5120]{1,0:T(8,128)(2,1)S(1)} %collective-permute-done.2.refs_3_), channel_id=1, source_target_pairs={{0,4},{1,5},{2,6},{3,7},{4,0},{5,1},{6,2},{7,3},{8,12},{9,13},{10,... | collective-permute-start | bytes 983048 | tf_op jit(solution)/shard_map/ppermute | solution.py:25
  18.9 9.4 %collective-permute-done.1.refs_2_ = bf16[32,5120]{1,0:T(8,128)(2,1)S(1)} collective-permute-done((bf16[32,5120]{1,0:T(8,128)(2,1)S(1)}, bf16[32,5120]{1,0:T(8,128)(2,1)S(1)}, u32[]{:S(2)}, u32[]{:S(2)}) %collective-permute-start.1) | collective-permute-done | bytes 327712 | tf_op jit(solution)/shard_map/ppermute | solution.py:25
  28.2 0.0 collective-permute-done.5.refs_8_
  28.3 0.0 copy-start.1
  28.3 3.1 %copy-done.1 = bf16[3,5120,256]{2,1,0:T(8,128)(2,1)} copy-done((bf16[3,5120,256]{2,1,0:T(8,128)(2,1)}, bf16[3,5120,256]{2,1,0:T(8,128)(2,1)S(1)}, u32[]{:S(2)}) %copy-start.1) | copy-done | bytes 7864344
  31.3 3.0 %collective-permute-start.7 = (bf16[32,5120]{1,0:T(8,128)(2,1)S(1)}, bf16[32,5120]{1,0:T(8,128)(2,1)S(1)}, u32[]{:S(2)}, u32[]{:S(2)}) collective-permute-start(bf16[32,5120]{1,0:T(8,128)(2,1)S(1)} %collective-permute-done.1.refs_2_), channel_id=1, source_target_pairs={{0,8},{1,9},{2,10},{3,11},{4,12},{5,13},{6,14},{7,15},{8,0},{9,1},... | collective-permute-start | bytes 983048 | tf_op jit(solution)/shard_map/ppermute | solution.py:25
  34.3 0.0 collective-permute-start.11
  34.3 0.0 collective-permute-done.3.refs_4_
  34.3 0.0 copy-start.2
  34.3 3.2 %copy-done.2 = bf16[3,5120,256]{2,1,0:T(8,128)(2,1)S(1)} copy-done((bf16[3,5120,256]{2,1,0:T(8,128)(2,1)S(1)}, bf16[3,5120,256]{2,1,0:T(8,128)(2,1)}, u32[]{:S(2)}) %copy-start.2) | copy-done | bytes 7864344
  37.5 8.1 %shard_map.92 = (bf16[2,160,256]{2,1,0:T(8,128)(2,1)S(1)}, bf16[4,160,256]{2,1,0:T(8,128)(2,1)S(1)}, bf16[6,5120,256]{2,1,0:T(8,128)(2,1)S(1)}) custom-call(bf16[32,5120]{1,0:T(8,128)(2,1)S(1)} %get-tuple-element.26.refs_0_, bf16[32,5120]{1,0:T(8,128)(2,1)S(1)} %collective-permute-done.refs_1_, bf16[32,5120]{1,0:T(8,128)(2,1)S(1)} %collective-permute-done.1.refs_2_, ...), custom_call_target="tpu_custom_call" | custom-call | flops 100663296000 | bytes 15728640 | tf_op jit(solution)/shard_map/pallas_call | solution.py:138
  45.7 0.6 collective-permute-start.9
  46.3 0.0 collective-permute-done.6.refs_0_
  46.3 0.0 collective-permute-done.8.refs_2_
  46.3 0.0 collective-permute-done.7.refs_1_
  46.3 0.0 copy-start
  46.3 2.8 %shard_map.93 = (bf16[2,96,256]{2,1,0:T(8,128)(2,1)S(1)}, bf16[4,96,256]{2,1,0:T(8,128)(2,1)S(1)}) custom-call(bf16[32,5120]{1,0:T(8,128)(2,1)S(1)} %collective-permute-done.6.refs_0_, bf16[32,5120]{1,0:T(8,128)(2,1)S(1)} %collective-permute-done.7.refs_1_, bf16[32,5120]{1,0:T(8,128)(2,1)S(1)} %collective-permute-done.8.refs_2_, ...), custom_call_target="tpu_custom_call" | custom-call | flops 1509949440 | bytes 15728640 | tf_op jit(solution)/shard_map/pallas_call | solution.py:160
  49.0 0.1 collective-permute-start.10
  49.2 0.0 collective-permute-done.9.far_a
  49.2 1.4 %collective-permute-done.10.far_b = bf16[4,96,256]{2,1,0:T(8,128)(2,1)S(1)} collective-permute-done((bf16[4,96,256]{2,1,0:T(8,128)(2,1)S(1)}, bf16[4,96,256]{2,1,0:T(8,128)(2,1)S(1)}, u32[]{:S(2)}, u32[]{:S(2)}) %collective-permute-start.10) | collective-permute-done | bytes 196640 | tf_op jit(solution)/shard_map/ppermute | solution.py:25
  50.6 0.0 collective-permute-done.11.w_other
  50.6 0.0 copy-done
  50.6 0.0 copy-start.3
  50.6 0.0 copy-start.4
  50.6 3.7 %shard_map.94 = (bf16[32,5120]{1,0:T(8,128)(2,1)S(1)}, bf16[32,5120]{1,0:T(8,128)(2,1)S(1)}, bf16[32,5120]{1,0:T(8,128)(2,1)S(1)}, bf16[32,5120]{1,0:T(8,128)(2,1)S(1)}, bf16[4,512,256]{2,1,0:T(8,128)(2,1)S(1)}) custom-call(bf16[2,160,256]{2,1,0:T(8,128)(2,1)S(1)} %get-tuple-element.29.q_a, bf16[2,96,256]{2,1,0:T(8,128)(2,1)S(1)} %get-tuple-element.32.q_b, ...), custom_call_target="tpu_custom_call" | custom-call | flops 805306368 | bytes 5242880 | tf_op jit(solution)/shard_map/pallas_call | solution.py:241
  54.3 0.6 collective-permute-start.13
  55.0 3.0 %collective-permute-start.15 = (bf16[32,5120]{1,0:T(8,128)(2,1)S(1)}, bf16[32,5120]{1,0:T(8,128)(2,1)S(1)}, u32[]{:S(2)}, u32[]{:S(2)}) collective-permute-start(bf16[32,5120]{1,0:T(8,128)(2,1)S(1)} %get-tuple-element.42), channel_id=1, source_target_pairs={{0,8},{1,9},{2,10},{3,11},{4,12},{5,13},{6,14},{7,15},{8,0},{9,1},... | collective-permute-start | bytes 983048 | tf_op jit(solution)/shard_map/ppermute | solution.py:25
  57.9 0.0 collective-permute-start.17
  57.9 3.5 %collective-permute-start.12 = (bf16[32,5120]{1,0:T(8,128)(2,1)S(1)}, bf16[32,5120]{1,0:T(8,128)(2,1)S(1)}, u32[]{:S(2)}, u32[]{:S(2)}) collective-permute-start(bf16[32,5120]{1,0:T(8,128)(2,1)S(1)} %get-tuple-element.38), channel_id=1, source_target_pairs={{0,4},{1,5},{2,6},{3,7},{4,0},{5,1},{6,2},{7,3},{8,12},{9,13},{10,... | collective-permute-start | bytes 983048 | tf_op jit(solution)/shard_map/ppermute | solution.py:25
  61.5 3.6 %shard_map.95 = (bf16[32,5120]{1,0:T(8,128)(2,1)S(1)}, bf16[32,5120]{1,0:T(8,128)(2,1)S(1)}, bf16[32,5120]{1,0:T(8,128)(2,1)S(1)}, bf16[32,5120]{1,0:T(8,128)(2,1)S(1)}) custom-call(bf16[2,160,256]{2,1,0:T(8,128)(2,1)S(1)} %get-tuple-element.29.q_a, bf16[4,512,256]{2,1,0:T(8,128)(2,1)S(1)} %get-tuple-element.36.kv_ref, bf16[256,5120]{1,0:T(8,128)(2,1)S(1)} %copy-done, ...), custom_call_target="tpu_custom_call" | custom-call | flops 805306368 | bytes 5242880 | tf_op jit(solution)/shard_map/pallas_call | solution.py:241
  65.1 1.4 %collective-permute-done.13 = bf16[32,5120]{1,0:T(8,128)(2,1)S(1)} collective-permute-done((bf16[32,5120]{1,0:T(8,128)(2,1)S(1)}, bf16[32,5120]{1,0:T(8,128)(2,1)S(1)}, u32[]{:S(2)}, u32[]{:S(2)}) %collective-permute-start.13) | collective-permute-done | bytes 327712 | tf_op jit(solution)/shard_map/ppermute | solution.py:25
  66.5 0.1 add_convert_fusion.3
  66.6 3.7 %collective-permute-start.14 = (bf16[32,5120]{1,0:T(8,128)(2,1)S(1)}, bf16[32,5120]{1,0:T(8,128)(2,1)S(1)}, u32[]{:S(2)}, u32[]{:S(2)}) collective-permute-start(bf16[32,5120]{1,0:T(8,128)(2,1)S(1)} %add_convert_fusion.3), channel_id=1, source_target_pairs={{0,6},{1,7},{2,0},{3,1},{4,2},{5,3},{6,4},{7,5},{8,14},{9,15},{10,... | collective-permute-start | bytes 983048 | tf_op jit(solution)/shard_map/ppermute | solution.py:25
  70.3 2.4 %collective-permute-done.15 = bf16[32,5120]{1,0:T(8,128)(2,1)S(1)} collective-permute-done((bf16[32,5120]{1,0:T(8,128)(2,1)S(1)}, bf16[32,5120]{1,0:T(8,128)(2,1)S(1)}, u32[]{:S(2)}, u32[]{:S(2)}) %collective-permute-start.15) | collective-permute-done | bytes 327712 | tf_op jit(solution)/shard_map/ppermute | solution.py:25
  72.7 0.1 add_convert_fusion.2
  72.8 0.1 collective-permute-start.16
  72.8 0.0 collective-permute-done.17
  72.8 0.1 add_convert_fusion.1
  72.9 0.6 collective-permute-start.18
  74.2 1.4 %collective-permute-done.12 = bf16[32,5120]{1,0:T(8,128)(2,1)S(1)} collective-permute-done((bf16[32,5120]{1,0:T(8,128)(2,1)S(1)}, bf16[32,5120]{1,0:T(8,128)(2,1)S(1)}, u32[]{:S(2)}, u32[]{:S(2)}) %collective-permute-start.12) | collective-permute-done | bytes 327712 | tf_op jit(solution)/shard_map/ppermute | solution.py:25
  75.6 8.1 %collective-permute-done.14 = bf16[32,5120]{1,0:T(8,128)(2,1)S(1)} collective-permute-done((bf16[32,5120]{1,0:T(8,128)(2,1)S(1)}, bf16[32,5120]{1,0:T(8,128)(2,1)S(1)}, u32[]{:S(2)}, u32[]{:S(2)}) %collective-permute-start.14) | collective-permute-done | bytes 327712 | tf_op jit(solution)/shard_map/ppermute | solution.py:25
  83.7 0.0 collective-permute-done.16
  83.7 0.0 collective-permute-done.18
  83.7 0.0 copy-done.3
  83.7 0.3 add_convert_fusion
  84.0 3.5 %collective-permute-start.19 = (bf16[8,5120]{1,0:T(8,128)(2,1)S(1)}, bf16[8,5120]{1,0:T(8,128)(2,1)S(1)}, u32[]{:S(2)}, u32[]{:S(2)}) collective-permute-start(bf16[8,5120]{1,0:T(8,128)(2,1)S(1)} %dynamic-slice_bitcast_fusion), channel_id=1, source_target_pairs={{0,16},{16,32},{32,48},{48,64},{64,80},{80,96},{96,112},{1,17},{17... | collective-permute-start | bytes 245768 | tf_op jit(solution)/shard_map/ppermute | solution.py:31
  87.5 4.9 %collective-permute-done.19 = bf16[8,5120]{1,0:T(8,128)(2,1)S(1)} collective-permute-done((bf16[8,5120]{1,0:T(8,128)(2,1)S(1)}, bf16[8,5120]{1,0:T(8,128)(2,1)S(1)}, u32[]{:S(2)}, u32[]{:S(2)}) %collective-permute-start.19) | collective-permute-done | bytes 81952 | tf_op jit(solution)/shard_map/ppermute | solution.py:31
  92.5 0.0 copy-done.4
  92.5 0.8 bitcast_select_fusion
  (3 shorter events, 0.0 us)
Async XLA Ops:
  2.1 1.2 %collective-permute-start.4 = (f32[2,256]{1,0:T(2,128)S(1)}, f32[2,256]{1,0:T(2,128)S(1)}, u32[]{:S(2)}, u32[]{:S(2)}) collective-permute-start(f32[2,256]{1,0:T(2,128)S(1)} %get-tuple-element.27.refs_5_.refs_3_), channel_id=1, source_target_pairs={{0,1},{1,0},{2,3},{3,2},{4,5},{5,4},{6,7},{7,6},{8,9},{9,8},{10,11... | collective-permute-start | bytes 6152 | tf_op jit(solution)/shard_map/ppermute | solution.py:25
  3.3 24.9 %collective-permute-start.5 = (bf16[3,5120,256]{2,1,0:T(8,128)(2,1)}, bf16[3,5120,256]{2,1,0:T(8,128)(2,1)S(1)}, u32[]{:S(2)}, u32[]{:S(2)}) collective-permute-start(bf16[3,5120,256]{2,1,0:T(8,128)(2,1)} %bitcast.21), channel_id=1, source_target_pairs={{0,1},{1,0},{2,3},{3,2},{4,5},{5,4},{6,7},{7,6},{8,9},{9,8},{10,11... | collective-permute-start | bytes 23592968 | tf_op jit(solution)/shard_map/ppermute | solution.py:25
  3.5 11.2 %collective-permute-start = (bf16[32,5120]{1,0:T(8,128)(2,1)S(1)}, bf16[32,5120]{1,0:T(8,128)(2,1)S(1)}, u32[]{:S(2)}, u32[]{:S(2)}) collective-permute-start(bf16[32,5120]{1,0:T(8,128)(2,1)S(1)} %get-tuple-element.26.refs_0_), channel_id=1, source_target_pairs={{0,2},{1,3},{2,4},{3,5},{4,6},{5,7},{6,0},{7,1},{8,10},{9,11},{10,... | collective-permute-start | bytes 983048 | tf_op jit(solution)/shard_map/ppermute | solution.py:25
  5.0 11.2 %collective-permute-start.2 = (bf16[32,5120]{1,0:T(8,128)(2,1)S(1)}, bf16[32,5120]{1,0:T(8,128)(2,1)S(1)}, u32[]{:S(2)}, u32[]{:S(2)}) collective-permute-start(bf16[32,5120]{1,0:T(8,128)(2,1)S(1)} %get-tuple-element.26.refs_0_), channel_id=1, source_target_pairs={{0,8},{1,9},{2,10},{3,11},{4,12},{5,13},{6,14},{7,15},{8,0},{9,1},... | collective-permute-start | bytes 983048 | tf_op jit(solution)/shard_map/ppermute | solution.py:25
  5.5 22.7 %collective-permute-start.1 = (bf16[32,5120]{1,0:T(8,128)(2,1)S(1)}, bf16[32,5120]{1,0:T(8,128)(2,1)S(1)}, u32[]{:S(2)}, u32[]{:S(2)}) collective-permute-start(bf16[32,5120]{1,0:T(8,128)(2,1)S(1)} %get-tuple-element.26.refs_0_), channel_id=1, source_target_pairs={{0,6},{1,7},{2,0},{3,1},{4,2},{5,3},{6,4},{7,5},{8,14},{9,15},{10,... | collective-permute-start | bytes 983048 | tf_op jit(solution)/shard_map/ppermute | solution.py:25
  7.3 27.0 %collective-permute-start.3 = (bf16[32,5120]{1,0:T(8,128)(2,1)S(1)}, bf16[32,5120]{1,0:T(8,128)(2,1)S(1)}, u32[]{:S(2)}, u32[]{:S(2)}) collective-permute-start(bf16[32,5120]{1,0:T(8,128)(2,1)S(1)} %get-tuple-element.26.refs_0_), channel_id=1, source_target_pairs={{0,4},{1,5},{2,6},{3,7},{4,0},{5,1},{6,2},{7,3},{8,12},{9,13},{10,... | collective-permute-start | bytes 983048 | tf_op jit(solution)/shard_map/ppermute | solution.py:25
  14.6 31.6 %collective-permute-start.6 = (bf16[32,5120]{1,0:T(8,128)(2,1)S(1)}, bf16[32,5120]{1,0:T(8,128)(2,1)S(1)}, u32[]{:S(2)}, u32[]{:S(2)}) collective-permute-start(bf16[32,5120]{1,0:T(8,128)(2,1)S(1)} %collective-permute-done.refs_1_), channel_id=1, source_target_pairs={{0,8},{1,9},{2,10},{3,11},{4,12},{5,13},{6,14},{7,15},{8,0},{9,1},... | collective-permute-start | bytes 983048 | tf_op jit(solution)/shard_map/ppermute | solution.py:25
  16.1 30.1 %collective-permute-start.8 = (bf16[32,5120]{1,0:T(8,128)(2,1)S(1)}, bf16[32,5120]{1,0:T(8,128)(2,1)S(1)}, u32[]{:S(2)}, u32[]{:S(2)}) collective-permute-start(bf16[32,5120]{1,0:T(8,128)(2,1)S(1)} %collective-permute-done.2.refs_3_), channel_id=1, source_target_pairs={{0,4},{1,5},{2,6},{3,7},{4,0},{5,1},{6,2},{7,3},{8,12},{9,13},{10,... | collective-permute-start | bytes 983048 | tf_op jit(solution)/shard_map/ppermute | solution.py:25
  28.3 3.1 %copy-start.1 = (bf16[3,5120,256]{2,1,0:T(8,128)(2,1)}, bf16[3,5120,256]{2,1,0:T(8,128)(2,1)S(1)}, u32[]{:S(2)}) copy-start(bf16[3,5120,256]{2,1,0:T(8,128)(2,1)S(1)} %collective-permute-done.5.refs_8_) | copy-start | bytes 23592964
  31.3 14.9 %collective-permute-start.7 = (bf16[32,5120]{1,0:T(8,128)(2,1)S(1)}, bf16[32,5120]{1,0:T(8,128)(2,1)S(1)}, u32[]{:S(2)}, u32[]{:S(2)}) collective-permute-start(bf16[32,5120]{1,0:T(8,128)(2,1)S(1)} %collective-permute-done.1.refs_2_), channel_id=1, source_target_pairs={{0,8},{1,9},{2,10},{3,11},{4,12},{5,13},{6,14},{7,15},{8,0},{9,1},... | collective-permute-start | bytes 983048 | tf_op jit(solution)/shard_map/ppermute | solution.py:25
  34.3 16.3 %collective-permute-start.11 = (bf16[256,5120]{1,0:T(8,128)(2,1)}, bf16[256,5120]{1,0:T(8,128)(2,1)S(1)}, u32[]{:S(2)}, u32[]{:S(2)}) collective-permute-start(bf16[256,5120]{1,0:T(8,128)(2,1)} %w_mine.3), channel_id=1, source_target_pairs={{0,1},{1,0},{2,3},{3,2},{4,5},{5,4},{6,7},{7,6},{8,9},{9,8},{10,11... | collective-permute-start | bytes 7864328 | tf_op jit(solution)/shard_map/ppermute | solution.py:25
  34.3 3.2 %copy-start.2 = (bf16[3,5120,256]{2,1,0:T(8,128)(2,1)S(1)}, bf16[3,5120,256]{2,1,0:T(8,128)(2,1)}, u32[]{:S(2)}) copy-start(bf16[3,5120,256]{2,1,0:T(8,128)(2,1)} %copy-done.1) | copy-start | bytes 23592964
  45.7 3.5 %collective-permute-start.9 = (bf16[4,160,256]{2,1,0:T(8,128)(2,1)S(1)}, bf16[4,160,256]{2,1,0:T(8,128)(2,1)S(1)}, u32[]{:S(2)}, u32[]{:S(2)}) collective-permute-start(bf16[4,160,256]{2,1,0:T(8,128)(2,1)S(1)} %get-tuple-element.33.kv_a), channel_id=1, source_target_pairs={{0,1},{1,0},{2,3},{3,2},{4,5},{5,4},{6,7},{7,6},{8,9},{9,8},{10,11... | collective-permute-start | bytes 983048 | tf_op jit(solution)/shard_map/ppermute | solution.py:25
  46.3 4.3 %copy-start = (bf16[256,5120]{1,0:T(8,128)(2,1)S(1)}, bf16[256,5120]{1,0:T(8,128)(2,1)}, u32[]{:S(2)}) copy-start(bf16[256,5120]{1,0:T(8,128)(2,1)} %w_mine.3) | copy-start | bytes 7864324
  49.0 1.5 %collective-permute-start.10 = (bf16[4,96,256]{2,1,0:T(8,128)(2,1)S(1)}, bf16[4,96,256]{2,1,0:T(8,128)(2,1)S(1)}, u32[]{:S(2)}, u32[]{:S(2)}) collective-permute-start(bf16[4,96,256]{2,1,0:T(8,128)(2,1)S(1)} %get-tuple-element.34.kv_b), channel_id=1, source_target_pairs={{0,1},{1,0},{2,3},{3,2},{4,5},{5,4},{6,7},{7,6},{8,9},{9,8},{10,11... | collective-permute-start | bytes 589832 | tf_op jit(solution)/shard_map/ppermute | solution.py:25
  50.6 33.1 %copy-start.3 = (bf16[1,4,8,5120]{3,2,1,0:T(8,128)(2,1)S(1)}, bf16[1,4,8,5120]{3,2,1,0:T(8,128)(2,1)}, u32[]{:S(2)}) copy-start(bf16[1,4,8,5120]{3,2,1,0:T(8,128)(2,1)} %param.9) | copy-start | bytes 983044
  50.6 41.9 %copy-start.4 = (bf16[8,5120]{1,0:T(8,128)(2,1)S(1)}, bf16[8,5120]{1,0:T(8,128)(2,1)}, u32[]{:S(2)}) copy-start(bf16[8,5120]{1,0:T(8,128)(2,1)} %param.12) | copy-start | bytes 245764
  54.3 12.1 %collective-permute-start.13 = (bf16[32,5120]{1,0:T(8,128)(2,1)S(1)}, bf16[32,5120]{1,0:T(8,128)(2,1)S(1)}, u32[]{:S(2)}, u32[]{:S(2)}) collective-permute-start(bf16[32,5120]{1,0:T(8,128)(2,1)S(1)} %get-tuple-element.40), channel_id=1, source_target_pairs={{0,8},{1,9},{2,10},{3,11},{4,12},{5,13},{6,14},{7,15},{8,0},{9,1},... | collective-permute-start | bytes 983048 | tf_op jit(solution)/shard_map/ppermute | solution.py:25
  55.0 17.7 %collective-permute-start.15 = (bf16[32,5120]{1,0:T(8,128)(2,1)S(1)}, bf16[32,5120]{1,0:T(8,128)(2,1)S(1)}, u32[]{:S(2)}, u32[]{:S(2)}) collective-permute-start(bf16[32,5120]{1,0:T(8,128)(2,1)S(1)} %get-tuple-element.42), channel_id=1, source_target_pairs={{0,8},{1,9},{2,10},{3,11},{4,12},{5,13},{6,14},{7,15},{8,0},{9,1},... | collective-permute-start | bytes 983048 | tf_op jit(solution)/shard_map/ppermute | solution.py:25
  57.9 14.9 %collective-permute-start.17 = (bf16[32,5120]{1,0:T(8,128)(2,1)S(1)}, bf16[32,5120]{1,0:T(8,128)(2,1)S(1)}, u32[]{:S(2)}, u32[]{:S(2)}) collective-permute-start(bf16[32,5120]{1,0:T(8,128)(2,1)S(1)} %get-tuple-element.44), channel_id=1, source_target_pairs={{0,4},{1,5},{2,6},{3,7},{4,0},{5,1},{6,2},{7,3},{8,12},{9,13},{10,... | collective-permute-start | bytes 983048 | tf_op jit(solution)/shard_map/ppermute | solution.py:25
  57.9 17.7 %collective-permute-start.12 = (bf16[32,5120]{1,0:T(8,128)(2,1)S(1)}, bf16[32,5120]{1,0:T(8,128)(2,1)S(1)}, u32[]{:S(2)}, u32[]{:S(2)}) collective-permute-start(bf16[32,5120]{1,0:T(8,128)(2,1)S(1)} %get-tuple-element.38), channel_id=1, source_target_pairs={{0,4},{1,5},{2,6},{3,7},{4,0},{5,1},{6,2},{7,3},{8,12},{9,13},{10,... | collective-permute-start | bytes 983048 | tf_op jit(solution)/shard_map/ppermute | solution.py:25
  66.6 17.1 %collective-permute-start.14 = (bf16[32,5120]{1,0:T(8,128)(2,1)S(1)}, bf16[32,5120]{1,0:T(8,128)(2,1)S(1)}, u32[]{:S(2)}, u32[]{:S(2)}) collective-permute-start(bf16[32,5120]{1,0:T(8,128)(2,1)S(1)} %add_convert_fusion.3), channel_id=1, source_target_pairs={{0,6},{1,7},{2,0},{3,1},{4,2},{5,3},{6,4},{7,5},{8,14},{9,15},{10,... | collective-permute-start | bytes 983048 | tf_op jit(solution)/shard_map/ppermute | solution.py:25
  72.8 10.9 %collective-permute-start.16 = (bf16[32,5120]{1,0:T(8,128)(2,1)S(1)}, bf16[32,5120]{1,0:T(8,128)(2,1)S(1)}, u32[]{:S(2)}, u32[]{:S(2)}) collective-permute-start(bf16[32,5120]{1,0:T(8,128)(2,1)S(1)} %add_convert_fusion.2), channel_id=1, source_target_pairs={{0,2},{1,3},{2,4},{3,5},{4,6},{5,7},{6,0},{7,1},{8,10},{9,11},{10,... | collective-permute-start | bytes 983048 | tf_op jit(solution)/shard_map/ppermute | solution.py:25
  72.9 10.8 %collective-permute-start.18 = (bf16[32,5120]{1,0:T(8,128)(2,1)S(1)}, bf16[32,5120]{1,0:T(8,128)(2,1)S(1)}, u32[]{:S(2)}, u32[]{:S(2)}) collective-permute-start(bf16[32,5120]{1,0:T(8,128)(2,1)S(1)} %add_convert_fusion.1), channel_id=1, source_target_pairs={{0,8},{1,9},{2,10},{3,11},{4,12},{5,13},{6,14},{7,15},{8,0},{9,1},... | collective-permute-start | bytes 983048 | tf_op jit(solution)/shard_map/ppermute | solution.py:25
  84.0 8.4 %collective-permute-start.19 = (bf16[8,5120]{1,0:T(8,128)(2,1)S(1)}, bf16[8,5120]{1,0:T(8,128)(2,1)S(1)}, u32[]{:S(2)}, u32[]{:S(2)}) collective-permute-start(bf16[8,5120]{1,0:T(8,128)(2,1)S(1)} %dynamic-slice_bitcast_fusion), channel_id=1, source_target_pairs={{0,16},{16,32},{32,48},{48,64},{64,80},{80,96},{96,112},{1,17},{17... | collective-permute-start | bytes 245768 | tf_op jit(solution)/shard_map/ppermute | solution.py:31

commit v4 on v3

--- a/solution.py
+++ b/solution.py
@@ -88,9 +88,10 @@
 
 def project(i, rows_ref, weights, gains, q_ref, kv_ref):
     owner, kind = divmod(i, 3)
-    acc = jnp.dot(rows_ref[...], weights[i], preferred_element_type=jnp.float32)
+    acc = jnp.dot(rows_ref[...], weights[owner][kind], preferred_element_type=jnp.float32)
     if kind < 2:
-        acc = head_norm(acc, gains[owner][kind : kind + 1, :])
+        gain = gains[1 + kind][...] if owner else gains[0][kind : kind + 1, :]
+        acc = head_norm(acc, gain)
     if kind == 0:
         q_ref[owner] = acc.astype(jnp.bfloat16)
     else:
@@ -104,24 +105,25 @@
 
 
 def first_kernel(pieces, *refs):
-    xs, gains = refs[:pieces], refs[pieces : pieces + 2]
-    w_mine, w_other, q_ref, kv_ref, held, rows_ref, sems = refs[pieces + 2 :]
+    xs, gains = refs[:pieces], refs[pieces : pieces + 3]
+    w_mine, w_other, q_ref, kv_ref, held, rows_ref, sems = refs[pieces + 3 :]
     copies = []
-    for i in range(6):
-        copies.append(pltpu.make_async_copy((w_mine, w_other)[i // 3].at[i % 3], held.at[i], sems.at[i]))
+    for i in range(3):
+        copies.append(pltpu.make_async_copy(w_mine.at[i], held.at[i], sems.at[i]))
         copies[i].start()
     gather_rows(xs, rows_ref)
-    for i in range(6):
-        copies[i].wait()
-        project(i, rows_ref, held, gains, q_ref, kv_ref)
+    for i in (3, 4, 5, 0, 1, 2):
+        if i < 3:
+            copies[i].wait()
+        project(i, rows_ref, (held, w_other), gains, q_ref, kv_ref)
 
 
 def rest_kernel(pieces, *refs):
-    xs, gains = refs[:pieces], refs[pieces : pieces + 2]
-    held, q_ref, kv_ref, rows_ref = refs[pieces + 2 :]
+    xs, gains = refs[:pieces], refs[pieces : pieces + 3]
+    held, w_other, q_ref, kv_ref, rows_ref = refs[pieces + 3 :]
     gather_rows(xs, rows_ref)
     for i in range(6):
-        project(i, rows_ref, held, gains, q_ref, kv_ref)
+        project(i, rows_ref, (held, w_other), gains, q_ref, kv_ref)
 
 
 def qkv_shapes(total, cols):
@@ -137,10 +139,10 @@
     total, cols = rows * pieces, w_mine.shape[2]
     return pl.pallas_call(
         functools.partial(first_kernel, pieces),
-        in_specs=[VMEM] * (pieces + 2) + [ANY, ANY],
+        in_specs=[VMEM] * (pieces + 3) + [ANY, VMEM],
         out_specs=[VMEM] * 3,
-        out_shape=qkv_shapes(total, cols) + [pltpu.VMEM((6, width, cols), jnp.bfloat16)],
-        scratch_shapes=[pltpu.VMEM((total, width), jnp.bfloat16), pltpu.SemaphoreType.DMA((6,))],
+        out_shape=qkv_shapes(total, cols) + [pltpu.VMEM((3, width, cols), jnp.bfloat16)],
+        scratch_shapes=[pltpu.VMEM((total, width), jnp.bfloat16), pltpu.SemaphoreType.DMA((3,))],
         compiler_params=pltpu.CompilerParams(vmem_limit_bytes=24 * MIB),
         cost_estimate=pl.CostEstimate(
             flops=40 * 12 * total * width * cols, bytes_accessed=12 * width * cols, transcendentals=0
@@ -149,17 +151,17 @@
         *xs,
         *gains,
         pltpu.with_memory_space_constraint(w_mine, pltpu.HBM),
-        w_other,
+        pltpu.with_memory_space_constraint(w_other, pltpu.VMEM),
     )
 
 
-def rest_call(xs, gains, held):
+def rest_call(xs, gains, held, w_other):
     pieces = len(xs)
     rows, width = xs[0].shape
     total, cols = rows * pieces, held.shape[2]
     return pl.pallas_call(
         functools.partial(rest_kernel, pieces),
-        in_specs=[VMEM] * (pieces + 3),
+        in_specs=[VMEM] * (pieces + 5),
         out_specs=[VMEM] * 2,
         out_shape=qkv_shapes(total, cols),
         scratch_shapes=[pltpu.VMEM((total, width), jnp.bfloat16)],
@@ -167,7 +169,12 @@
         cost_estimate=pl.CostEstimate(
             flops=12 * total * width * cols, bytes_accessed=12 * width * cols, transcendentals=0
         ),
-    )(*xs, *gains, pltpu.with_memory_space_constraint(held, pltpu.VMEM))
+    )(
+        *xs,
+        *gains,
+        pltpu.with_memory_space_constraint(held, pltpu.VMEM),
+        pltpu.with_memory_space_constraint(w_other, pltpu.VMEM),
+    )
 
 
 def attend(q_ref, kv_ref, attn_ref):
@@ -264,24 +271,26 @@
     normed, gate, gain = norm_call(steps, own, mod_table, q_gain[None], k_gain[None])
 
     w_mine = w_qkv.transpose(1, 0, 2)
-    gains = [gain, hop(gain, dc=1)]
-    w_send, _ = lax.optimization_barrier((w_mine, gains[1]))
+    q_other, k_other = hop(q_gain[None], dc=1), hop(k_gain[None], dc=1)
+    gains = [gain, q_other, k_other]
+    w_send, _, _, _ = lax.optimization_barrier((w_mine, q_other, k_other, normed))
     w_other = hop(w_send, dc=1)
 
     left = hop(normed, dx=1)
     right = hop(normed, dx=-1)
     far = hop(normed, dz=1)
-    across = hop(normed, dx=2)
+    across_send, _ = lax.optimization_barrier((normed, left))
+    across = hop(across_send, dx=2)
     far_left = hop(left, dz=1)
-    right_send, out_send, _ = lax.optimization_barrier((right, w_out, w_other))
-    far_right = hop(right_send, dz=1)
-    far_across = hop(far, dx=2)
+    far_right = hop(right, dz=1)
+    far_send, out_send, _ = lax.optimization_barrier((far, w_out, w_other))
+    far_across = hop(far_send, dx=2)
 
     out_other = hop(out_send, dc=1)
 
     q_a, kv_a, held = first_call([normed, left, right, far, across], gains, w_mine, w_other)
     far_a = hop(kv_a, dc=1)
-    q_b, kv_b = rest_call([far_left, far_right, far_across], gains, held)
+    q_b, kv_b = rest_call([far_left, far_right, far_across], gains, held, w_other)
     far_b = hop(kv_b, dc=1)
     keys = (4, 16 * rows, kv_a.shape[2])
     operands = (q_a, q_b, kv_a, kv_b, far_a, far_b)
@@ -293,10 +302,12 @@
     def add(a, b):
         return (a.astype(jnp.float32) + b.astype(jnp.float32)).astype(jnp.bfloat16)
 
+    from_across = hop(p_far_across, dx=2)
+    across_send, _ = lax.optimization_barrier((p_across, from_across))
     s_left = add(p_left, hop(p_far_left, dz=1))
     s_right = add(p_right, hop(p_far_right, dz=1))
-    s_far = add(p_far, hop(p_far_across, dx=2))
-    arrived = [hop(p_across, dx=2), hop(s_left, dx=-1), hop(s_right, dx=1), hop(s_far, dz=1)]
+    s_far = add(p_far, from_across)
+    arrived = [hop(across_send, dx=2), hop(s_left, dx=-1), hop(s_right, dx=1), hop(s_far, dz=1)]
     proj = p_own.astype(jnp.float32)
     for piece in arrived:
         proj = proj + piece.astype(jnp.float32)

time: 95 us -> 81.5 us (0.86); the launches traced: 93.3 us -> 81.2 us
  local copies, waits for them, and re-layouts: 6.32 us -> 0.03 us
  starting transfers between devices: 27.9 us -> 24.8 us
  Pallas kernels: 19.7 us -> 17.3 us
    unnamed x10 -> x6, local copies, waits for them, and re-layouts: 6.3 us -> 0.01 us
    ppermute x19 -> x20, starting transfers between devices: 24.4 us -> 21.4 us  [hop(): return lax.ppermute(value, 'seq', pairs)]
    pallas_call x1, Pallas kernels: 8.13 us -> 5.79 us  [first_call(): pl.pallas_call(functools.partial(first_kernel, pieces), in_specs=[VMEM] *...]
    ppermute x19 -> x20, waiting for transfers between devices: 31.7 us -> 31.3 us  [hop(): return lax.ppermute(value, 'seq', pairs)]
  transfers between devices with their start and end apart: 20 -> 21, of which waited for: 10 -> 12; matrix products, arithmetic and copies ran while one was open for 0% -> 0% of each run, Pallas kernels for 16% -> 17%
where the time goes in v4:
time: 81.5 us; the launch traced here: 81.2 us
  waiting for transfers between devices  36.3 us (45%)
  starting transfers between devices  24.8 us (30%)
  Pallas kernels  17.3 us (21%)
  between operations  1.48 us (2%)
  other arithmetic  1.34 us (2%)
    ppermute x20, waiting for transfers between devices, hop(): return lax.ppermute(value, 'seq', pairs)  31.3 us
    ppermute x20, starting transfers between devices, hop(): return lax.ppermute(value, 'seq', pairs)  21.4 us
    pallas_call x2, Pallas kernels, attend_call(): pl.pallas_call(functools.partial(kernel, pieces), grid=(width // block,),...  7.38 us
    pallas_call x1, Pallas kernels, first_call(): pl.pallas_call(functools.partial(first_kernel, pieces), in_specs=[VMEM] *...  5.79 us
    ppermute x1, waiting for transfers between devices, from_behind(): return lax.ppermute(x, axis, pairs)  4.98 us
    ppermute x1, starting transfers between devices, from_behind(): return lax.ppermute(x, axis, pairs)  3.44 us
    pallas_call x1, Pallas kernels, rest_call(): pl.pallas_call(functools.partial(rest_kernel, pieces), in_specs=[VMEM] *...  2.71 us
  transfers between devices with their start and end apart: 21, of which 12 were waited for; matrix products, arithmetic and copies ran while one was open for 0% of the time, Pallas kernels for 17%

profile of v4, /device:TPU:96, one launch (start us, length us, event | category | flops | bytes accessed | tf_op | source)
XLA Modules:
  0.0 81.2 jit_solution(17618615347903391217)
XLA Ops:
  0.0 0.0 collective-permute-start.4
  0.0 0.5 collective-permute-start.5
  1.2 1.4 %shard_map.91 = (bf16[32,5120]{1,0:T(8,128)(2,1)S(1)}, f32[1,5120]{1,0:T(1,128)S(1)}, f32[2,256]{1,0:T(2,128)S(1)}) custom-call(s32[1]{0:T(128)S(6)} %copy.10.step, bf16[32,5120]{1,0:T(8,128)(2,1)} %bitcast.18, f32[50,15360]{1,0:T(8,128)} %table.1, f32[1,256]{1,0:T(1,128)} %bitcast.20, f32[1,256]{1,0:T(1,128)} %bitcast.22), custom_call_target="tpu_custom_call" | custom-call | flops 1638400 | bytes 655360 | tf_op jit(solution)/shard_map/pallas_call | solution.py:59
  2.6 0.0 collective-permute-done.4.refs_6_.refs_4_
  2.6 0.0 collective-permute-done.5.refs_7_.refs_5_
  2.6 0.1 collective-permute-start.6
  2.7 1.6 %collective-permute-start = (bf16[32,5120]{1,0:T(8,128)(2,1)S(1)}, bf16[32,5120]{1,0:T(8,128)(2,1)S(1)}, u32[]{:S(2)}, u32[]{:S(2)}) collective-permute-start(bf16[32,5120]{1,0:T(8,128)(2,1)S(1)} %get-tuple-element.29.refs_0_), channel_id=1, source_target_pairs={{0,2},{1,3},{2,4},{3,5},{4,6},{5,7},{6,0},{7,1},{8,10},{9,11},{10,... | collective-permute-start | bytes 983048 | tf_op jit(solution)/shard_map/ppermute | solution.py:25
  4.3 1.7 %collective-permute-start.1 = (bf16[32,5120]{1,0:T(8,128)(2,1)S(1)}, bf16[32,5120]{1,0:T(8,128)(2,1)S(1)}, u32[]{:S(2)}, u32[]{:S(2)}) collective-permute-start(bf16[32,5120]{1,0:T(8,128)(2,1)S(1)} %get-tuple-element.29.refs_0_), channel_id=1, source_target_pairs={{0,6},{1,7},{2,0},{3,1},{4,2},{5,3},{6,4},{7,5},{8,14},{9,15},{10,... | collective-permute-start | bytes 983048 | tf_op jit(solution)/shard_map/ppermute | solution.py:25
  6.0 0.6 collective-permute-start.2
  6.6 7.5 %collective-permute-done.refs_1_ = bf16[32,5120]{1,0:T(8,128)(2,1)S(1)} collective-permute-done((bf16[32,5120]{1,0:T(8,128)(2,1)S(1)}, bf16[32,5120]{1,0:T(8,128)(2,1)S(1)}, u32[]{:S(2)}, u32[]{:S(2)}) %collective-permute-start) | collective-permute-done | bytes 327712 | tf_op jit(solution)/shard_map/ppermute | solution.py:25
  14.0 1.8 %collective-permute-start.3 = (bf16[32,5120]{1,0:T(8,128)(2,1)S(1)}, bf16[32,5120]{1,0:T(8,128)(2,1)S(1)}, u32[]{:S(2)}, u32[]{:S(2)}) collective-permute-start(bf16[32,5120]{1,0:T(8,128)(2,1)S(1)} %get-tuple-element.29.refs_0_), channel_id=1, source_target_pairs={{0,4},{1,5},{2,6},{3,7},{4,0},{5,1},{6,2},{7,3},{8,12},{9,13},{10,... | collective-permute-start | bytes 983048 | tf_op jit(solution)/shard_map/ppermute | solution.py:25
  15.8 0.6 collective-permute-start.7
  16.4 0.0 collective-permute-done.1.refs_2_
  16.4 3.0 %collective-permute-start.8 = (bf16[32,5120]{1,0:T(8,128)(2,1)S(1)}, bf16[32,5120]{1,0:T(8,128)(2,1)S(1)}, u32[]{:S(2)}, u32[]{:S(2)}) collective-permute-start(bf16[32,5120]{1,0:T(8,128)(2,1)S(1)} %collective-permute-done.1.refs_2_), channel_id=1, source_target_pairs={{0,8},{1,9},{2,10},{3,11},{4,12},{5,13},{6,14},{7,15},{8,0},{9,1},... | collective-permute-start | bytes 983048 | tf_op jit(solution)/shard_map/ppermute | solution.py:25
  19.4 0.0 collective-permute-done.2.refs_3_
  19.4 0.0 collective-permute-done.6.refs_9_.refs_7_
  19.4 1.7 %collective-permute-start.9 = (bf16[32,5120]{1,0:T(8,128)(2,1)S(1)}, bf16[32,5120]{1,0:T(8,128)(2,1)S(1)}, u32[]{:S(2)}, u32[]{:S(2)}) collective-permute-start(bf16[32,5120]{1,0:T(8,128)(2,1)S(1)} %collective-permute-done.2.refs_3_), channel_id=1, source_target_pairs={{0,4},{1,5},{2,6},{3,7},{4,0},{5,1},{6,2},{7,3},{8,12},{9,13},{10,... | collective-permute-start | bytes 983048 | tf_op jit(solution)/shard_map/ppermute | solution.py:25
  21.1 0.0 collective-permute-start.12
  21.1 5.1 %collective-permute-done.3.refs_4_ = bf16[32,5120]{1,0:T(8,128)(2,1)S(1)} collective-permute-done((bf16[32,5120]{1,0:T(8,128)(2,1)S(1)}, bf16[32,5120]{1,0:T(8,128)(2,1)S(1)}, u32[]{:S(2)}, u32[]{:S(2)}) %collective-permute-start.3) | collective-permute-done | bytes 327712 | tf_op jit(solution)/shard_map/ppermute | solution.py:25
  26.2 5.8 %shard_map.92 = (bf16[2,160,256]{2,1,0:T(8,128)(2,1)S(1)}, bf16[4,160,256]{2,1,0:T(8,128)(2,1)S(1)}, bf16[3,5120,256]{2,1,0:T(8,128)(2,1)S(1)}) custom-call(bf16[32,5120]{1,0:T(8,128)(2,1)S(1)} %get-tuple-element.29.refs_0_, bf16[32,5120]{1,0:T(8,128)(2,1)S(1)} %collective-permute-done.refs_1_, bf16[32,5120]{1,0:T(8,128)(2,1)S(1)} %collective-permute-done.1.refs_2_, ...), custom_call_target="tpu_custom_call" | custom-call | flops 100663296000 | bytes 15728640 | tf_op jit(solution)/shard_map/pallas_call | solution.py:140
  32.0 0.1 collective-permute-start.10
  32.1 0.0 collective-permute-done.7.refs_0_
  32.1 1.3 %collective-permute-done.8.refs_1_ = bf16[32,5120]{1,0:T(8,128)(2,1)S(1)} collective-permute-done((bf16[32,5120]{1,0:T(8,128)(2,1)S(1)}, bf16[32,5120]{1,0:T(8,128)(2,1)S(1)}, u32[]{:S(2)}, u32[]{:S(2)}) %collective-permute-start.8) | collective-permute-done | bytes 327712 | tf_op jit(solution)/shard_map/ppermute | solution.py:25
  33.4 0.0 collective-permute-done.9.refs_2_
  33.4 0.0 copy-start
  33.4 2.7 %shard_map.93 = (bf16[2,96,256]{2,1,0:T(8,128)(2,1)S(1)}, bf16[4,96,256]{2,1,0:T(8,128)(2,1)S(1)}) custom-call(bf16[32,5120]{1,0:T(8,128)(2,1)S(1)} %collective-permute-done.7.refs_0_, bf16[32,5120]{1,0:T(8,128)(2,1)S(1)} %collective-permute-done.8.refs_1_, bf16[32,5120]{1,0:T(8,128)(2,1)S(1)} %collective-permute-done.9.refs_2_, ...), custom_call_target="tpu_custom_call" | custom-call | flops 1509949440 | bytes 15728640 | tf_op jit(solution)/shard_map/pallas_call | solution.py:162
  36.1 0.1 collective-permute-start.11
  36.2 0.0 collective-permute-done.10.far_a
  36.2 1.4 %collective-permute-done.11.far_b = bf16[4,96,256]{2,1,0:T(8,128)(2,1)S(1)} collective-permute-done((bf16[4,96,256]{2,1,0:T(8,128)(2,1)S(1)}, bf16[4,96,256]{2,1,0:T(8,128)(2,1)S(1)}, u32[]{:S(2)}, u32[]{:S(2)}) %collective-permute-start.11) | collective-permute-done | bytes 196640 | tf_op jit(solution)/shard_map/ppermute | solution.py:25
  37.6 0.0 collective-permute-done.12.w_other
  37.6 0.0 copy-done
  37.6 0.0 copy-start.1
  37.6 0.0 copy-start.2
  37.6 3.7 %shard_map.94 = (bf16[32,5120]{1,0:T(8,128)(2,1)S(1)}, bf16[32,5120]{1,0:T(8,128)(2,1)S(1)}, bf16[32,5120]{1,0:T(8,128)(2,1)S(1)}, bf16[32,5120]{1,0:T(8,128)(2,1)S(1)}, bf16[4,512,256]{2,1,0:T(8,128)(2,1)S(1)}) custom-call(bf16[2,160,256]{2,1,0:T(8,128)(2,1)S(1)} %get-tuple-element.32.q_a, bf16[2,96,256]{2,1,0:T(8,128)(2,1)S(1)} %get-tuple-element.35.q_b, ...), custom_call_target="tpu_custom_call" | custom-call | flops 805306368 | bytes 5242880 | tf_op jit(solution)/shard_map/pallas_call | solution.py:248
  41.4 1.8 %collective-permute-start.13 = (bf16[32,5120]{1,0:T(8,128)(2,1)S(1)}, bf16[32,5120]{1,0:T(8,128)(2,1)S(1)}, u32[]{:S(2)}, u32[]{:S(2)}) collective-permute-start(bf16[32,5120]{1,0:T(8,128)(2,1)S(1)} %get-tuple-element.42), channel_id=1, source_target_pairs={{0,4},{1,5},{2,6},{3,7},{4,0},{5,1},{6,2},{7,3},{8,12},{9,13},{10,... | collective-permute-start | bytes 983048 | tf_op jit(solution)/shard_map/ppermute | solution.py:25
  43.1 0.6 collective-permute-start.15
  43.7 3.0 %collective-permute-start.17 = (bf16[32,5120]{1,0:T(8,128)(2,1)S(1)}, bf16[32,5120]{1,0:T(8,128)(2,1)S(1)}, u32[]{:S(2)}, u32[]{:S(2)}) collective-permute-start(bf16[32,5120]{1,0:T(8,128)(2,1)S(1)} %get-tuple-element.47), channel_id=1, source_target_pairs={{0,8},{1,9},{2,10},{3,11},{4,12},{5,13},{6,14},{7,15},{8,0},{9,1},... | collective-permute-start | bytes 983048 | tf_op jit(solution)/shard_map/ppermute | solution.py:25
  46.7 3.7 %shard_map.95 = (bf16[32,5120]{1,0:T(8,128)(2,1)S(1)}, bf16[32,5120]{1,0:T(8,128)(2,1)S(1)}, bf16[32,5120]{1,0:T(8,128)(2,1)S(1)}, bf16[32,5120]{1,0:T(8,128)(2,1)S(1)}) custom-call(bf16[2,160,256]{2,1,0:T(8,128)(2,1)S(1)} %get-tuple-element.32.q_a, bf16[4,512,256]{2,1,0:T(8,128)(2,1)S(1)} %get-tuple-element.39.kv_ref, bf16[256,5120]{1,0:T(8,128)(2,1)S(1)} %copy-done, ...), custom_call_target="tpu_custom_call" | custom-call | flops 805306368 | bytes 5242880 | tf_op jit(solution)/shard_map/pallas_call | solution.py:248
  50.3 2.3 %collective-permute-done.13 = bf16[32,5120]{1,0:T(8,128)(2,1)S(1)} collective-permute-done((bf16[32,5120]{1,0:T(8,128)(2,1)S(1)}, bf16[32,5120]{1,0:T(8,128)(2,1)S(1)}, u32[]{:S(2)}, u32[]{:S(2)}) %collective-permute-start.13) | collective-permute-done | bytes 327712 | tf_op jit(solution)/shard_map/ppermute | solution.py:25
  52.7 1.7 %collective-permute-start.14 = (bf16[32,5120]{1,0:T(8,128)(2,1)S(1)}, bf16[32,5120]{1,0:T(8,128)(2,1)S(1)}, u32[]{:S(2)}, u32[]{:S(2)}) collective-permute-start(bf16[32,5120]{1,0:T(8,128)(2,1)S(1)} %get-tuple-element.43), channel_id=1, source_target_pairs={{0,4},{1,5},{2,6},{3,7},{4,0},{5,1},{6,2},{7,3},{8,12},{9,13},{10,... | collective-permute-start | bytes 983048 | tf_op jit(solution)/shard_map/ppermute | solution.py:25
  54.4 0.8 %collective-permute-done.15 = bf16[32,5120]{1,0:T(8,128)(2,1)S(1)} collective-permute-done((bf16[32,5120]{1,0:T(8,128)(2,1)S(1)}, bf16[32,5120]{1,0:T(8,128)(2,1)S(1)}, u32[]{:S(2)}, u32[]{:S(2)}) %collective-permute-start.15) | collective-permute-done | bytes 327712 | tf_op jit(solution)/shard_map/ppermute | solution.py:25
  55.2 0.1 add_convert_fusion.3
  55.3 1.6 %collective-permute-start.16 = (bf16[32,5120]{1,0:T(8,128)(2,1)S(1)}, bf16[32,5120]{1,0:T(8,128)(2,1)S(1)}, u32[]{:S(2)}, u32[]{:S(2)}) collective-permute-start(bf16[32,5120]{1,0:T(8,128)(2,1)S(1)} %add_convert_fusion.3), channel_id=1, source_target_pairs={{0,6},{1,7},{2,0},{3,1},{4,2},{5,3},{6,4},{7,5},{8,14},{9,15},{10,... | collective-permute-start | bytes 983048 | tf_op jit(solution)/shard_map/ppermute | solution.py:25
  57.0 4.2 %collective-permute-done.17 = bf16[32,5120]{1,0:T(8,128)(2,1)S(1)} collective-permute-done((bf16[32,5120]{1,0:T(8,128)(2,1)S(1)}, bf16[32,5120]{1,0:T(8,128)(2,1)S(1)}, u32[]{:S(2)}, u32[]{:S(2)}) %collective-permute-start.17) | collective-permute-done | bytes 327712 | tf_op jit(solution)/shard_map/ppermute | solution.py:25
  61.2 0.1 add_convert_fusion.2
  61.2 0.3 collective-permute-start.18
  61.6 0.1 add_convert_fusion.1
  61.7 0.7 collective-permute-start.19
  63.0 0.1 collective-permute-done.14
  63.1 5.5 %collective-permute-done.16 = bf16[32,5120]{1,0:T(8,128)(2,1)S(1)} collective-permute-done((bf16[32,5120]{1,0:T(8,128)(2,1)S(1)}, bf16[32,5120]{1,0:T(8,128)(2,1)S(1)}, u32[]{:S(2)}, u32[]{:S(2)}) %collective-permute-start.16) | collective-permute-done | bytes 327712 | tf_op jit(solution)/shard_map/ppermute | solution.py:25
  68.6 2.5 %collective-permute-done.18 = bf16[32,5120]{1,0:T(8,128)(2,1)S(1)} collective-permute-done((bf16[32,5120]{1,0:T(8,128)(2,1)S(1)}, bf16[32,5120]{1,0:T(8,128)(2,1)S(1)}, u32[]{:S(2)}, u32[]{:S(2)}) %collective-permute-start.18) | collective-permute-done | bytes 327712 | tf_op jit(solution)/shard_map/ppermute | solution.py:25
  71.1 0.5 collective-permute-done.19
  71.6 0.0 copy-done.1
  71.6 0.3 add_convert_fusion
  71.9 3.4 %collective-permute-start.20 = (bf16[8,5120]{1,0:T(8,128)(2,1)S(1)}, bf16[8,5120]{1,0:T(8,128)(2,1)S(1)}, u32[]{:S(2)}, u32[]{:S(2)}) collective-permute-start(bf16[8,5120]{1,0:T(8,128)(2,1)S(1)} %dynamic-slice_bitcast_fusion), channel_id=1, source_target_pairs={{0,16},{16,32},{32,48},{48,64},{64,80},{80,96},{96,112},{1,17},{17... | collective-permute-start | bytes 245768 | tf_op jit(solution)/shard_map/ppermute | solution.py:31
  75.4 5.0 %collective-permute-done.20 = bf16[8,5120]{1,0:T(8,128)(2,1)S(1)} collective-permute-done((bf16[8,5120]{1,0:T(8,128)(2,1)S(1)}, bf16[8,5120]{1,0:T(8,128)(2,1)S(1)}, u32[]{:S(2)}, u32[]{:S(2)}) %collective-permute-start.20) | collective-permute-done | bytes 81952 | tf_op jit(solution)/shard_map/ppermute | solution.py:31
  80.4 0.0 copy-done.2
  80.4 0.8 %bitcast_select_fusion = bf16[1,4,8,5120]{3,2,1,0:T(8,128)(2,1)} fusion(bf16[32,5120]{1,0:T(8,128)(2,1)S(1)} %add_convert_fusion, pred[4]{0:T(512)(128)(4,1)S(1)} %iota_compare_fusion, bf16[8,5120]{1,0:T(8,128)(2,1)S(1)} %broadcast_select_fusion), kind=kLoop, calls=%fused_computation.4 | loop fusion | flops 163840 | bytes 737284 | tf_op jit(solution)/shard_map/jit(_where)/select_n | solution.py:320
  (3 shorter events, 0.0 us)
Async XLA Ops:
  0.0 2.6 %collective-permute-start.4 = (f32[1,256]{1,0:T(1,128)}, f32[1,256]{1,0:T(1,128)S(1)}, u32[]{:S(2)}, u32[]{:S(2)}) collective-permute-start(f32[1,256]{1,0:T(1,128)} %bitcast.19), channel_id=1, source_target_pairs={{0,1},{1,0},{2,3},{3,2},{4,5},{5,4},{6,7},{7,6},{8,9},{9,8},{10,11... | collective-permute-start | bytes 3080 | tf_op jit(solution)/shard_map/ppermute | solution.py:25
  0.0 2.6 %collective-permute-start.5 = (f32[1,256]{1,0:T(1,128)}, f32[1,256]{1,0:T(1,128)S(1)}, u32[]{:S(2)}, u32[]{:S(2)}) collective-permute-start(f32[1,256]{1,0:T(1,128)} %bitcast.21), channel_id=1, source_target_pairs={{0,1},{1,0},{2,3},{3,2},{4,5},{5,4},{6,7},{7,6},{8,9},{9,8},{10,11... | collective-permute-start | bytes 3080 | tf_op jit(solution)/shard_map/ppermute | solution.py:25
  2.6 16.8 %collective-permute-start.6 = (bf16[3,5120,256]{2,1,0:T(8,128)(2,1)}, bf16[3,5120,256]{2,1,0:T(8,128)(2,1)S(1)}, u32[]{:S(2)}, u32[]{:S(2)}) collective-permute-start(bf16[3,5120,256]{2,1,0:T(8,128)(2,1)} %bitcast.23), channel_id=1, source_target_pairs={{0,1},{1,0},{2,3},{3,2},{4,5},{5,4},{6,7},{7,6},{8,9},{9,8},{10,11... | collective-permute-start | bytes 23592968 | tf_op jit(solution)/shard_map/ppermute | solution.py:25
  2.7 11.3 %collective-permute-start = (bf16[32,5120]{1,0:T(8,128)(2,1)S(1)}, bf16[32,5120]{1,0:T(8,128)(2,1)S(1)}, u32[]{:S(2)}, u32[]{:S(2)}) collective-permute-start(bf16[32,5120]{1,0:T(8,128)(2,1)S(1)} %get-tuple-element.29.refs_0_), channel_id=1, source_target_pairs={{0,2},{1,3},{2,4},{3,5},{4,6},{5,7},{6,0},{7,1},{8,10},{9,11},{10,... | collective-permute-start | bytes 983048 | tf_op jit(solution)/shard_map/ppermute | solution.py:25
  4.3 12.1 %collective-permute-start.1 = (bf16[32,5120]{1,0:T(8,128)(2,1)S(1)}, bf16[32,5120]{1,0:T(8,128)(2,1)S(1)}, u32[]{:S(2)}, u32[]{:S(2)}) collective-permute-start(bf16[32,5120]{1,0:T(8,128)(2,1)S(1)} %get-tuple-element.29.refs_0_), channel_id=1, source_target_pairs={{0,6},{1,7},{2,0},{3,1},{4,2},{5,3},{6,4},{7,5},{8,14},{9,15},{10,... | collective-permute-start | bytes 983048 | tf_op jit(solution)/shard_map/ppermute | solution.py:25
  6.0 13.4 %collective-permute-start.2 = (bf16[32,5120]{1,0:T(8,128)(2,1)S(1)}, bf16[32,5120]{1,0:T(8,128)(2,1)S(1)}, u32[]{:S(2)}, u32[]{:S(2)}) collective-permute-start(bf16[32,5120]{1,0:T(8,128)(2,1)S(1)} %get-tuple-element.29.refs_0_), channel_id=1, source_target_pairs={{0,8},{1,9},{2,10},{3,11},{4,12},{5,13},{6,14},{7,15},{8,0},{9,1},... | collective-permute-start | bytes 983048 | tf_op jit(solution)/shard_map/ppermute | solution.py:25
  14.0 12.1 %collective-permute-start.3 = (bf16[32,5120]{1,0:T(8,128)(2,1)S(1)}, bf16[32,5120]{1,0:T(8,128)(2,1)S(1)}, u32[]{:S(2)}, u32[]{:S(2)}) collective-permute-start(bf16[32,5120]{1,0:T(8,128)(2,1)S(1)} %get-tuple-element.29.refs_0_), channel_id=1, source_target_pairs={{0,4},{1,5},{2,6},{3,7},{4,0},{5,1},{6,2},{7,3},{8,12},{9,13},{10,... | collective-permute-start | bytes 983048 | tf_op jit(solution)/shard_map/ppermute | solution.py:25
  15.8 16.2 %collective-permute-start.7 = (bf16[32,5120]{1,0:T(8,128)(2,1)S(1)}, bf16[32,5120]{1,0:T(8,128)(2,1)S(1)}, u32[]{:S(2)}, u32[]{:S(2)}) collective-permute-start(bf16[32,5120]{1,0:T(8,128)(2,1)S(1)} %collective-permute-done.refs_1_), channel_id=1, source_target_pairs={{0,8},{1,9},{2,10},{3,11},{4,12},{5,13},{6,14},{7,15},{8,0},{9,1},... | collective-permute-start | bytes 983048 | tf_op jit(solution)/shard_map/ppermute | solution.py:25
  16.4 17.0 %collective-permute-start.8 = (bf16[32,5120]{1,0:T(8,128)(2,1)S(1)}, bf16[32,5120]{1,0:T(8,128)(2,1)S(1)}, u32[]{:S(2)}, u32[]{:S(2)}) collective-permute-start(bf16[32,5120]{1,0:T(8,128)(2,1)S(1)} %collective-permute-done.1.refs_2_), channel_id=1, source_target_pairs={{0,8},{1,9},{2,10},{3,11},{4,12},{5,13},{6,14},{7,15},{8,0},{9,1},... | collective-permute-start | bytes 983048 | tf_op jit(solution)/shard_map/ppermute | solution.py:25
  19.4 14.0 %collective-permute-start.9 = (bf16[32,5120]{1,0:T(8,128)(2,1)S(1)}, bf16[32,5120]{1,0:T(8,128)(2,1)S(1)}, u32[]{:S(2)}, u32[]{:S(2)}) collective-permute-start(bf16[32,5120]{1,0:T(8,128)(2,1)S(1)} %collective-permute-done.2.refs_3_), channel_id=1, source_target_pairs={{0,4},{1,5},{2,6},{3,7},{4,0},{5,1},{6,2},{7,3},{8,12},{9,13},{10,... | collective-permute-start | bytes 983048 | tf_op jit(solution)/shard_map/ppermute | solution.py:25
  21.1 16.5 %collective-permute-start.12 = (bf16[256,5120]{1,0:T(8,128)(2,1)}, bf16[256,5120]{1,0:T(8,128)(2,1)S(1)}, u32[]{:S(2)}, u32[]{:S(2)}) collective-permute-start(bf16[256,5120]{1,0:T(8,128)(2,1)} %w_mine.3), channel_id=1, source_target_pairs={{0,1},{1,0},{2,3},{3,2},{4,5},{5,4},{6,7},{7,6},{8,9},{9,8},{10,11... | collective-permute-start | bytes 7864328 | tf_op jit(solution)/shard_map/ppermute | solution.py:25
  32.0 4.2 %collective-permute-start.10 = (bf16[4,160,256]{2,1,0:T(8,128)(2,1)S(1)}, bf16[4,160,256]{2,1,0:T(8,128)(2,1)S(1)}, u32[]{:S(2)}, u32[]{:S(2)}) collective-permute-start(bf16[4,160,256]{2,1,0:T(8,128)(2,1)S(1)} %get-tuple-element.36.kv_a), channel_id=1, source_target_pairs={{0,1},{1,0},{2,3},{3,2},{4,5},{5,4},{6,7},{7,6},{8,9},{9,8},{10,11... | collective-permute-start | bytes 983048 | tf_op jit(solution)/shard_map/ppermute | solution.py:25
  33.4 4.2 %copy-start = (bf16[256,5120]{1,0:T(8,128)(2,1)S(1)}, bf16[256,5120]{1,0:T(8,128)(2,1)}, u32[]{:S(2)}) copy-start(bf16[256,5120]{1,0:T(8,128)(2,1)} %w_mine.3) | copy-start | bytes 7864324
  36.1 1.5 %collective-permute-start.11 = (bf16[4,96,256]{2,1,0:T(8,128)(2,1)S(1)}, bf16[4,96,256]{2,1,0:T(8,128)(2,1)S(1)}, u32[]{:S(2)}, u32[]{:S(2)}) collective-permute-start(bf16[4,96,256]{2,1,0:T(8,128)(2,1)S(1)} %get-tuple-element.37.kv_b), channel_id=1, source_target_pairs={{0,1},{1,0},{2,3},{3,2},{4,5},{5,4},{6,7},{7,6},{8,9},{9,8},{10,11... | collective-permute-start | bytes 589832 | tf_op jit(solution)/shard_map/ppermute | solution.py:25
  37.6 34.0 %copy-start.1 = (bf16[1,4,8,5120]{3,2,1,0:T(8,128)(2,1)S(1)}, bf16[1,4,8,5120]{3,2,1,0:T(8,128)(2,1)}, u32[]{:S(2)}) copy-start(bf16[1,4,8,5120]{3,2,1,0:T(8,128)(2,1)} %param.9) | copy-start | bytes 983044
  37.6 42.8 %copy-start.2 = (bf16[8,5120]{1,0:T(8,128)(2,1)S(1)}, bf16[8,5120]{1,0:T(8,128)(2,1)}, u32[]{:S(2)}) copy-start(bf16[8,5120]{1,0:T(8,128)(2,1)} %param.12) | copy-start | bytes 245764
  41.4 11.3 %collective-permute-start.13 = (bf16[32,5120]{1,0:T(8,128)(2,1)S(1)}, bf16[32,5120]{1,0:T(8,128)(2,1)S(1)}, u32[]{:S(2)}, u32[]{:S(2)}) collective-permute-start(bf16[32,5120]{1,0:T(8,128)(2,1)S(1)} %get-tuple-element.42), channel_id=1, source_target_pairs={{0,4},{1,5},{2,6},{3,7},{4,0},{5,1},{6,2},{7,3},{8,12},{9,13},{10,... | collective-permute-start | bytes 983048 | tf_op jit(solution)/shard_map/ppermute | solution.py:25
  43.1 12.1 %collective-permute-start.15 = (bf16[32,5120]{1,0:T(8,128)(2,1)S(1)}, bf16[32,5120]{1,0:T(8,128)(2,1)S(1)}, u32[]{:S(2)}, u32[]{:S(2)}) collective-permute-start(bf16[32,5120]{1,0:T(8,128)(2,1)S(1)} %get-tuple-element.45), channel_id=1, source_target_pairs={{0,8},{1,9},{2,10},{3,11},{4,12},{5,13},{6,14},{7,15},{8,0},{9,1},... | collective-permute-start | bytes 983048 | tf_op jit(solution)/shard_map/ppermute | solution.py:25
  43.7 17.5 %collective-permute-start.17 = (bf16[32,5120]{1,0:T(8,128)(2,1)S(1)}, bf16[32,5120]{1,0:T(8,128)(2,1)S(1)}, u32[]{:S(2)}, u32[]{:S(2)}) collective-permute-start(bf16[32,5120]{1,0:T(8,128)(2,1)S(1)} %get-tuple-element.47), channel_id=1, source_target_pairs={{0,8},{1,9},{2,10},{3,11},{4,12},{5,13},{6,14},{7,15},{8,0},{9,1},... | collective-permute-start | bytes 983048 | tf_op jit(solution)/shard_map/ppermute | solution.py:25
  52.7 10.4 %collective-permute-start.14 = (bf16[32,5120]{1,0:T(8,128)(2,1)S(1)}, bf16[32,5120]{1,0:T(8,128)(2,1)S(1)}, u32[]{:S(2)}, u32[]{:S(2)}) collective-permute-start(bf16[32,5120]{1,0:T(8,128)(2,1)S(1)} %get-tuple-element.43), channel_id=1, source_target_pairs={{0,4},{1,5},{2,6},{3,7},{4,0},{5,1},{6,2},{7,3},{8,12},{9,13},{10,... | collective-permute-start | bytes 983048 | tf_op jit(solution)/shard_map/ppermute | solution.py:25
  55.3 13.3 %collective-permute-start.16 = (bf16[32,5120]{1,0:T(8,128)(2,1)S(1)}, bf16[32,5120]{1,0:T(8,128)(2,1)S(1)}, u32[]{:S(2)}, u32[]{:S(2)}) collective-permute-start(bf16[32,5120]{1,0:T(8,128)(2,1)S(1)} %add_convert_fusion.3), channel_id=1, source_target_pairs={{0,6},{1,7},{2,0},{3,1},{4,2},{5,3},{6,4},{7,5},{8,14},{9,15},{10,... | collective-permute-start | bytes 983048 | tf_op jit(solution)/shard_map/ppermute | solution.py:25
  61.2 9.9 %collective-permute-start.18 = (bf16[32,5120]{1,0:T(8,128)(2,1)S(1)}, bf16[32,5120]{1,0:T(8,128)(2,1)S(1)}, u32[]{:S(2)}, u32[]{:S(2)}) collective-permute-start(bf16[32,5120]{1,0:T(8,128)(2,1)S(1)} %add_convert_fusion.2), channel_id=1, source_target_pairs={{0,2},{1,3},{2,4},{3,5},{4,6},{5,7},{6,0},{7,1},{8,10},{9,11},{10,... | collective-permute-start | bytes 983048 | tf_op jit(solution)/shard_map/ppermute | solution.py:25
  61.7 10.0 %collective-permute-start.19 = (bf16[32,5120]{1,0:T(8,128)(2,1)S(1)}, bf16[32,5120]{1,0:T(8,128)(2,1)S(1)}, u32[]{:S(2)}, u32[]{:S(2)}) collective-permute-start(bf16[32,5120]{1,0:T(8,128)(2,1)S(1)} %add_convert_fusion.1), channel_id=1, source_target_pairs={{0,8},{1,9},{2,10},{3,11},{4,12},{5,13},{6,14},{7,15},{8,0},{9,1},... | collective-permute-start | bytes 983048 | tf_op jit(solution)/shard_map/ppermute | solution.py:25
  71.9 8.4 %collective-permute-start.20 = (bf16[8,5120]{1,0:T(8,128)(2,1)S(1)}, bf16[8,5120]{1,0:T(8,128)(2,1)S(1)}, u32[]{:S(2)}, u32[]{:S(2)}) collective-permute-start(bf16[8,5120]{1,0:T(8,128)(2,1)S(1)} %dynamic-slice_bitcast_fusion), channel_id=1, source_target_pairs={{0,16},{16,32},{32,48},{48,64},{64,80},{80,96},{96,112},{1,17},{17... | collective-permute-start | bytes 245768 | tf_op jit(solution)/shard_map/ppermute | solution.py:31

commit v5 on v4

--- a/solution.py
+++ b/solution.py
@@ -27,7 +27,7 @@
 
 def from_behind(x, axis, by):
     count = lax.axis_size(axis)
-    pairs = [(i, i + by) for i in range(count) if 0 <= i + by < count]
+    pairs = [(i, (i + by) % count) for i in range(count)]
     return lax.ppermute(x, axis, pairs)
 
 
@@ -99,9 +99,10 @@
 
 
 def gather_rows(xs, rows_ref):
-    rows = xs[0].shape[0]
-    for i, x in enumerate(xs):
-        rows_ref[i * rows : (i + 1) * rows, :] = x[...]
+    at = 0
+    for x in xs:
+        rows_ref[at : at + x.shape[0], :] = x[...]
+        at += x.shape[0]
 
 
 def first_kernel(pieces, *refs):
@@ -135,8 +136,8 @@
 
 def first_call(xs, gains, w_mine, w_other):
     pieces = len(xs)
-    rows, width = xs[0].shape
-    total, cols = rows * pieces, w_mine.shape[2]
+    width = xs[0].shape[1]
+    total, cols = sum(x.shape[0] for x in xs), w_mine.shape[2]
     return pl.pallas_call(
         functools.partial(first_kernel, pieces),
         in_specs=[VMEM] * (pieces + 3) + [ANY, VMEM],
@@ -157,8 +158,8 @@
 
 def rest_call(xs, gains, held, w_other):
     pieces = len(xs)
-    rows, width = xs[0].shape
-    total, cols = rows * pieces, held.shape[2]
+    width = xs[0].shape[1]
+    total, cols = sum(x.shape[0] for x in xs), held.shape[2]
     return pl.pallas_call(
         functools.partial(rest_kernel, pieces),
         in_specs=[VMEM] * (pieces + 5),
@@ -195,12 +196,13 @@
 
 
 def out_project(attn_ref, w_mine, w_other, outs):
-    rows, cols = outs[0].shape[0], w_mine.shape[0]
+    cols, at = w_mine.shape[0], 0
     part = jnp.dot(attn_ref[:, :cols], w_mine[...], preferred_element_type=jnp.float32)
     part += jnp.dot(attn_ref[:, cols:], w_other[...], preferred_element_type=jnp.float32)
     part = part.astype(jnp.bfloat16)
-    for i, out in enumerate(outs):
-        out[...] = part[i * rows : (i + 1) * rows, :]
+    for out in outs:
+        out[...] = part[at : at + out.shape[0], :]
+        at += out.shape[0]
 
 
 def far_kernel(pieces, q_a, q_b, kv_a, kv_b, far_a, far_b, w_mine, w_other, *refs):
@@ -212,7 +214,8 @@
         half, tail = cut + most, q_ref.shape[1] - most
         for owner in range(2):
             q_ref[owner, :most, :] = q_b[owner]
-            q_ref[owner, most:, :] = q_a[owner, cut - tail :, :]
+            if tail:
+                q_ref[owner, most:, :] = q_a[owner, cut - tail :, :]
             for kind in range(2):
                 near, far = 2 * owner + kind, 2 * (1 - owner) + kind
                 kv_ref[near, :cut, :] = kv_a[near]
@@ -235,18 +238,17 @@
     out_project(attn_ref, w_mine, w_other, outs)
 
 
-def attend_call(kernel, operands, w_mine, w_other, rows, pieces, keys=None):
+def attend_call(kernel, operands, w_mine, w_other, sizes, length, keys=None):
     cols, width = w_mine.shape
-    total, block = rows * pieces, 1024
+    total, block = sum(sizes), 1024
     whole = lambda shape: pl.BlockSpec(shape, lambda i: (0,) * len(shape))
-    length = 2 * 8 * rows
-    out_shape = [jax.ShapeDtypeStruct((rows, width), jnp.bfloat16)] * pieces
-    out_specs = [pl.BlockSpec((rows, block), lambda i: (0, i))] * pieces
+    out_shape = [jax.ShapeDtypeStruct((rows, width), jnp.bfloat16) for rows in sizes]
+    out_specs = [pl.BlockSpec((rows, block), lambda i: (0, i)) for rows in sizes]
     if keys is not None:
         out_shape = out_shape + [jax.ShapeDtypeStruct(keys, jnp.bfloat16)]
         out_specs = out_specs + [whole(keys)]
     return pl.pallas_call(
-        functools.partial(kernel, pieces),
+        functools.partial(kernel, len(sizes)),
         grid=(width // block,),
         in_specs=[whole(x.shape) for x in operands] + [pl.BlockSpec((cols, block), lambda i: (0, i))] * 2,
         out_specs=out_specs,
@@ -280,7 +282,7 @@
     right = hop(normed, dx=-1)
     far = hop(normed, dz=1)
     across_send, _ = lax.optimization_barrier((normed, left))
-    across = hop(across_send, dx=2)
+    across = [hop(across_send, dx=2)]
     far_left = hop(left, dz=1)
     far_right = hop(right, dz=1)
     far_send, out_send, _ = lax.optimization_barrier((far, w_out, w_other))
@@ -288,26 +290,32 @@
 
     out_other = hop(out_send, dc=1)
 
-    q_a, kv_a, held = first_call([normed, left, right, far, across], gains, w_mine, w_other)
+    q_a, kv_a, held = first_call([normed, left, right, far], gains, w_mine, w_other)
     far_a = hop(kv_a, dc=1)
-    q_b, kv_b = rest_call([far_left, far_right, far_across], gains, held, w_other)
+    q_b, kv_b = rest_call([far_left, far_right, far_across, *across], gains, held, w_other)
     far_b = hop(kv_b, dc=1)
     keys = (4, 16 * rows, kv_a.shape[2])
     operands = (q_a, q_b, kv_a, kv_b, far_a, far_b)
-    p_far_left, p_far_right, p_far_across, p_across, kv = attend_call(
-        far_kernel, operands, w_out, out_other, rows, 4, keys
+    sizes = [rows, rows, rows, rows // 2, rows // 2]
+    p_far_left, p_far_right, p_far_across, p_before, p_after, kv = attend_call(
+        far_kernel, operands, w_out, out_other, sizes, keys[1], keys
     )
-    p_own, p_left, p_right, p_far = attend_call(near_kernel, (q_a, kv), w_out, out_other, rows, 4)
+    p_own, p_left, p_right, p_far = attend_call(near_kernel, (q_a, kv), w_out, out_other, [rows] * 4, keys[1])
 
     def add(a, b):
         return (a.astype(jnp.float32) + b.astype(jnp.float32)).astype(jnp.bfloat16)
 
-    from_across = hop(p_far_across, dx=2)
-    across_send, _ = lax.optimization_barrier((p_across, from_across))
-    s_left = add(p_left, hop(p_far_left, dz=1))
-    s_right = add(p_right, hop(p_far_right, dz=1))
-    s_far = add(p_far, from_across)
-    arrived = [hop(across_send, dx=2), hop(s_left, dx=-1), hop(s_right, dx=1), hop(s_far, dz=1)]
+    def add_part(a, b, part, at):
+        total = a.astype(jnp.float32) + b.astype(jnp.float32)
+        part = part.astype(jnp.float32)
+        halves = (total[: rows // 2], total[rows // 2 :])
+        halves = (halves[0] + part, halves[1]) if at == 0 else (halves[0], halves[1] + part)
+        return jnp.concatenate(halves, axis=0).astype(jnp.bfloat16)
+
+    s_right = add_part(p_right, hop(p_far_right, dz=1), hop(p_before, dx=1), 0)
+    s_left = add_part(p_left, hop(p_far_left, dz=1), hop(p_after, dx=-1), 1)
+    s_far = add(p_far, hop(p_far_across, dx=2))
+    arrived = [hop(s_left, dx=-1), hop(s_right, dx=1), hop(s_far, dz=1)]
     proj = p_own.astype(jnp.float32)
     for piece in arrived:
         proj = proj + piece.astype(jnp.float32)

time: 81.5 us -> 79.2 us (0.972)
  Pallas kernels: 17.3 us -> 15.6 us
  starting transfers between devices: 24.8 us -> 23.1 us
    ppermute x1, starting transfers between devices: 3.44 us -> 1.64 us  [from_behind(): return lax.ppermute(x, axis, pairs)]
    pallas_call x1, Pallas kernels: 5.79 us -> 4.44 us  [first_call(): pl.pallas_call(functools.partial(first_kernel, pieces), in_specs=[VMEM] *...]
    ppermute x20 -> x21, waiting for transfers between devices: 31.3 us -> 31.7 us  [hop(): return lax.ppermute(value, 'seq', pairs)]
    ppermute x20 -> x21, starting transfers between devices: 21.4 us -> 21.5 us  [hop(): return lax.ppermute(value, 'seq', pairs)]
  transfers between devices with their start and end apart: 21 -> 22, of which waited for: 12 -> 11; matrix products, arithmetic and copies ran while one was open for 0% -> 0% of each run, Pallas kernels for 17% -> 15%
where the time goes in v5:
time: 79.2 us; the launch traced here: 78.3 us
  waiting for transfers between devices  36.7 us (46%)
  starting transfers between devices  23.1 us (29%)
  Pallas kernels  15.6 us (20%)
  between operations  1.52 us (2%)
  other arithmetic  1.39 us (2%)
    ppermute x21, waiting for transfers between devices, hop(): return lax.ppermute(value, 'seq', pairs)  31.7 us
    ppermute x21, starting transfers between devices, hop(): return lax.ppermute(value, 'seq', pairs)  21.5 us
    pallas_call x2, Pallas kernels, attend_call(): pl.pallas_call(functools.partial(kernel, len(sizes)), grid=(width // bloc...  7.39 us
    ppermute x1, waiting for transfers between devices, from_behind(): return lax.ppermute(x, axis, pairs)  4.97 us
    pallas_call x1, Pallas kernels, first_call(): pl.pallas_call(functools.partial(first_kernel, pieces), in_specs=[VMEM] *...  4.44 us
    pallas_call x1, Pallas kernels, rest_call(): pl.pallas_call(functools.partial(rest_kernel, pieces), in_specs=[VMEM] *...  2.33 us
    ppermute x1, starting transfers between devices, from_behind(): return lax.ppermute(x, axis, pairs)  1.64 us
  transfers between devices with their start and end apart: 22, of which 11 were waited for; matrix products, arithmetic and copies ran while one was open for 0% of the time, Pallas kernels for 15%

profile of v5, /device:TPU:96, one launch (start us, length us, event | category | flops | bytes accessed | tf_op | source)
XLA Modules:
  0.0 78.3 jit_solution(10473788018609568808)
XLA Ops:
  0.0 0.0 collective-permute-start.3
  0.0 0.5 collective-permute-start.4
  1.2 1.4 %shard_map.91 = (bf16[32,5120]{1,0:T(8,128)(2,1)S(1)}, f32[1,5120]{1,0:T(1,128)S(1)}, f32[2,256]{1,0:T(2,128)S(1)}) custom-call(s32[1]{0:T(128)S(6)} %copy.10.step, bf16[32,5120]{1,0:T(8,128)(2,1)} %bitcast.18, f32[50,15360]{1,0:T(8,128)} %table.1, f32[1,256]{1,0:T(1,128)} %bitcast.20, f32[1,256]{1,0:T(1,128)} %bitcast.22), custom_call_target="tpu_custom_call" | custom-call | flops 1638400 | bytes 655360 | tf_op jit(solution)/shard_map/pallas_call | solution.py:59
  2.6 0.0 collective-permute-done.3.refs_5_
  2.6 0.0 collective-permute-done.4.refs_6_
  2.6 0.1 collective-permute-start.5
  2.7 1.6 %collective-permute-start = (bf16[32,5120]{1,0:T(8,128)(2,1)S(1)}, bf16[32,5120]{1,0:T(8,128)(2,1)S(1)}, u32[]{:S(2)}, u32[]{:S(2)}) collective-permute-start(bf16[32,5120]{1,0:T(8,128)(2,1)S(1)} %get-tuple-element.33.refs_0_), channel_id=1, source_target_pairs={{0,2},{1,3},{2,4},{3,5},{4,6},{5,7},{6,0},{7,1},{8,10},{9,11},{10,... | collective-permute-start | bytes 983048 | tf_op jit(solution)/shard_map/ppermute | solution.py:25
  4.3 1.7 %collective-permute-start.1 = (bf16[32,5120]{1,0:T(8,128)(2,1)S(1)}, bf16[32,5120]{1,0:T(8,128)(2,1)S(1)}, u32[]{:S(2)}, u32[]{:S(2)}) collective-permute-start(bf16[32,5120]{1,0:T(8,128)(2,1)S(1)} %get-tuple-element.33.refs_0_), channel_id=1, source_target_pairs={{0,6},{1,7},{2,0},{3,1},{4,2},{5,3},{6,4},{7,5},{8,14},{9,15},{10,... | collective-permute-start | bytes 983048 | tf_op jit(solution)/shard_map/ppermute | solution.py:25
  6.0 0.6 collective-permute-start.2
  6.6 7.5 %collective-permute-done.refs_1_ = bf16[32,5120]{1,0:T(8,128)(2,1)S(1)} collective-permute-done((bf16[32,5120]{1,0:T(8,128)(2,1)S(1)}, bf16[32,5120]{1,0:T(8,128)(2,1)S(1)}, u32[]{:S(2)}, u32[]{:S(2)}) %collective-permute-start) | collective-permute-done | bytes 327712 | tf_op jit(solution)/shard_map/ppermute | solution.py:25
  14.0 1.8 %collective-permute-start.9 = (bf16[32,5120]{1,0:T(8,128)(2,1)S(1)}, bf16[32,5120]{1,0:T(8,128)(2,1)S(1)}, u32[]{:S(2)}, u32[]{:S(2)}) collective-permute-start(bf16[32,5120]{1,0:T(8,128)(2,1)S(1)} %get-tuple-element.33.refs_0_), channel_id=1, source_target_pairs={{0,4},{1,5},{2,6},{3,7},{4,0},{5,1},{6,2},{7,3},{8,12},{9,13},{10,... | collective-permute-start | bytes 983048 | tf_op jit(solution)/shard_map/ppermute | solution.py:25
  15.8 0.6 collective-permute-start.6
  16.4 0.0 collective-permute-done.1.refs_2_
  16.4 3.0 %collective-permute-start.7 = (bf16[32,5120]{1,0:T(8,128)(2,1)S(1)}, bf16[32,5120]{1,0:T(8,128)(2,1)S(1)}, u32[]{:S(2)}, u32[]{:S(2)}) collective-permute-start(bf16[32,5120]{1,0:T(8,128)(2,1)S(1)} %collective-permute-done.1.refs_2_), channel_id=1, source_target_pairs={{0,8},{1,9},{2,10},{3,11},{4,12},{5,13},{6,14},{7,15},{8,0},{9,1},... | collective-permute-start | bytes 983048 | tf_op jit(solution)/shard_map/ppermute | solution.py:25
  19.4 0.0 collective-permute-done.2.refs_3_
  19.4 0.0 collective-permute-done.5.refs_8_
  19.4 1.7 %collective-permute-start.8 = (bf16[32,5120]{1,0:T(8,128)(2,1)S(1)}, bf16[32,5120]{1,0:T(8,128)(2,1)S(1)}, u32[]{:S(2)}, u32[]{:S(2)}) collective-permute-start(bf16[32,5120]{1,0:T(8,128)(2,1)S(1)} %collective-permute-done.2.refs_3_), channel_id=1, source_target_pairs={{0,4},{1,5},{2,6},{3,7},{4,0},{5,1},{6,2},{7,3},{8,12},{9,13},{10,... | collective-permute-start | bytes 983048 | tf_op jit(solution)/shard_map/ppermute | solution.py:25
  21.1 0.0 collective-permute-start.12
  21.1 4.4 %shard_map.92 = (bf16[2,128,256]{2,1,0:T(8,128)(2,1)S(1)}, bf16[4,128,256]{2,1,0:T(8,128)(2,1)S(1)}, bf16[3,5120,256]{2,1,0:T(8,128)(2,1)S(1)}) custom-call(bf16[32,5120]{1,0:T(8,128)(2,1)S(1)} %get-tuple-element.33.refs_0_, bf16[32,5120]{1,0:T(8,128)(2,1)S(1)} %collective-permute-done.refs_1_, bf16[32,5120]{1,0:T(8,128)(2,1)S(1)} %collective-permute-done.1.refs_2_, ...), custom_call_target="tpu_custom_call" | custom-call | flops 80530636800 | bytes 15728640 | tf_op jit(solution)/shard_map/pallas_call | solution.py:141
  25.5 0.6 collective-permute-done.9.refs_3_
  26.2 0.0 collective-permute-start.10
  26.2 1.8 %collective-permute-done.6.refs_0_ = bf16[32,5120]{1,0:T(8,128)(2,1)S(1)} collective-permute-done((bf16[32,5120]{1,0:T(8,128)(2,1)S(1)}, bf16[32,5120]{1,0:T(8,128)(2,1)S(1)}, u32[]{:S(2)}, u32[]{:S(2)}) %collective-permute-start.6) | collective-permute-done | bytes 327712 | tf_op jit(solution)/shard_map/ppermute | solution.py:25
  28.0 5.4 %collective-permute-done.7.refs_1_ = bf16[32,5120]{1,0:T(8,128)(2,1)S(1)} collective-permute-done((bf16[32,5120]{1,0:T(8,128)(2,1)S(1)}, bf16[32,5120]{1,0:T(8,128)(2,1)S(1)}, u32[]{:S(2)}, u32[]{:S(2)}) %collective-permute-start.7) | collective-permute-done | bytes 327712 | tf_op jit(solution)/shard_map/ppermute | solution.py:25
  33.4 0.0 collective-permute-done.8.refs_2_
  33.4 0.0 copy-start
  33.4 2.3 %shard_map.93 = (bf16[2,128,256]{2,1,0:T(8,128)(2,1)S(1)}, bf16[4,128,256]{2,1,0:T(8,128)(2,1)S(1)}) custom-call(bf16[32,5120]{1,0:T(8,128)(2,1)S(1)} %collective-permute-done.6.refs_0_, bf16[32,5120]{1,0:T(8,128)(2,1)S(1)} %collective-permute-done.7.refs_1_, bf16[32,5120]{1,0:T(8,128)(2,1)S(1)} %collective-permute-done.8.refs_2_, ...), custom_call_target="tpu_custom_call" | custom-call | flops 2013265920 | bytes 15728640 | tf_op jit(solution)/shard_map/pallas_call | solution.py:163
  35.7 0.1 collective-permute-start.11
  35.8 0.0 collective-permute-done.10.far_a
  35.8 1.5 %collective-permute-done.11.far_b = bf16[4,128,256]{2,1,0:T(8,128)(2,1)S(1)} collective-permute-done((bf16[4,128,256]{2,1,0:T(8,128)(2,1)S(1)}, bf16[4,128,256]{2,1,0:T(8,128)(2,1)S(1)}, u32[]{:S(2)}, u32[]{:S(2)}) %collective-permute-start.11) | collective-permute-done | bytes 262176 | tf_op jit(solution)/shard_map/ppermute | solution.py:25
  37.3 0.0 collective-permute-done.12.w_other
  37.3 0.0 copy-done
  37.3 3.7 %shard_map.94 = (bf16[32,5120]{1,0:T(8,128)(2,1)S(1)}, bf16[32,5120]{1,0:T(8,128)(2,1)S(1)}, bf16[32,5120]{1,0:T(8,128)(2,1)S(1)}, bf16[16,5120]{1,0:T(8,128)(2,...) custom-call(bf16[2,128,256]{2,1,0:T(8,128)(2,1)S(1)} %get-tuple-element.31.q_a, ...), custom_call_target="tpu_custom_call" | custom-call | flops 805306368 | bytes 5242880 | tf_op jit(solution)/shard_map/pallas_call | solution.py:250
  41.1 0.0 copy-start.1
  41.1 0.0 copy-start.2
  41.1 0.6 collective-permute-start.13
  41.7 1.1 %collective-permute-start.14 = (bf16[16,5120]{1,0:T(8,128)(2,1)S(1)}, bf16[16,5120]{1,0:T(8,128)(2,1)S(1)}, u32[]{:S(2)}, u32[]{:S(2)}) collective-permute-start(bf16[16,5120]{1,0:T(8,128)(2,1)S(1)} %get-tuple-element.43), channel_id=1, source_target_pairs={{0,6},{1,7},{2,0},{3,1},{4,2},{5,3},{6,4},{7,5},{8,14},{9,15},{10,... | collective-permute-start | bytes 491528 | tf_op jit(solution)/shard_map/ppermute | solution.py:25
  42.9 3.0 %collective-permute-start.16 = (bf16[32,5120]{1,0:T(8,128)(2,1)S(1)}, bf16[32,5120]{1,0:T(8,128)(2,1)S(1)}, u32[]{:S(2)}, u32[]{:S(2)}) collective-permute-start(bf16[32,5120]{1,0:T(8,128)(2,1)S(1)} %get-tuple-element.45), channel_id=1, source_target_pairs={{0,8},{1,9},{2,10},{3,11},{4,12},{5,13},{6,14},{7,15},{8,0},{9,1},... | collective-permute-start | bytes 983048 | tf_op jit(solution)/shard_map/ppermute | solution.py:25
  45.8 0.9 %collective-permute-start.17 = (bf16[16,5120]{1,0:T(8,128)(2,1)S(1)}, bf16[16,5120]{1,0:T(8,128)(2,1)S(1)}, u32[]{:S(2)}, u32[]{:S(2)}) collective-permute-start(bf16[16,5120]{1,0:T(8,128)(2,1)S(1)} %get-tuple-element.46), channel_id=1, source_target_pairs={{0,2},{1,3},{2,4},{3,5},{4,6},{5,7},{6,0},{7,1},{8,10},{9,11},{10,... | collective-permute-start | bytes 491528 | tf_op jit(solution)/shard_map/ppermute | solution.py:25
  46.7 1.7 %collective-permute-start.19 = (bf16[32,5120]{1,0:T(8,128)(2,1)S(1)}, bf16[32,5120]{1,0:T(8,128)(2,1)S(1)}, u32[]{:S(2)}, u32[]{:S(2)}) collective-permute-start(bf16[32,5120]{1,0:T(8,128)(2,1)S(1)} %get-tuple-element.48), channel_id=1, source_target_pairs={{0,4},{1,5},{2,6},{3,7},{4,0},{5,1},{6,2},{7,3},{8,12},{9,13},{10,... | collective-permute-start | bytes 983048 | tf_op jit(solution)/shard_map/ppermute | solution.py:25
  48.4 3.7 %shard_map.95 = (bf16[32,5120]{1,0:T(8,128)(2,1)S(1)}, bf16[32,5120]{1,0:T(8,128)(2,1)S(1)}, bf16[32,5120]{1,0:T(8,128)(2,1)S(1)}, bf16[32,5120]{1,0:T(8,128)(2,1)S(1)}) custom-call(bf16[2,128,256]{2,1,0:T(8,128)(2,1)S(1)} %get-tuple-element.31.q_a, bf16[4,512,256]{2,1,0:T(8,128)(2,1)S(1)} %get-tuple-element.39.kv_ref, bf16[256,5120]{1,0:T(8,128)(2,1)S(1)} %copy-done, ...), custom_call_target="tpu_custom_call" | custom-call | flops 805306368 | bytes 5242880 | tf_op jit(solution)/shard_map/pallas_call | solution.py:250
  52.1 1.1 %collective-permute-done.13 = bf16[32,5120]{1,0:T(8,128)(2,1)S(1)} collective-permute-done((bf16[32,5120]{1,0:T(8,128)(2,1)S(1)}, bf16[32,5120]{1,0:T(8,128)(2,1)S(1)}, u32[]{:S(2)}, u32[]{:S(2)}) %collective-permute-start.13) | collective-permute-done | bytes 327712 | tf_op jit(solution)/shard_map/ppermute | solution.py:25
  53.2 0.1 convert_add_fusion.1
  53.3 0.0 collective-permute-done.14
  53.4 1.2 %collective-permute-start.15 = (bf16[32,5120]{1,0:T(8,128)(2,1)S(1)}, bf16[32,5120]{1,0:T(8,128)(2,1)S(1)}, u32[]{:S(2)}, u32[]{:S(2)}) collective-permute-start(bf16[32,5120]{1,0:T(8,128)(2,1)S(1)} %pad_maximum_fusion), channel_id=1, source_target_pairs={{0,6},{1,7},{2,0},{3,1},{4,2},{5,3},{6,4},{7,5},{8,14},{9,15},{10,... | collective-permute-start | bytes 983048 | tf_op jit(solution)/shard_map/ppermute | solution.py:25
  54.6 4.8 %collective-permute-done.16 = bf16[32,5120]{1,0:T(8,128)(2,1)S(1)} collective-permute-done((bf16[32,5120]{1,0:T(8,128)(2,1)S(1)}, bf16[32,5120]{1,0:T(8,128)(2,1)S(1)}, u32[]{:S(2)}, u32[]{:S(2)}) %collective-permute-start.16) | collective-permute-done | bytes 327712 | tf_op jit(solution)/shard_map/ppermute | solution.py:25
  59.4 0.1 convert_add_fusion
  59.5 0.0 collective-permute-done.17
  59.6 0.7 collective-permute-start.18
  60.3 0.0 collective-permute-done.19
  60.3 0.1 add_convert_fusion.1
  60.4 0.6 collective-permute-start.20
  61.7 1.9 %collective-permute-done.15 = bf16[32,5120]{1,0:T(8,128)(2,1)S(1)} collective-permute-done((bf16[32,5120]{1,0:T(8,128)(2,1)S(1)}, bf16[32,5120]{1,0:T(8,128)(2,1)S(1)}, u32[]{:S(2)}, u32[]{:S(2)}) %collective-permute-start.15) | collective-permute-done | bytes 327712 | tf_op jit(solution)/shard_map/ppermute | solution.py:25
  63.6 6.3 %collective-permute-done.18 = bf16[32,5120]{1,0:T(8,128)(2,1)S(1)} collective-permute-done((bf16[32,5120]{1,0:T(8,128)(2,1)S(1)}, bf16[32,5120]{1,0:T(8,128)(2,1)S(1)}, u32[]{:S(2)}, u32[]{:S(2)}) %collective-permute-start.18) | collective-permute-done | bytes 327712 | tf_op jit(solution)/shard_map/ppermute | solution.py:25
  69.8 0.8 collective-permute-done.20
  70.6 0.0 copy-done.1
  70.6 0.2 add_convert_fusion
  70.9 1.6 %collective-permute-start.21 = (bf16[8,5120]{1,0:T(8,128)(2,1)S(1)}, bf16[8,5120]{1,0:T(8,128)(2,1)S(1)}, u32[]{:S(2)}, u32[]{:S(2)}) collective-permute-start(bf16[8,5120]{1,0:T(8,128)(2,1)S(1)} %dynamic-slice_bitcast_fusion), channel_id=1, source_target_pairs={{0,16},{16,32},{32,48},{48,64},{64,80},{80,96},{96,112},{112,0},{1... | collective-permute-start | bytes 245768 | tf_op jit(solution)/shard_map/ppermute | solution.py:31
  72.5 5.0 %collective-permute-done.21 = bf16[8,5120]{1,0:T(8,128)(2,1)S(1)} collective-permute-done((bf16[8,5120]{1,0:T(8,128)(2,1)S(1)}, bf16[8,5120]{1,0:T(8,128)(2,1)S(1)}, u32[]{:S(2)}, u32[]{:S(2)}) %collective-permute-start.21) | collective-permute-done | bytes 81952 | tf_op jit(solution)/shard_map/ppermute | solution.py:31
  77.5 0.0 copy-done.2
  77.5 0.8 %bitcast_select_fusion = bf16[1,4,8,5120]{3,2,1,0:T(8,128)(2,1)} fusion(bf16[32,5120]{1,0:T(8,128)(2,1)S(1)} %add_convert_fusion, pred[4]{0:T(512)(128)(4,1)S(1)} %iota_compare_fusion, bf16[8,5120]{1,0:T(8,128)(2,1)S(1)} %broadcast_select_fusion), kind=kLoop, calls=%fused_computation.12 | loop fusion | flops 163840 | bytes 737284 | tf_op jit(solution)/shard_map/jit(_where)/select_n | solution.py:328
  (9 shorter events, 0.2 us)
Async XLA Ops:
  0.0 2.6 %collective-permute-start.3 = (f32[1,256]{1,0:T(1,128)}, f32[1,256]{1,0:T(1,128)S(1)}, u32[]{:S(2)}, u32[]{:S(2)}) collective-permute-start(f32[1,256]{1,0:T(1,128)} %bitcast.19), channel_id=1, source_target_pairs={{0,1},{1,0},{2,3},{3,2},{4,5},{5,4},{6,7},{7,6},{8,9},{9,8},{10,11... | collective-permute-start | bytes 3080 | tf_op jit(solution)/shard_map/ppermute | solution.py:25
  0.0 2.6 %collective-permute-start.4 = (f32[1,256]{1,0:T(1,128)}, f32[1,256]{1,0:T(1,128)S(1)}, u32[]{:S(2)}, u32[]{:S(2)}) collective-permute-start(f32[1,256]{1,0:T(1,128)} %bitcast.21), channel_id=1, source_target_pairs={{0,1},{1,0},{2,3},{3,2},{4,5},{5,4},{6,7},{7,6},{8,9},{9,8},{10,11... | collective-permute-start | bytes 3080 | tf_op jit(solution)/shard_map/ppermute | solution.py:25
  2.6 16.8 %collective-permute-start.5 = (bf16[3,5120,256]{2,1,0:T(8,128)(2,1)}, bf16[3,5120,256]{2,1,0:T(8,128)(2,1)S(1)}, u32[]{:S(2)}, u32[]{:S(2)}) collective-permute-start(bf16[3,5120,256]{2,1,0:T(8,128)(2,1)} %bitcast.23), channel_id=1, source_target_pairs={{0,1},{1,0},{2,3},{3,2},{4,5},{5,4},{6,7},{7,6},{8,9},{9,8},{10,11... | collective-permute-start | bytes 23592968 | tf_op jit(solution)/shard_map/ppermute | solution.py:25
  2.7 11.3 %collective-permute-start = (bf16[32,5120]{1,0:T(8,128)(2,1)S(1)}, bf16[32,5120]{1,0:T(8,128)(2,1)S(1)}, u32[]{:S(2)}, u32[]{:S(2)}) collective-permute-start(bf16[32,5120]{1,0:T(8,128)(2,1)S(1)} %get-tuple-element.33.refs_0_), channel_id=1, source_target_pairs={{0,2},{1,3},{2,4},{3,5},{4,6},{5,7},{6,0},{7,1},{8,10},{9,11},{10,... | collective-permute-start | bytes 983048 | tf_op jit(solution)/shard_map/ppermute | solution.py:25
  4.3 12.1 %collective-permute-start.1 = (bf16[32,5120]{1,0:T(8,128)(2,1)S(1)}, bf16[32,5120]{1,0:T(8,128)(2,1)S(1)}, u32[]{:S(2)}, u32[]{:S(2)}) collective-permute-start(bf16[32,5120]{1,0:T(8,128)(2,1)S(1)} %get-tuple-element.33.refs_0_), channel_id=1, source_target_pairs={{0,6},{1,7},{2,0},{3,1},{4,2},{5,3},{6,4},{7,5},{8,14},{9,15},{10,... | collective-permute-start | bytes 983048 | tf_op jit(solution)/shard_map/ppermute | solution.py:25
  6.0 13.4 %collective-permute-start.2 = (bf16[32,5120]{1,0:T(8,128)(2,1)S(1)}, bf16[32,5120]{1,0:T(8,128)(2,1)S(1)}, u32[]{:S(2)}, u32[]{:S(2)}) collective-permute-start(bf16[32,5120]{1,0:T(8,128)(2,1)S(1)} %get-tuple-element.33.refs_0_), channel_id=1, source_target_pairs={{0,8},{1,9},{2,10},{3,11},{4,12},{5,13},{6,14},{7,15},{8,0},{9,1},... | collective-permute-start | bytes 983048 | tf_op jit(solution)/shard_map/ppermute | solution.py:25
  14.0 12.1 %collective-permute-start.9 = (bf16[32,5120]{1,0:T(8,128)(2,1)S(1)}, bf16[32,5120]{1,0:T(8,128)(2,1)S(1)}, u32[]{:S(2)}, u32[]{:S(2)}) collective-permute-start(bf16[32,5120]{1,0:T(8,128)(2,1)S(1)} %get-tuple-element.33.refs_0_), channel_id=1, source_target_pairs={{0,4},{1,5},{2,6},{3,7},{4,0},{5,1},{6,2},{7,3},{8,12},{9,13},{10,... | collective-permute-start | bytes 983048 | tf_op jit(solution)/shard_map/ppermute | solution.py:25
  15.8 12.2 %collective-permute-start.6 = (bf16[32,5120]{1,0:T(8,128)(2,1)S(1)}, bf16[32,5120]{1,0:T(8,128)(2,1)S(1)}, u32[]{:S(2)}, u32[]{:S(2)}) collective-permute-start(bf16[32,5120]{1,0:T(8,128)(2,1)S(1)} %collective-permute-done.refs_1_), channel_id=1, source_target_pairs={{0,8},{1,9},{2,10},{3,11},{4,12},{5,13},{6,14},{7,15},{8,0},{9,1},... | collective-permute-start | bytes 983048 | tf_op jit(solution)/shard_map/ppermute | solution.py:25
  16.4 17.0 %collective-permute-start.7 = (bf16[32,5120]{1,0:T(8,128)(2,1)S(1)}, bf16[32,5120]{1,0:T(8,128)(2,1)S(1)}, u32[]{:S(2)}, u32[]{:S(2)}) collective-permute-start(bf16[32,5120]{1,0:T(8,128)(2,1)S(1)} %collective-permute-done.1.refs_2_), channel_id=1, source_target_pairs={{0,8},{1,9},{2,10},{3,11},{4,12},{5,13},{6,14},{7,15},{8,0},{9,1},... | collective-permute-start | bytes 983048 | tf_op jit(solution)/shard_map/ppermute | solution.py:25
  19.4 14.0 %collective-permute-start.8 = (bf16[32,5120]{1,0:T(8,128)(2,1)S(1)}, bf16[32,5120]{1,0:T(8,128)(2,1)S(1)}, u32[]{:S(2)}, u32[]{:S(2)}) collective-permute-start(bf16[32,5120]{1,0:T(8,128)(2,1)S(1)} %collective-permute-done.2.refs_3_), channel_id=1, source_target_pairs={{0,4},{1,5},{2,6},{3,7},{4,0},{5,1},{6,2},{7,3},{8,12},{9,13},{10,... | collective-permute-start | bytes 983048 | tf_op jit(solution)/shard_map/ppermute | solution.py:25
  21.1 16.2 %collective-permute-start.12 = (bf16[256,5120]{1,0:T(8,128)(2,1)}, bf16[256,5120]{1,0:T(8,128)(2,1)S(1)}, u32[]{:S(2)}, u32[]{:S(2)}) collective-permute-start(bf16[256,5120]{1,0:T(8,128)(2,1)} %w_mine.3), channel_id=1, source_target_pairs={{0,1},{1,0},{2,3},{3,2},{4,5},{5,4},{6,7},{7,6},{8,9},{9,8},{10,11... | collective-permute-start | bytes 7864328 | tf_op jit(solution)/shard_map/ppermute | solution.py:25
  26.2 9.6 %collective-permute-start.10 = (bf16[4,128,256]{2,1,0:T(8,128)(2,1)S(1)}, bf16[4,128,256]{2,1,0:T(8,128)(2,1)S(1)}, u32[]{:S(2)}, u32[]{:S(2)}) collective-permute-start(bf16[4,128,256]{2,1,0:T(8,128)(2,1)S(1)} %get-tuple-element.36.kv_a), channel_id=1, source_target_pairs={{0,1},{1,0},{2,3},{3,2},{4,5},{5,4},{6,7},{7,6},{8,9},{9,8},{10,11... | collective-permute-start | bytes 786440 | tf_op jit(solution)/shard_map/ppermute | solution.py:25
  33.4 4.0 %copy-start = (bf16[256,5120]{1,0:T(8,128)(2,1)S(1)}, bf16[256,5120]{1,0:T(8,128)(2,1)}, u32[]{:S(2)}) copy-start(bf16[256,5120]{1,0:T(8,128)(2,1)} %w_mine.3) | copy-start | bytes 7864324
  35.7 1.6 %collective-permute-start.11 = (bf16[4,128,256]{2,1,0:T(8,128)(2,1)S(1)}, bf16[4,128,256]{2,1,0:T(8,128)(2,1)S(1)}, u32[]{:S(2)}, u32[]{:S(2)}) collective-permute-start(bf16[4,128,256]{2,1,0:T(8,128)(2,1)S(1)} %get-tuple-element.37.kv_b), channel_id=1, source_target_pairs={{0,1},{1,0},{2,3},{3,2},{4,5},{5,4},{6,7},{7,6},{8,9},{9,8},{10,11... | collective-permute-start | bytes 786440 | tf_op jit(solution)/shard_map/ppermute | solution.py:25
  41.1 29.5 %copy-start.1 = (bf16[1,4,8,5120]{3,2,1,0:T(8,128)(2,1)S(1)}, bf16[1,4,8,5120]{3,2,1,0:T(8,128)(2,1)}, u32[]{:S(2)}) copy-start(bf16[1,4,8,5120]{3,2,1,0:T(8,128)(2,1)} %param.9) | copy-start | bytes 983044
  41.1 36.4 %copy-start.2 = (bf16[8,5120]{1,0:T(8,128)(2,1)S(1)}, bf16[8,5120]{1,0:T(8,128)(2,1)}, u32[]{:S(2)}) copy-start(bf16[8,5120]{1,0:T(8,128)(2,1)} %param.12) | copy-start | bytes 245764
  41.1 12.1 %collective-permute-start.13 = (bf16[32,5120]{1,0:T(8,128)(2,1)S(1)}, bf16[32,5120]{1,0:T(8,128)(2,1)S(1)}, u32[]{:S(2)}, u32[]{:S(2)}) collective-permute-start(bf16[32,5120]{1,0:T(8,128)(2,1)S(1)} %get-tuple-element.42), channel_id=1, source_target_pairs={{0,8},{1,9},{2,10},{3,11},{4,12},{5,13},{6,14},{7,15},{8,0},{9,1},... | collective-permute-start | bytes 983048 | tf_op jit(solution)/shard_map/ppermute | solution.py:25
  41.7 11.6 %collective-permute-start.14 = (bf16[16,5120]{1,0:T(8,128)(2,1)S(1)}, bf16[16,5120]{1,0:T(8,128)(2,1)S(1)}, u32[]{:S(2)}, u32[]{:S(2)}) collective-permute-start(bf16[16,5120]{1,0:T(8,128)(2,1)S(1)} %get-tuple-element.43), channel_id=1, source_target_pairs={{0,6},{1,7},{2,0},{3,1},{4,2},{5,3},{6,4},{7,5},{8,14},{9,15},{10,... | collective-permute-start | bytes 491528 | tf_op jit(solution)/shard_map/ppermute | solution.py:25
  42.9 16.6 %collective-permute-start.16 = (bf16[32,5120]{1,0:T(8,128)(2,1)S(1)}, bf16[32,5120]{1,0:T(8,128)(2,1)S(1)}, u32[]{:S(2)}, u32[]{:S(2)}) collective-permute-start(bf16[32,5120]{1,0:T(8,128)(2,1)S(1)} %get-tuple-element.45), channel_id=1, source_target_pairs={{0,8},{1,9},{2,10},{3,11},{4,12},{5,13},{6,14},{7,15},{8,0},{9,1},... | collective-permute-start | bytes 983048 | tf_op jit(solution)/shard_map/ppermute | solution.py:25
  45.8 13.7 %collective-permute-start.17 = (bf16[16,5120]{1,0:T(8,128)(2,1)S(1)}, bf16[16,5120]{1,0:T(8,128)(2,1)S(1)}, u32[]{:S(2)}, u32[]{:S(2)}) collective-permute-start(bf16[16,5120]{1,0:T(8,128)(2,1)S(1)} %get-tuple-element.46), channel_id=1, source_target_pairs={{0,2},{1,3},{2,4},{3,5},{4,6},{5,7},{6,0},{7,1},{8,10},{9,11},{10,... | collective-permute-start | bytes 491528 | tf_op jit(solution)/shard_map/ppermute | solution.py:25
  46.7 13.6 %collective-permute-start.19 = (bf16[32,5120]{1,0:T(8,128)(2,1)S(1)}, bf16[32,5120]{1,0:T(8,128)(2,1)S(1)}, u32[]{:S(2)}, u32[]{:S(2)}) collective-permute-start(bf16[32,5120]{1,0:T(8,128)(2,1)S(1)} %get-tuple-element.48), channel_id=1, source_target_pairs={{0,4},{1,5},{2,6},{3,7},{4,0},{5,1},{6,2},{7,3},{8,12},{9,13},{10,... | collective-permute-start | bytes 983048 | tf_op jit(solution)/shard_map/ppermute | solution.py:25
  53.4 10.2 %collective-permute-start.15 = (bf16[32,5120]{1,0:T(8,128)(2,1)S(1)}, bf16[32,5120]{1,0:T(8,128)(2,1)S(1)}, u32[]{:S(2)}, u32[]{:S(2)}) collective-permute-start(bf16[32,5120]{1,0:T(8,128)(2,1)S(1)} %pad_maximum_fusion), channel_id=1, source_target_pairs={{0,6},{1,7},{2,0},{3,1},{4,2},{5,3},{6,4},{7,5},{8,14},{9,15},{10,... | collective-permute-start | bytes 983048 | tf_op jit(solution)/shard_map/ppermute | solution.py:25
  59.6 10.2 %collective-permute-start.18 = (bf16[32,5120]{1,0:T(8,128)(2,1)S(1)}, bf16[32,5120]{1,0:T(8,128)(2,1)S(1)}, u32[]{:S(2)}, u32[]{:S(2)}) collective-permute-start(bf16[32,5120]{1,0:T(8,128)(2,1)S(1)} %pad_maximum_fusion.1), channel_id=1, source_target_pairs={{0,2},{1,3},{2,4},{3,5},{4,6},{5,7},{6,0},{7,1},{8,10},{9,11},{10,... | collective-permute-start | bytes 983048 | tf_op jit(solution)/shard_map/ppermute | solution.py:25
  60.4 10.2 %collective-permute-start.20 = (bf16[32,5120]{1,0:T(8,128)(2,1)S(1)}, bf16[32,5120]{1,0:T(8,128)(2,1)S(1)}, u32[]{:S(2)}, u32[]{:S(2)}) collective-permute-start(bf16[32,5120]{1,0:T(8,128)(2,1)S(1)} %add_convert_fusion.1), channel_id=1, source_target_pairs={{0,8},{1,9},{2,10},{3,11},{4,12},{5,13},{6,14},{7,15},{8,0},{9,1},... | collective-permute-start | bytes 983048 | tf_op jit(solution)/shard_map/ppermute | solution.py:25
  70.9 6.6 %collective-permute-start.21 = (bf16[8,5120]{1,0:T(8,128)(2,1)S(1)}, bf16[8,5120]{1,0:T(8,128)(2,1)S(1)}, u32[]{:S(2)}, u32[]{:S(2)}) collective-permute-start(bf16[8,5120]{1,0:T(8,128)(2,1)S(1)} %dynamic-slice_bitcast_fusion), channel_id=1, source_target_pairs={{0,16},{16,32},{32,48},{48,64},{64,80},{80,96},{96,112},{112,0},{1... | collective-permute-start | bytes 245768 | tf_op jit(solution)/shard_map/ppermute | solution.py:31

commit v6 on v5

--- a/solution.py
+++ b/solution.py
@@ -196,74 +196,60 @@
 
 
 def out_project(attn_ref, w_mine, w_other, outs):
-    cols, at = w_mine.shape[0], 0
-    part = jnp.dot(attn_ref[:, :cols], w_mine[...], preferred_element_type=jnp.float32)
-    part += jnp.dot(attn_ref[:, cols:], w_other[...], preferred_element_type=jnp.float32)
-    part = part.astype(jnp.bfloat16)
-    for out in outs:
-        out[...] = part[at : at + out.shape[0], :]
-        at += out.shape[0]
-
-
-def far_kernel(pieces, q_a, q_b, kv_a, kv_b, far_a, far_b, w_mine, w_other, *refs):
-    outs, (kv_ref, q_ref, attn_ref) = refs[:pieces], refs[pieces:]
-
-    @pl.when(pl.program_id(0) == 0)
-    def _():
-        cut, most = q_a.shape[1], q_b.shape[1]
-        half, tail = cut + most, q_ref.shape[1] - most
-        for owner in range(2):
-            q_ref[owner, :most, :] = q_b[owner]
-            if tail:
-                q_ref[owner, most:, :] = q_a[owner, cut - tail :, :]
-            for kind in range(2):
-                near, far = 2 * owner + kind, 2 * (1 - owner) + kind
-                kv_ref[near, :cut, :] = kv_a[near]
-                kv_ref[near, cut:half, :] = kv_b[near]
-                kv_ref[near, half : half + cut, :] = far_a[far]
-                kv_ref[near, half + cut :, :] = far_b[far]
-        attend(q_ref, kv_ref, attn_ref)
-
+    cols, width = w_mine.shape
+    block = 1024
+    for start in range(0, width, block):
+        span = slice(start, start + block)
+        part = jnp.dot(attn_ref[:, :cols], w_mine[:, span], preferred_element_type=jnp.float32)
+        part += jnp.dot(attn_ref[:, cols:], w_other[:, span], preferred_element_type=jnp.float32)
+        part = part.astype(jnp.bfloat16)
+        at = 0
+        for out in outs:
+            out[:, span] = part[at : at + out.shape[0], :]
+            at += out.shape[0]
+
+
+def far_kernel(pieces, q_b, kv_a, kv_b, far_a, far_b, w_mine, w_other, *refs):
+    outs, (kv_ref, attn_ref) = refs[:pieces], refs[pieces:]
+    cut, most = kv_a.shape[1], kv_b.shape[1]
+    half = cut + most
+    for owner in range(2):
+        for kind in range(2):
+            near, far = 2 * owner + kind, 2 * (1 - owner) + kind
+            kv_ref[near, :cut, :] = kv_a[near]
+            kv_ref[near, cut:half, :] = kv_b[near]
+            kv_ref[near, half : half + cut, :] = far_a[far]
+            kv_ref[near, half + cut :, :] = far_b[far]
+    attend(q_b, kv_ref, attn_ref)
     out_project(attn_ref, w_mine, w_other, outs)
 
 
-def near_kernel(pieces, q_a, kv_ref, w_mine, w_other, *refs):
-    outs, (q_ref, attn_ref) = refs[:pieces], refs[pieces:]
-
-    @pl.when(pl.program_id(0) == 0)
-    def _():
-        q_ref[...] = q_a[:, : q_ref.shape[1], :]
-        attend(q_ref, kv_ref, attn_ref)
-
+def near_kernel(pieces, q_ref, kv_ref, w_mine, w_other, *refs):
+    outs, attn_ref = refs[:pieces], refs[pieces]
+    attend(q_ref, kv_ref, attn_ref)
     out_project(attn_ref, w_mine, w_other, outs)
 
 
 def attend_call(kernel, operands, w_mine, w_other, sizes, length, keys=None):
     cols, width = w_mine.shape
-    total, block = sum(sizes), 1024
-    whole = lambda shape: pl.BlockSpec(shape, lambda i: (0,) * len(shape))
+    total = sum(sizes)
     out_shape = [jax.ShapeDtypeStruct((rows, width), jnp.bfloat16) for rows in sizes]
-    out_specs = [pl.BlockSpec((rows, block), lambda i: (0, i)) for rows in sizes]
     if keys is not None:
         out_shape = out_shape + [jax.ShapeDtypeStruct(keys, jnp.bfloat16)]
-        out_specs = out_specs + [whole(keys)]
+    in_vmem = lambda array: pltpu.with_memory_space_constraint(array, pltpu.VMEM)
     return pl.pallas_call(
         functools.partial(kernel, len(sizes)),
-        grid=(width // block,),
-        in_specs=[whole(x.shape) for x in operands] + [pl.BlockSpec((cols, block), lambda i: (0, i))] * 2,
-        out_specs=out_specs,
+        in_specs=[VMEM] * (len(operands) + 2),
+        out_specs=[VMEM] * len(out_shape),
         out_shape=out_shape,
-        scratch_shapes=[
-            pltpu.VMEM((2, total, cols), jnp.bfloat16),
-            pltpu.VMEM((total, 2 * cols), jnp.bfloat16),
-        ],
+        scratch_shapes=[pltpu.VMEM((total, 2 * cols), jnp.bfloat16)],
         compiler_params=pltpu.CompilerParams(vmem_limit_bytes=24 * MIB),
         cost_estimate=pl.CostEstimate(
             flops=4 * total * cols * width + 8 * total * length * cols,
             bytes_accessed=4 * cols * width,
             transcendentals=4 * total * length,
         ),
-    )(*operands, w_mine, w_other)
+    )(*operands, in_vmem(w_mine), in_vmem(w_other))
 
 
 def body(latents, steps, leaving, fresh, mod_table, w_qkv, q_gain, k_gain, w_out):
@@ -295,10 +281,9 @@
     q_b, kv_b = rest_call([far_left, far_right, far_across, *across], gains, held, w_other)
     far_b = hop(kv_b, dc=1)
     keys = (4, 16 * rows, kv_a.shape[2])
-    operands = (q_a, q_b, kv_a, kv_b, far_a, far_b)
-    sizes = [rows, rows, rows, rows // 2, rows // 2]
+    half = rows // 2
     p_far_left, p_far_right, p_far_across, p_before, p_after, kv = attend_call(
-        far_kernel, operands, w_out, out_other, sizes, keys[1], keys
+        far_kernel, (q_b, kv_a, kv_b, far_a, far_b), w_out, out_other, [rows] * 3 + [half] * 2, keys[1], keys
     )
     p_own, p_left, p_right, p_far = attend_call(near_kernel, (q_a, kv), w_out, out_other, [rows] * 4, keys[1])
 

time: 79.2 us -> 77.8 us (0.982)
  Pallas kernels: 15.6 us -> 12.9 us
  waiting for transfers between devices: 36.7 us -> 38 us
    pallas_call x2, Pallas kernels: 7.39 us -> 4.69 us  [attend_call(): pl.pallas_call(functools.partial(kernel, len(sizes)), in_specs=[VMEM] * (...]
    ppermute x21, waiting for transfers between devices: 31.7 us -> 33 us  [hop(): return lax.ppermute(value, 'seq', pairs)]
  transfers between devices with their start and end apart: 22 -> 22, of which waited for: 11 -> 11; matrix products, arithmetic and copies ran while one was open for 0% -> 0% of each run, Pallas kernels for 15% -> 14%
where the time goes in v6:
time: 77.8 us; the launch traced here: 76.9 us
  waiting for transfers between devices  38 us (49%)
  starting transfers between devices  23.1 us (30%)
  Pallas kernels  12.9 us (17%)
  between operations  1.51 us (2%)
  other arithmetic  1.4 us (2%)
    ppermute x21, waiting for transfers between devices, hop(): return lax.ppermute(value, 'seq', pairs)  33 us
    ppermute x21, starting transfers between devices, hop(): return lax.ppermute(value, 'seq', pairs)  21.5 us
    ppermute x1, waiting for transfers between devices, from_behind(): return lax.ppermute(x, axis, pairs)  4.97 us
    pallas_call x2, Pallas kernels, attend_call(): pl.pallas_call(functools.partial(kernel, len(sizes)), in_specs=[VMEM] * (...  4.69 us
    pallas_call x1, Pallas kernels, first_call(): pl.pallas_call(functools.partial(first_kernel, pieces), in_specs=[VMEM] *...  4.43 us
    pallas_call x1, Pallas kernels, rest_call(): pl.pallas_call(functools.partial(rest_kernel, pieces), in_specs=[VMEM] *...  2.33 us
    ppermute x1, starting transfers between devices, from_behind(): return lax.ppermute(x, axis, pairs)  1.64 us
  transfers between devices with their start and end apart: 22, of which 11 were waited for; matrix products, arithmetic and copies ran while one was open for 0% of the time, Pallas kernels for 14%

profile of v6, /device:TPU:96, one launch (start us, length us, event | category | flops | bytes accessed | tf_op | source)
XLA Modules:
  0.0 76.9 jit_solution(17086617431346164437)
XLA Ops:
  0.0 0.0 collective-permute-start.3
  0.0 0.5 collective-permute-start.4
  1.2 1.4 %shard_map.91 = (bf16[32,5120]{1,0:T(8,128)(2,1)S(1)}, f32[1,5120]{1,0:T(1,128)S(1)}, f32[2,256]{1,0:T(2,128)S(1)}) custom-call(s32[1]{0:T(128)S(6)} %copy.10.step, bf16[32,5120]{1,0:T(8,128)(2,1)} %bitcast.18, f32[50,15360]{1,0:T(8,128)} %table.1, f32[1,256]{1,0:T(1,128)} %bitcast.20, f32[1,256]{1,0:T(1,128)} %bitcast.22), custom_call_target="tpu_custom_call" | custom-call | flops 1638400 | bytes 655360 | tf_op jit(solution)/shard_map/pallas_call | solution.py:59
  2.6 0.0 collective-permute-done.3.refs_5_
  2.6 0.0 collective-permute-done.4.refs_6_
  2.6 0.1 collective-permute-start.5
  2.7 1.6 %collective-permute-start = (bf16[32,5120]{1,0:T(8,128)(2,1)S(1)}, bf16[32,5120]{1,0:T(8,128)(2,1)S(1)}, u32[]{:S(2)}, u32[]{:S(2)}) collective-permute-start(bf16[32,5120]{1,0:T(8,128)(2,1)S(1)} %get-tuple-element.33.refs_0_), channel_id=1, source_target_pairs={{0,2},{1,3},{2,4},{3,5},{4,6},{5,7},{6,0},{7,1},{8,10},{9,11},{10,... | collective-permute-start | bytes 983048 | tf_op jit(solution)/shard_map/ppermute | solution.py:25
  4.3 1.7 %collective-permute-start.1 = (bf16[32,5120]{1,0:T(8,128)(2,1)S(1)}, bf16[32,5120]{1,0:T(8,128)(2,1)S(1)}, u32[]{:S(2)}, u32[]{:S(2)}) collective-permute-start(bf16[32,5120]{1,0:T(8,128)(2,1)S(1)} %get-tuple-element.33.refs_0_), channel_id=1, source_target_pairs={{0,6},{1,7},{2,0},{3,1},{4,2},{5,3},{6,4},{7,5},{8,14},{9,15},{10,... | collective-permute-start | bytes 983048 | tf_op jit(solution)/shard_map/ppermute | solution.py:25
  6.0 0.6 collective-permute-start.2
  6.6 7.5 %collective-permute-done.refs_1_ = bf16[32,5120]{1,0:T(8,128)(2,1)S(1)} collective-permute-done((bf16[32,5120]{1,0:T(8,128)(2,1)S(1)}, bf16[32,5120]{1,0:T(8,128)(2,1)S(1)}, u32[]{:S(2)}, u32[]{:S(2)}) %collective-permute-start) | collective-permute-done | bytes 327712 | tf_op jit(solution)/shard_map/ppermute | solution.py:25
  14.0 1.8 %collective-permute-start.9 = (bf16[32,5120]{1,0:T(8,128)(2,1)S(1)}, bf16[32,5120]{1,0:T(8,128)(2,1)S(1)}, u32[]{:S(2)}, u32[]{:S(2)}) collective-permute-start(bf16[32,5120]{1,0:T(8,128)(2,1)S(1)} %get-tuple-element.33.refs_0_), channel_id=1, source_target_pairs={{0,4},{1,5},{2,6},{3,7},{4,0},{5,1},{6,2},{7,3},{8,12},{9,13},{10,... | collective-permute-start | bytes 983048 | tf_op jit(solution)/shard_map/ppermute | solution.py:25
  15.8 0.6 collective-permute-start.6
  16.4 0.0 collective-permute-done.1.refs_2_
  16.4 3.0 %collective-permute-start.7 = (bf16[32,5120]{1,0:T(8,128)(2,1)S(1)}, bf16[32,5120]{1,0:T(8,128)(2,1)S(1)}, u32[]{:S(2)}, u32[]{:S(2)}) collective-permute-start(bf16[32,5120]{1,0:T(8,128)(2,1)S(1)} %collective-permute-done.1.refs_2_), channel_id=1, source_target_pairs={{0,8},{1,9},{2,10},{3,11},{4,12},{5,13},{6,14},{7,15},{8,0},{9,1},... | collective-permute-start | bytes 983048 | tf_op jit(solution)/shard_map/ppermute | solution.py:25
  19.4 0.0 collective-permute-done.2.refs_3_
  19.4 0.0 collective-permute-done.5.refs_8_
  19.4 1.7 %collective-permute-start.8 = (bf16[32,5120]{1,0:T(8,128)(2,1)S(1)}, bf16[32,5120]{1,0:T(8,128)(2,1)S(1)}, u32[]{:S(2)}, u32[]{:S(2)}) collective-permute-start(bf16[32,5120]{1,0:T(8,128)(2,1)S(1)} %collective-permute-done.2.refs_3_), channel_id=1, source_target_pairs={{0,4},{1,5},{2,6},{3,7},{4,0},{5,1},{6,2},{7,3},{8,12},{9,13},{10,... | collective-permute-start | bytes 983048 | tf_op jit(solution)/shard_map/ppermute | solution.py:25
  21.1 0.0 collective-permute-start.12
  21.1 4.4 %shard_map.92 = (bf16[2,128,256]{2,1,0:T(8,128)(2,1)S(1)}, bf16[4,128,256]{2,1,0:T(8,128)(2,1)S(1)}, bf16[3,5120,256]{2,1,0:T(8,128)(2,1)S(1)}) custom-call(bf16[32,5120]{1,0:T(8,128)(2,1)S(1)} %get-tuple-element.33.refs_0_, bf16[32,5120]{1,0:T(8,128)(2,1)S(1)} %collective-permute-done.refs_1_, bf16[32,5120]{1,0:T(8,128)(2,1)S(1)} %collective-permute-done.1.refs_2_, ...), custom_call_target="tpu_custom_call" | custom-call | flops 80530636800 | bytes 15728640 | tf_op jit(solution)/shard_map/pallas_call | solution.py:141
  25.5 0.6 collective-permute-done.9.refs_3_
  26.2 0.0 collective-permute-start.10
  26.2 1.8 %collective-permute-done.6.refs_0_ = bf16[32,5120]{1,0:T(8,128)(2,1)S(1)} collective-permute-done((bf16[32,5120]{1,0:T(8,128)(2,1)S(1)}, bf16[32,5120]{1,0:T(8,128)(2,1)S(1)}, u32[]{:S(2)}, u32[]{:S(2)}) %collective-permute-start.6) | collective-permute-done | bytes 327712 | tf_op jit(solution)/shard_map/ppermute | solution.py:25
  28.0 5.4 %collective-permute-done.7.refs_1_ = bf16[32,5120]{1,0:T(8,128)(2,1)S(1)} collective-permute-done((bf16[32,5120]{1,0:T(8,128)(2,1)S(1)}, bf16[32,5120]{1,0:T(8,128)(2,1)S(1)}, u32[]{:S(2)}, u32[]{:S(2)}) %collective-permute-start.7) | collective-permute-done | bytes 327712 | tf_op jit(solution)/shard_map/ppermute | solution.py:25
  33.4 0.0 collective-permute-done.8.refs_2_
  33.4 0.0 copy-start
  33.4 2.3 %shard_map.93 = (bf16[2,128,256]{2,1,0:T(8,128)(2,1)S(1)}, bf16[4,128,256]{2,1,0:T(8,128)(2,1)S(1)}) custom-call(bf16[32,5120]{1,0:T(8,128)(2,1)S(1)} %collective-permute-done.6.refs_0_, bf16[32,5120]{1,0:T(8,128)(2,1)S(1)} %collective-permute-done.7.refs_1_, bf16[32,5120]{1,0:T(8,128)(2,1)S(1)} %collective-permute-done.8.refs_2_, ...), custom_call_target="tpu_custom_call" | custom-call | flops 2013265920 | bytes 15728640 | tf_op jit(solution)/shard_map/pallas_call | solution.py:163
  35.7 0.1 collective-permute-start.11
  35.8 0.0 collective-permute-done.10.far_a
  35.8 1.5 %collective-permute-done.11.far_b = bf16[4,128,256]{2,1,0:T(8,128)(2,1)S(1)} collective-permute-done((bf16[4,128,256]{2,1,0:T(8,128)(2,1)S(1)}, bf16[4,128,256]{2,1,0:T(8,128)(2,1)S(1)}, u32[]{:S(2)}, u32[]{:S(2)}) %collective-permute-start.11) | collective-permute-done | bytes 262176 | tf_op jit(solution)/shard_map/ppermute | solution.py:25
  37.3 0.0 collective-permute-done.12.w_other
  37.3 0.0 copy-done
  37.3 2.4 %shard_map.94 = (bf16[32,5120]{1,0:T(8,128)(2,1)S(1)}, bf16[32,5120]{1,0:T(8,128)(2,1)S(1)}, bf16[32,5120]{1,0:T(8,128)(2,1)S(1)}, bf16[16,5120]{1,0:T(8,128)(2,...) custom-call(bf16[2,128,256]{2,1,0:T(8,128)(2,1)S(1)} %get-tuple-element.35.q_b, ...), custom_call_target="tpu_custom_call" | custom-call | flops 805306368 | bytes 5242880 | tf_op jit(solution)/shard_map/pallas_call | solution.py:240
  39.7 0.0 copy-start.1
  39.7 0.0 copy-start.2
  39.7 0.6 collective-permute-start.13
  40.3 1.1 %collective-permute-start.14 = (bf16[16,5120]{1,0:T(8,128)(2,1)S(1)}, bf16[16,5120]{1,0:T(8,128)(2,1)S(1)}, u32[]{:S(2)}, u32[]{:S(2)}) collective-permute-start(bf16[16,5120]{1,0:T(8,128)(2,1)S(1)} %get-tuple-element.43), channel_id=1, source_target_pairs={{0,6},{1,7},{2,0},{3,1},{4,2},{5,3},{6,4},{7,5},{8,14},{9,15},{10,... | collective-permute-start | bytes 491528 | tf_op jit(solution)/shard_map/ppermute | solution.py:25
  41.5 3.0 %collective-permute-start.16 = (bf16[32,5120]{1,0:T(8,128)(2,1)S(1)}, bf16[32,5120]{1,0:T(8,128)(2,1)S(1)}, u32[]{:S(2)}, u32[]{:S(2)}) collective-permute-start(bf16[32,5120]{1,0:T(8,128)(2,1)S(1)} %get-tuple-element.45), channel_id=1, source_target_pairs={{0,8},{1,9},{2,10},{3,11},{4,12},{5,13},{6,14},{7,15},{8,0},{9,1},... | collective-permute-start | bytes 983048 | tf_op jit(solution)/shard_map/ppermute | solution.py:25
  44.5 0.9 %collective-permute-start.17 = (bf16[16,5120]{1,0:T(8,128)(2,1)S(1)}, bf16[16,5120]{1,0:T(8,128)(2,1)S(1)}, u32[]{:S(2)}, u32[]{:S(2)}) collective-permute-start(bf16[16,5120]{1,0:T(8,128)(2,1)S(1)} %get-tuple-element.46), channel_id=1, source_target_pairs={{0,2},{1,3},{2,4},{3,5},{4,6},{5,7},{6,0},{7,1},{8,10},{9,11},{10,... | collective-permute-start | bytes 491528 | tf_op jit(solution)/shard_map/ppermute | solution.py:25
  45.3 1.7 %collective-permute-start.19 = (bf16[32,5120]{1,0:T(8,128)(2,1)S(1)}, bf16[32,5120]{1,0:T(8,128)(2,1)S(1)}, u32[]{:S(2)}, u32[]{:S(2)}) collective-permute-start(bf16[32,5120]{1,0:T(8,128)(2,1)S(1)} %get-tuple-element.48), channel_id=1, source_target_pairs={{0,4},{1,5},{2,6},{3,7},{4,0},{5,1},{6,2},{7,3},{8,12},{9,13},{10,... | collective-permute-start | bytes 983048 | tf_op jit(solution)/shard_map/ppermute | solution.py:25
  47.1 2.3 %shard_map.95 = (bf16[32,5120]{1,0:T(8,128)(2,1)S(1)}, bf16[32,5120]{1,0:T(8,128)(2,1)S(1)}, bf16[32,5120]{1,0:T(8,128)(2,1)S(1)}, bf16[32,5120]{1,0:T(8,128)(2,1)S(1)}) custom-call(bf16[2,128,256]{2,1,0:T(8,128)(2,1)S(1)} %get-tuple-element.31.q_ref, bf16[4,512,256]{2,1,0:T(8,128)(2,1)S(1)} %get-tuple-element.39.kv_ref, bf16[256,5120]{1,0:T(8,128)(2,1)S(1)} %copy-done, ...), custom_call_target="tpu_custom_call" | custom-call | flops 805306368 | bytes 5242880 | tf_op jit(solution)/shard_map/pallas_call | solution.py:240
  49.4 2.4 %collective-permute-done.13 = bf16[32,5120]{1,0:T(8,128)(2,1)S(1)} collective-permute-done((bf16[32,5120]{1,0:T(8,128)(2,1)S(1)}, bf16[32,5120]{1,0:T(8,128)(2,1)S(1)}, u32[]{:S(2)}, u32[]{:S(2)}) %collective-permute-start.13) | collective-permute-done | bytes 327712 | tf_op jit(solution)/shard_map/ppermute | solution.py:25
  51.8 0.1 convert_add_fusion.1
  51.9 0.0 collective-permute-done.14
  52.0 1.2 %collective-permute-start.15 = (bf16[32,5120]{1,0:T(8,128)(2,1)S(1)}, bf16[32,5120]{1,0:T(8,128)(2,1)S(1)}, u32[]{:S(2)}, u32[]{:S(2)}) collective-permute-start(bf16[32,5120]{1,0:T(8,128)(2,1)S(1)} %pad_maximum_fusion), channel_id=1, source_target_pairs={{0,6},{1,7},{2,0},{3,1},{4,2},{5,3},{6,4},{7,5},{8,14},{9,15},{10,... | collective-permute-start | bytes 983048 | tf_op jit(solution)/shard_map/ppermute | solution.py:25
  53.2 4.8 %collective-permute-done.16 = bf16[32,5120]{1,0:T(8,128)(2,1)S(1)} collective-permute-done((bf16[32,5120]{1,0:T(8,128)(2,1)S(1)}, bf16[32,5120]{1,0:T(8,128)(2,1)S(1)}, u32[]{:S(2)}, u32[]{:S(2)}) %collective-permute-start.16) | collective-permute-done | bytes 327712 | tf_op jit(solution)/shard_map/ppermute | solution.py:25
  58.1 0.1 convert_add_fusion
  58.2 0.0 collective-permute-done.17
  58.2 0.7 collective-permute-start.18
  58.9 0.0 collective-permute-done.19
  58.9 0.1 add_convert_fusion.1
  59.0 0.6 collective-permute-start.20
  60.3 1.9 %collective-permute-done.15 = bf16[32,5120]{1,0:T(8,128)(2,1)S(1)} collective-permute-done((bf16[32,5120]{1,0:T(8,128)(2,1)S(1)}, bf16[32,5120]{1,0:T(8,128)(2,1)S(1)}, u32[]{:S(2)}, u32[]{:S(2)}) %collective-permute-start.15) | collective-permute-done | bytes 327712 | tf_op jit(solution)/shard_map/ppermute | solution.py:25
  62.2 6.3 %collective-permute-done.18 = bf16[32,5120]{1,0:T(8,128)(2,1)S(1)} collective-permute-done((bf16[32,5120]{1,0:T(8,128)(2,1)S(1)}, bf16[32,5120]{1,0:T(8,128)(2,1)S(1)}, u32[]{:S(2)}, u32[]{:S(2)}) %collective-permute-start.18) | collective-permute-done | bytes 327712 | tf_op jit(solution)/shard_map/ppermute | solution.py:25
  68.4 0.8 %collective-permute-done.20 = bf16[32,5120]{1,0:T(8,128)(2,1)S(1)} collective-permute-done((bf16[32,5120]{1,0:T(8,128)(2,1)S(1)}, bf16[32,5120]{1,0:T(8,128)(2,1)S(1)}, u32[]{:S(2)}, u32[]{:S(2)}) %collective-permute-start.20) | collective-permute-done | bytes 327712 | tf_op jit(solution)/shard_map/ppermute | solution.py:25
  69.2 0.0 copy-done.1
  69.2 0.2 add_convert_fusion
  69.5 1.6 %collective-permute-start.21 = (bf16[8,5120]{1,0:T(8,128)(2,1)S(1)}, bf16[8,5120]{1,0:T(8,128)(2,1)S(1)}, u32[]{:S(2)}, u32[]{:S(2)}) collective-permute-start(bf16[8,5120]{1,0:T(8,128)(2,1)S(1)} %dynamic-slice_bitcast_fusion), channel_id=1, source_target_pairs={{0,16},{16,32},{32,48},{48,64},{64,80},{80,96},{96,112},{112,0},{1... | collective-permute-start | bytes 245768 | tf_op jit(solution)/shard_map/ppermute | solution.py:31
  71.1 5.0 %collective-permute-done.21 = bf16[8,5120]{1,0:T(8,128)(2,1)S(1)} collective-permute-done((bf16[8,5120]{1,0:T(8,128)(2,1)S(1)}, bf16[8,5120]{1,0:T(8,128)(2,1)S(1)}, u32[]{:S(2)}, u32[]{:S(2)}) %collective-permute-start.21) | collective-permute-done | bytes 81952 | tf_op jit(solution)/shard_map/ppermute | solution.py:31
  76.1 0.0 copy-done.2
  76.1 0.8 %bitcast_select_fusion = bf16[1,4,8,5120]{3,2,1,0:T(8,128)(2,1)} fusion(bf16[32,5120]{1,0:T(8,128)(2,1)S(1)} %add_convert_fusion, pred[4]{0:T(512)(128)(4,1)S(1)} %iota_compare_fusion, bf16[8,5120]{1,0:T(8,128)(2,1)S(1)} %broadcast_select_fusion), kind=kLoop, calls=%fused_computation.12 | loop fusion | flops 163840 | bytes 737284 | tf_op jit(solution)/shard_map/jit(_where)/select_n | solution.py:313
  (9 shorter events, 0.2 us)
Async XLA Ops:
  0.0 2.6 %collective-permute-start.3 = (f32[1,256]{1,0:T(1,128)}, f32[1,256]{1,0:T(1,128)S(1)}, u32[]{:S(2)}, u32[]{:S(2)}) collective-permute-start(f32[1,256]{1,0:T(1,128)} %bitcast.19), channel_id=1, source_target_pairs={{0,1},{1,0},{2,3},{3,2},{4,5},{5,4},{6,7},{7,6},{8,9},{9,8},{10,11... | collective-permute-start | bytes 3080 | tf_op jit(solution)/shard_map/ppermute | solution.py:25
  0.0 2.6 %collective-permute-start.4 = (f32[1,256]{1,0:T(1,128)}, f32[1,256]{1,0:T(1,128)S(1)}, u32[]{:S(2)}, u32[]{:S(2)}) collective-permute-start(f32[1,256]{1,0:T(1,128)} %bitcast.21), channel_id=1, source_target_pairs={{0,1},{1,0},{2,3},{3,2},{4,5},{5,4},{6,7},{7,6},{8,9},{9,8},{10,11... | collective-permute-start | bytes 3080 | tf_op jit(solution)/shard_map/ppermute | solution.py:25
  2.6 16.8 %collective-permute-start.5 = (bf16[3,5120,256]{2,1,0:T(8,128)(2,1)}, bf16[3,5120,256]{2,1,0:T(8,128)(2,1)S(1)}, u32[]{:S(2)}, u32[]{:S(2)}) collective-permute-start(bf16[3,5120,256]{2,1,0:T(8,128)(2,1)} %bitcast.23), channel_id=1, source_target_pairs={{0,1},{1,0},{2,3},{3,2},{4,5},{5,4},{6,7},{7,6},{8,9},{9,8},{10,11... | collective-permute-start | bytes 23592968 | tf_op jit(solution)/shard_map/ppermute | solution.py:25
  2.7 11.3 %collective-permute-start = (bf16[32,5120]{1,0:T(8,128)(2,1)S(1)}, bf16[32,5120]{1,0:T(8,128)(2,1)S(1)}, u32[]{:S(2)}, u32[]{:S(2)}) collective-permute-start(bf16[32,5120]{1,0:T(8,128)(2,1)S(1)} %get-tuple-element.33.refs_0_), channel_id=1, source_target_pairs={{0,2},{1,3},{2,4},{3,5},{4,6},{5,7},{6,0},{7,1},{8,10},{9,11},{10,... | collective-permute-start | bytes 983048 | tf_op jit(solution)/shard_map/ppermute | solution.py:25
  4.3 12.1 %collective-permute-start.1 = (bf16[32,5120]{1,0:T(8,128)(2,1)S(1)}, bf16[32,5120]{1,0:T(8,128)(2,1)S(1)}, u32[]{:S(2)}, u32[]{:S(2)}) collective-permute-start(bf16[32,5120]{1,0:T(8,128)(2,1)S(1)} %get-tuple-element.33.refs_0_), channel_id=1, source_target_pairs={{0,6},{1,7},{2,0},{3,1},{4,2},{5,3},{6,4},{7,5},{8,14},{9,15},{10,... | collective-permute-start | bytes 983048 | tf_op jit(solution)/shard_map/ppermute | solution.py:25
  6.0 13.4 %collective-permute-start.2 = (bf16[32,5120]{1,0:T(8,128)(2,1)S(1)}, bf16[32,5120]{1,0:T(8,128)(2,1)S(1)}, u32[]{:S(2)}, u32[]{:S(2)}) collective-permute-start(bf16[32,5120]{1,0:T(8,128)(2,1)S(1)} %get-tuple-element.33.refs_0_), channel_id=1, source_target_pairs={{0,8},{1,9},{2,10},{3,11},{4,12},{5,13},{6,14},{7,15},{8,0},{9,1},... | collective-permute-start | bytes 983048 | tf_op jit(solution)/shard_map/ppermute | solution.py:25
  14.0 12.1 %collective-permute-start.9 = (bf16[32,5120]{1,0:T(8,128)(2,1)S(1)}, bf16[32,5120]{1,0:T(8,128)(2,1)S(1)}, u32[]{:S(2)}, u32[]{:S(2)}) collective-permute-start(bf16[32,5120]{1,0:T(8,128)(2,1)S(1)} %get-tuple-element.33.refs_0_), channel_id=1, source_target_pairs={{0,4},{1,5},{2,6},{3,7},{4,0},{5,1},{6,2},{7,3},{8,12},{9,13},{10,... | collective-permute-start | bytes 983048 | tf_op jit(solution)/shard_map/ppermute | solution.py:25
  15.8 12.2 %collective-permute-start.6 = (bf16[32,5120]{1,0:T(8,128)(2,1)S(1)}, bf16[32,5120]{1,0:T(8,128)(2,1)S(1)}, u32[]{:S(2)}, u32[]{:S(2)}) collective-permute-start(bf16[32,5120]{1,0:T(8,128)(2,1)S(1)} %collective-permute-done.refs_1_), channel_id=1, source_target_pairs={{0,8},{1,9},{2,10},{3,11},{4,12},{5,13},{6,14},{7,15},{8,0},{9,1},... | collective-permute-start | bytes 983048 | tf_op jit(solution)/shard_map/ppermute | solution.py:25
  16.4 17.0 %collective-permute-start.7 = (bf16[32,5120]{1,0:T(8,128)(2,1)S(1)}, bf16[32,5120]{1,0:T(8,128)(2,1)S(1)}, u32[]{:S(2)}, u32[]{:S(2)}) collective-permute-start(bf16[32,5120]{1,0:T(8,128)(2,1)S(1)} %collective-permute-done.1.refs_2_), channel_id=1, source_target_pairs={{0,8},{1,9},{2,10},{3,11},{4,12},{5,13},{6,14},{7,15},{8,0},{9,1},... | collective-permute-start | bytes 983048 | tf_op jit(solution)/shard_map/ppermute | solution.py:25
  19.4 14.0 %collective-permute-start.8 = (bf16[32,5120]{1,0:T(8,128)(2,1)S(1)}, bf16[32,5120]{1,0:T(8,128)(2,1)S(1)}, u32[]{:S(2)}, u32[]{:S(2)}) collective-permute-start(bf16[32,5120]{1,0:T(8,128)(2,1)S(1)} %collective-permute-done.2.refs_3_), channel_id=1, source_target_pairs={{0,4},{1,5},{2,6},{3,7},{4,0},{5,1},{6,2},{7,3},{8,12},{9,13},{10,... | collective-permute-start | bytes 983048 | tf_op jit(solution)/shard_map/ppermute | solution.py:25
  21.1 16.2 %collective-permute-start.12 = (bf16[256,5120]{1,0:T(8,128)(2,1)}, bf16[256,5120]{1,0:T(8,128)(2,1)S(1)}, u32[]{:S(2)}, u32[]{:S(2)}) collective-permute-start(bf16[256,5120]{1,0:T(8,128)(2,1)} %w_mine.3), channel_id=1, source_target_pairs={{0,1},{1,0},{2,3},{3,2},{4,5},{5,4},{6,7},{7,6},{8,9},{9,8},{10,11... | collective-permute-start | bytes 7864328 | tf_op jit(solution)/shard_map/ppermute | solution.py:25
  26.2 9.6 %collective-permute-start.10 = (bf16[4,128,256]{2,1,0:T(8,128)(2,1)S(1)}, bf16[4,128,256]{2,1,0:T(8,128)(2,1)S(1)}, u32[]{:S(2)}, u32[]{:S(2)}) collective-permute-start(bf16[4,128,256]{2,1,0:T(8,128)(2,1)S(1)} %get-tuple-element.36.kv_a), channel_id=1, source_target_pairs={{0,1},{1,0},{2,3},{3,2},{4,5},{5,4},{6,7},{7,6},{8,9},{9,8},{10,11... | collective-permute-start | bytes 786440 | tf_op jit(solution)/shard_map/ppermute | solution.py:25
  33.4 4.0 %copy-start = (bf16[256,5120]{1,0:T(8,128)(2,1)S(1)}, bf16[256,5120]{1,0:T(8,128)(2,1)}, u32[]{:S(2)}) copy-start(bf16[256,5120]{1,0:T(8,128)(2,1)} %w_mine.3) | copy-start | bytes 7864324
  35.7 1.6 %collective-permute-start.11 = (bf16[4,128,256]{2,1,0:T(8,128)(2,1)S(1)}, bf16[4,128,256]{2,1,0:T(8,128)(2,1)S(1)}, u32[]{:S(2)}, u32[]{:S(2)}) collective-permute-start(bf16[4,128,256]{2,1,0:T(8,128)(2,1)S(1)} %get-tuple-element.37.kv_b), channel_id=1, source_target_pairs={{0,1},{1,0},{2,3},{3,2},{4,5},{5,4},{6,7},{7,6},{8,9},{9,8},{10,11... | collective-permute-start | bytes 786440 | tf_op jit(solution)/shard_map/ppermute | solution.py:25
  39.7 29.5 %copy-start.1 = (bf16[1,4,8,5120]{3,2,1,0:T(8,128)(2,1)S(1)}, bf16[1,4,8,5120]{3,2,1,0:T(8,128)(2,1)}, u32[]{:S(2)}) copy-start(bf16[1,4,8,5120]{3,2,1,0:T(8,128)(2,1)} %param.9) | copy-start | bytes 983044
  39.7 36.4 %copy-start.2 = (bf16[8,5120]{1,0:T(8,128)(2,1)S(1)}, bf16[8,5120]{1,0:T(8,128)(2,1)}, u32[]{:S(2)}) copy-start(bf16[8,5120]{1,0:T(8,128)(2,1)} %param.12) | copy-start | bytes 245764
  39.7 12.1 %collective-permute-start.13 = (bf16[32,5120]{1,0:T(8,128)(2,1)S(1)}, bf16[32,5120]{1,0:T(8,128)(2,1)S(1)}, u32[]{:S(2)}, u32[]{:S(2)}) collective-permute-start(bf16[32,5120]{1,0:T(8,128)(2,1)S(1)} %get-tuple-element.42), channel_id=1, source_target_pairs={{0,8},{1,9},{2,10},{3,11},{4,12},{5,13},{6,14},{7,15},{8,0},{9,1},... | collective-permute-start | bytes 983048 | tf_op jit(solution)/shard_map/ppermute | solution.py:25
  40.3 11.6 %collective-permute-start.14 = (bf16[16,5120]{1,0:T(8,128)(2,1)S(1)}, bf16[16,5120]{1,0:T(8,128)(2,1)S(1)}, u32[]{:S(2)}, u32[]{:S(2)}) collective-permute-start(bf16[16,5120]{1,0:T(8,128)(2,1)S(1)} %get-tuple-element.43), channel_id=1, source_target_pairs={{0,6},{1,7},{2,0},{3,1},{4,2},{5,3},{6,4},{7,5},{8,14},{9,15},{10,... | collective-permute-start | bytes 491528 | tf_op jit(solution)/shard_map/ppermute | solution.py:25
  41.5 16.6 %collective-permute-start.16 = (bf16[32,5120]{1,0:T(8,128)(2,1)S(1)}, bf16[32,5120]{1,0:T(8,128)(2,1)S(1)}, u32[]{:S(2)}, u32[]{:S(2)}) collective-permute-start(bf16[32,5120]{1,0:T(8,128)(2,1)S(1)} %get-tuple-element.45), channel_id=1, source_target_pairs={{0,8},{1,9},{2,10},{3,11},{4,12},{5,13},{6,14},{7,15},{8,0},{9,1},... | collective-permute-start | bytes 983048 | tf_op jit(solution)/shard_map/ppermute | solution.py:25
  44.5 13.7 %collective-permute-start.17 = (bf16[16,5120]{1,0:T(8,128)(2,1)S(1)}, bf16[16,5120]{1,0:T(8,128)(2,1)S(1)}, u32[]{:S(2)}, u32[]{:S(2)}) collective-permute-start(bf16[16,5120]{1,0:T(8,128)(2,1)S(1)} %get-tuple-element.46), channel_id=1, source_target_pairs={{0,2},{1,3},{2,4},{3,5},{4,6},{5,7},{6,0},{7,1},{8,10},{9,11},{10,... | collective-permute-start | bytes 491528 | tf_op jit(solution)/shard_map/ppermute | solution.py:25
  45.3 13.6 %collective-permute-start.19 = (bf16[32,5120]{1,0:T(8,128)(2,1)S(1)}, bf16[32,5120]{1,0:T(8,128)(2,1)S(1)}, u32[]{:S(2)}, u32[]{:S(2)}) collective-permute-start(bf16[32,5120]{1,0:T(8,128)(2,1)S(1)} %get-tuple-element.48), channel_id=1, source_target_pairs={{0,4},{1,5},{2,6},{3,7},{4,0},{5,1},{6,2},{7,3},{8,12},{9,13},{10,... | collective-permute-start | bytes 983048 | tf_op jit(solution)/shard_map/ppermute | solution.py:25
  52.0 10.2 %collective-permute-start.15 = (bf16[32,5120]{1,0:T(8,128)(2,1)S(1)}, bf16[32,5120]{1,0:T(8,128)(2,1)S(1)}, u32[]{:S(2)}, u32[]{:S(2)}) collective-permute-start(bf16[32,5120]{1,0:T(8,128)(2,1)S(1)} %pad_maximum_fusion), channel_id=1, source_target_pairs={{0,6},{1,7},{2,0},{3,1},{4,2},{5,3},{6,4},{7,5},{8,14},{9,15},{10,... | collective-permute-start | bytes 983048 | tf_op jit(solution)/shard_map/ppermute | solution.py:25
  58.2 10.2 %collective-permute-start.18 = (bf16[32,5120]{1,0:T(8,128)(2,1)S(1)}, bf16[32,5120]{1,0:T(8,128)(2,1)S(1)}, u32[]{:S(2)}, u32[]{:S(2)}) collective-permute-start(bf16[32,5120]{1,0:T(8,128)(2,1)S(1)} %pad_maximum_fusion.1), channel_id=1, source_target_pairs={{0,2},{1,3},{2,4},{3,5},{4,6},{5,7},{6,0},{7,1},{8,10},{9,11},{10,... | collective-permute-start | bytes 983048 | tf_op jit(solution)/shard_map/ppermute | solution.py:25
  59.0 10.2 %collective-permute-start.20 = (bf16[32,5120]{1,0:T(8,128)(2,1)S(1)}, bf16[32,5120]{1,0:T(8,128)(2,1)S(1)}, u32[]{:S(2)}, u32[]{:S(2)}) collective-permute-start(bf16[32,5120]{1,0:T(8,128)(2,1)S(1)} %add_convert_fusion.1), channel_id=1, source_target_pairs={{0,8},{1,9},{2,10},{3,11},{4,12},{5,13},{6,14},{7,15},{8,0},{9,1},... | collective-permute-start | bytes 983048 | tf_op jit(solution)/shard_map/ppermute | solution.py:25
  69.5 6.6 %collective-permute-start.21 = (bf16[8,5120]{1,0:T(8,128)(2,1)S(1)}, bf16[8,5120]{1,0:T(8,128)(2,1)S(1)}, u32[]{:S(2)}, u32[]{:S(2)}) collective-permute-start(bf16[8,5120]{1,0:T(8,128)(2,1)S(1)} %dynamic-slice_bitcast_fusion), channel_id=1, source_target_pairs={{0,16},{16,32},{32,48},{48,64},{64,80},{80,96},{96,112},{112,0},{1... | collective-permute-start | bytes 245768 | tf_op jit(solution)/shard_map/ppermute | solution.py:31

commit v7 on v6

--- a/solution.py
+++ b/solution.py
@@ -119,12 +119,18 @@
         project(i, rows_ref, (held, w_other), gains, q_ref, kv_ref)
 
 
-def rest_kernel(pieces, *refs):
+def rest_keys_kernel(pieces, *refs):
     xs, gains = refs[:pieces], refs[pieces : pieces + 3]
-    held, w_other, q_ref, kv_ref, rows_ref = refs[pieces + 3 :]
+    held, w_other, kv_ref, rows_ref = refs[pieces + 3 :]
     gather_rows(xs, rows_ref)
-    for i in range(6):
-        project(i, rows_ref, (held, w_other), gains, q_ref, kv_ref)
+    for i in (1, 2, 4, 5):
+        project(i, rows_ref, (held, w_other), gains, None, kv_ref)
+
+
+def rest_queries_kernel(rows_ref, *refs):
+    gains, (held, w_other, q_ref) = refs[:3], refs[3:]
+    for i in (0, 3):
+        project(i, rows_ref, (held, w_other), gains, q_ref, None)
 
 
 def qkv_shapes(total, cols):
@@ -160,22 +166,29 @@
     pieces = len(xs)
     width = xs[0].shape[1]
     total, cols = sum(x.shape[0] for x in xs), held.shape[2]
-    return pl.pallas_call(
-        functools.partial(rest_kernel, pieces),
+    in_vmem = lambda array: pltpu.with_memory_space_constraint(array, pltpu.VMEM)
+    params = pltpu.CompilerParams(vmem_limit_bytes=24 * MIB)
+    cost = lambda count: pl.CostEstimate(
+        flops=2 * count * total * width * cols, bytes_accessed=2 * count * width * cols, transcendentals=0
+    )
+    q_shape, kv_shape = qkv_shapes(total, cols)
+    kv, rows = pl.pallas_call(
+        functools.partial(rest_keys_kernel, pieces),
         in_specs=[VMEM] * (pieces + 5),
         out_specs=[VMEM] * 2,
-        out_shape=qkv_shapes(total, cols),
-        scratch_shapes=[pltpu.VMEM((total, width), jnp.bfloat16)],
-        compiler_params=pltpu.CompilerParams(vmem_limit_bytes=24 * MIB),
-        cost_estimate=pl.CostEstimate(
-            flops=12 * total * width * cols, bytes_accessed=12 * width * cols, transcendentals=0
-        ),
-    )(
-        *xs,
-        *gains,
-        pltpu.with_memory_space_constraint(held, pltpu.VMEM),
-        pltpu.with_memory_space_constraint(w_other, pltpu.VMEM),
-    )
+        out_shape=[kv_shape, jax.ShapeDtypeStruct((total, width), jnp.bfloat16)],
+        compiler_params=params,
+        cost_estimate=cost(4),
+    )(*xs, *gains, in_vmem(held), in_vmem(w_other))
+    q = pl.pallas_call(
+        rest_queries_kernel,
+        in_specs=[VMEM] * 6,
+        out_specs=VMEM,
+        out_shape=q_shape,
+        compiler_params=params,
+        cost_estimate=cost(2),
+    )(in_vmem(rows), *gains, in_vmem(held), in_vmem(w_other))
+    return q, kv
 
 
 def attend(q_ref, kv_ref, attn_ref):
@@ -309,8 +322,7 @@
     handed = lax.dynamic_slice_in_dim(updated, leaving[0], 1, axis=0)[0]
     arriving = from_behind(handed, "queue", 1)
     first = jnp.where(lax.axis_index("queue") == 0, fresh, arriving)
-    select = jnp.arange(frames) == leaving[0]
-    return jnp.where(select[:, None, None], first[None], updated)[None]
+    return lax.dynamic_update_slice_in_dim(updated, first[None], leaving[0], axis=0)[None]
 
 
 def solution(mesh):

time: 77.8 us -> 77.2 us (level)
  waiting for transfers between devices: 38 us -> 37 us
    ppermute x21, waiting for transfers between devices: 33 us -> 32 us  [hop(): return lax.ppermute(value, 'seq', pairs)]
    select_n x2 -> x0, other arithmetic: 0.83 us -> none  [the longest x1 0.82 us: body(): return jnp.where(select[:, None, None], first[None], updated)[None]]
    pallas_call x1 -> x2, Pallas kernels: 2.33 us -> 2.58 us  [the longest x1 1.61 us: rest_call(): pl.pallas_call(functools.partial(rest_keys_kernel, pieces), in_specs=[VME...]
  transfers between devices with their start and end apart: 22 -> 22, of which waited for: 11 -> 11; matrix products, arithmetic and copies ran while one was open for 0% -> 1% of each run, Pallas kernels for 14% -> 14%
where the time goes in v7:
time: 77.2 us; the launch traced here: 76.3 us
  waiting for transfers between devices  37 us (48%)
  starting transfers between devices  23.1 us (30%)
  Pallas kernels  13.1 us (17%)
  between operations  1.75 us (2%)
  other arithmetic  1.26 us (2%)
    ppermute x21, waiting for transfers between devices, hop(): return lax.ppermute(value, 'seq', pairs)  32 us
    ppermute x21, starting transfers between devices, hop(): return lax.ppermute(value, 'seq', pairs)  21.4 us
    ppermute x1, waiting for transfers between devices, from_behind(): return lax.ppermute(x, axis, pairs)  4.97 us
    pallas_call x2, Pallas kernels, attend_call(): pl.pallas_call(functools.partial(kernel, len(sizes)), in_specs=[VMEM] * (...  4.69 us
    pallas_call x1, Pallas kernels, first_call(): pl.pallas_call(functools.partial(first_kernel, pieces), in_specs=[VMEM] *...  4.43 us
    ppermute x1, starting transfers between devices, from_behind(): return lax.ppermute(x, axis, pairs)  1.65 us
    pallas_call x1, Pallas kernels, rest_call(): pl.pallas_call(functools.partial(rest_keys_kernel, pieces), in_specs=[VME...  1.61 us
  transfers between devices with their start and end apart: 22, of which 11 were waited for; matrix products, arithmetic and copies ran while one was open for 1% of the time, Pallas kernels for 14%

profile of v7, /device:TPU:96, one launch (start us, length us, event | category | flops | bytes accessed | tf_op | source)
XLA Modules:
  0.0 76.3 jit_solution(11136118212108779376)
XLA Ops:
  0.0 0.0 copy-start
  0.0 0.0 collective-permute-start.3
  0.0 0.5 collective-permute-start.4
  1.4 1.4 %shard_map.91 = (bf16[32,5120]{1,0:T(8,128)(2,1)S(1)}, f32[1,5120]{1,0:T(1,128)S(1)}, f32[2,256]{1,0:T(2,128)S(1)}) custom-call(s32[1]{0:T(128)S(6)} %copy.11.step, bf16[32,5120]{1,0:T(8,128)(2,1)} %bitcast.17, f32[50,15360]{1,0:T(8,128)} %table.1, f32[1,256]{1,0:T(1,128)} %bitcast.21, f32[1,256]{1,0:T(1,128)} %bitcast.23), custom_call_target="tpu_custom_call" | custom-call | flops 1638400 | bytes 655360 | tf_op jit(solution)/shard_map/pallas_call | solution.py:59
  2.8 0.0 collective-permute-done.3.refs_5_.refs_1_
  2.8 0.0 collective-permute-done.4.refs_6_.refs_2_
  2.9 0.1 collective-permute-start.5
  2.9 1.6 %collective-permute-start = (bf16[32,5120]{1,0:T(8,128)(2,1)S(1)}, bf16[32,5120]{1,0:T(8,128)(2,1)S(1)}, u32[]{:S(2)}, u32[]{:S(2)}) collective-permute-start(bf16[32,5120]{1,0:T(8,128)(2,1)S(1)} %get-tuple-element.33.refs_0_), channel_id=1, source_target_pairs={{0,2},{1,3},{2,4},{3,5},{4,6},{5,7},{6,0},{7,1},{8,10},{9,11},{10,... | collective-permute-start | bytes 983048 | tf_op jit(solution)/shard_map/ppermute | solution.py:25
  4.5 1.7 %collective-permute-start.1 = (bf16[32,5120]{1,0:T(8,128)(2,1)S(1)}, bf16[32,5120]{1,0:T(8,128)(2,1)S(1)}, u32[]{:S(2)}, u32[]{:S(2)}) collective-permute-start(bf16[32,5120]{1,0:T(8,128)(2,1)S(1)} %get-tuple-element.33.refs_0_), channel_id=1, source_target_pairs={{0,6},{1,7},{2,0},{3,1},{4,2},{5,3},{6,4},{7,5},{8,14},{9,15},{10,... | collective-permute-start | bytes 983048 | tf_op jit(solution)/shard_map/ppermute | solution.py:25
  6.3 0.6 collective-permute-start.2
  6.8 7.5 %collective-permute-done.refs_1_ = bf16[32,5120]{1,0:T(8,128)(2,1)S(1)} collective-permute-done((bf16[32,5120]{1,0:T(8,128)(2,1)S(1)}, bf16[32,5120]{1,0:T(8,128)(2,1)S(1)}, u32[]{:S(2)}, u32[]{:S(2)}) %collective-permute-start) | collective-permute-done | bytes 327712 | tf_op jit(solution)/shard_map/ppermute | solution.py:25
  14.3 1.8 %collective-permute-start.9 = (bf16[32,5120]{1,0:T(8,128)(2,1)S(1)}, bf16[32,5120]{1,0:T(8,128)(2,1)S(1)}, u32[]{:S(2)}, u32[]{:S(2)}) collective-permute-start(bf16[32,5120]{1,0:T(8,128)(2,1)S(1)} %get-tuple-element.33.refs_0_), channel_id=1, source_target_pairs={{0,4},{1,5},{2,6},{3,7},{4,0},{5,1},{6,2},{7,3},{8,12},{9,13},{10,... | collective-permute-start | bytes 983048 | tf_op jit(solution)/shard_map/ppermute | solution.py:25
  16.1 0.6 collective-permute-start.6
  16.7 0.0 collective-permute-done.1.refs_2_
  16.7 3.0 %collective-permute-start.7 = (bf16[32,5120]{1,0:T(8,128)(2,1)S(1)}, bf16[32,5120]{1,0:T(8,128)(2,1)S(1)}, u32[]{:S(2)}, u32[]{:S(2)}) collective-permute-start(bf16[32,5120]{1,0:T(8,128)(2,1)S(1)} %collective-permute-done.1.refs_2_), channel_id=1, source_target_pairs={{0,8},{1,9},{2,10},{3,11},{4,12},{5,13},{6,14},{7,15},{8,0},{9,1},... | collective-permute-start | bytes 983048 | tf_op jit(solution)/shard_map/ppermute | solution.py:25
  19.6 0.0 collective-permute-done.2.refs_3_
  19.6 0.0 collective-permute-done.5.refs_8_.refs_4_
  19.6 1.7 %collective-permute-start.8 = (bf16[32,5120]{1,0:T(8,128)(2,1)S(1)}, bf16[32,5120]{1,0:T(8,128)(2,1)S(1)}, u32[]{:S(2)}, u32[]{:S(2)}) collective-permute-start(bf16[32,5120]{1,0:T(8,128)(2,1)S(1)} %collective-permute-done.2.refs_3_), channel_id=1, source_target_pairs={{0,4},{1,5},{2,6},{3,7},{4,0},{5,1},{6,2},{7,3},{8,12},{9,13},{10,... | collective-permute-start | bytes 983048 | tf_op jit(solution)/shard_map/ppermute | solution.py:25
  21.4 0.0 copy-done
  21.4 0.0 collective-permute-start.12
  21.4 4.4 %shard_map.92 = (bf16[2,128,256]{2,1,0:T(8,128)(2,1)S(1)}, bf16[4,128,256]{2,1,0:T(8,128)(2,1)S(1)}, bf16[3,5120,256]{2,1,0:T(8,128)(2,1)S(1)}) custom-call(bf16[32,5120]{1,0:T(8,128)(2,1)S(1)} %get-tuple-element.33.refs_0_, bf16[32,5120]{1,0:T(8,128)(2,1)S(1)} %collective-permute-done.refs_1_, bf16[32,5120]{1,0:T(8,128)(2,1)S(1)} %collective-permute-done.1.refs_2_, ...), custom_call_target="tpu_custom_call" | custom-call | flops 80530636800 | bytes 15728640 | tf_op jit(solution)/shard_map/pallas_call | solution.py:147
  25.8 0.6 collective-permute-done.9.refs_3_
  26.4 0.0 collective-permute-start.10
  26.4 1.8 %collective-permute-done.6.refs_0_ = bf16[32,5120]{1,0:T(8,128)(2,1)S(1)} collective-permute-done((bf16[32,5120]{1,0:T(8,128)(2,1)S(1)}, bf16[32,5120]{1,0:T(8,128)(2,1)S(1)}, u32[]{:S(2)}, u32[]{:S(2)}) %collective-permute-start.6) | collective-permute-done | bytes 327712 | tf_op jit(solution)/shard_map/ppermute | solution.py:25
  28.3 5.4 %collective-permute-done.7.refs_1_ = bf16[32,5120]{1,0:T(8,128)(2,1)S(1)} collective-permute-done((bf16[32,5120]{1,0:T(8,128)(2,1)S(1)}, bf16[32,5120]{1,0:T(8,128)(2,1)S(1)}, u32[]{:S(2)}, u32[]{:S(2)}) %collective-permute-start.7) | collective-permute-done | bytes 327712 | tf_op jit(solution)/shard_map/ppermute | solution.py:25
  33.6 0.0 collective-permute-done.8.refs_2_
  33.6 1.6 %shard_map.93 = (bf16[4,128,256]{2,1,0:T(8,128)(2,1)S(1)}, bf16[128,5120]{1,0:T(8,128)(2,1)S(1)}) custom-call(bf16[32,5120]{1,0:T(8,128)(2,1)S(1)} %collective-permute-done.6.refs_0_, bf16[32,5120]{1,0:T(8,128)(2,1)S(1)} %collective-permute-done.7.refs_1_, bf16[32,5120]{1,0:T(8,128)(2,1)S(1)} %collective-permute-done.8.refs_2_, ...), custom_call_target="tpu_custom_call" | custom-call | flops 1342177280 | bytes 10485760 | tf_op jit(solution)/shard_map/pallas_call | solution.py:175
  35.2 0.1 collective-permute-start.11
  35.3 1.0 %shard_map.94.q_b = bf16[2,128,256]{2,1,0:T(8,128)(2,1)S(1)} custom-call(bf16[128,5120]{1,0:T(8,128)(2,1)S(1)} %get-tuple-element.35.rows_ref, f32[2,256]{1,0:T(2,128)S(1)} %get-tuple-element.29.refs_4_.refs_0_, f32[1,256]{1,0:T(1,128)S(1)} %collective-permute-done.3.refs_5_.refs_1_, f32[1,256]{1,0:T(1,128)S(1)} %collective-permute-done.4.refs_6_.refs_2_, ...), custom_call_target="tpu_custom_call" | custom-call | flops 671088640 | bytes 5242880 | tf_op jit(solution)/shard_map/pallas_call | solution.py:183
  36.3 0.0 collective-permute-done.10.far_a
  36.3 0.5 collective-permute-done.11.far_b
  36.8 0.0 collective-permute-done.12.w_other
  36.8 2.4 %shard_map.95 = (bf16[32,5120]{1,0:T(8,128)(2,1)S(1)}, bf16[32,5120]{1,0:T(8,128)(2,1)S(1)}, bf16[32,5120]{1,0:T(8,128)(2,1)S(1)}, bf16[16,5120]{1,0:T(8,128)(2,...) custom-call(bf16[2,128,256]{2,1,0:T(8,128)(2,1)S(1)} %shard_map.94.q_b, ...), custom_call_target="tpu_custom_call" | custom-call | flops 805306368 | bytes 5242880 | tf_op jit(solution)/shard_map/pallas_call | solution.py:253
  39.2 0.6 collective-permute-start.13
  39.8 1.1 %collective-permute-start.14 = (bf16[16,5120]{1,0:T(8,128)(2,1)S(1)}, bf16[16,5120]{1,0:T(8,128)(2,1)S(1)}, u32[]{:S(2)}, u32[]{:S(2)}) collective-permute-start(bf16[16,5120]{1,0:T(8,128)(2,1)S(1)} %get-tuple-element.43), channel_id=1, source_target_pairs={{0,6},{1,7},{2,0},{3,1},{4,2},{5,3},{6,4},{7,5},{8,14},{9,15},{10,... | collective-permute-start | bytes 491528 | tf_op jit(solution)/shard_map/ppermute | solution.py:25
  41.0 3.0 %collective-permute-start.16 = (bf16[32,5120]{1,0:T(8,128)(2,1)S(1)}, bf16[32,5120]{1,0:T(8,128)(2,1)S(1)}, u32[]{:S(2)}, u32[]{:S(2)}) collective-permute-start(bf16[32,5120]{1,0:T(8,128)(2,1)S(1)} %get-tuple-element.45), channel_id=1, source_target_pairs={{0,8},{1,9},{2,10},{3,11},{4,12},{5,13},{6,14},{7,15},{8,0},{9,1},... | collective-permute-start | bytes 983048 | tf_op jit(solution)/shard_map/ppermute | solution.py:25
  44.0 0.9 %collective-permute-start.17 = (bf16[16,5120]{1,0:T(8,128)(2,1)S(1)}, bf16[16,5120]{1,0:T(8,128)(2,1)S(1)}, u32[]{:S(2)}, u32[]{:S(2)}) collective-permute-start(bf16[16,5120]{1,0:T(8,128)(2,1)S(1)} %get-tuple-element.46), channel_id=1, source_target_pairs={{0,2},{1,3},{2,4},{3,5},{4,6},{5,7},{6,0},{7,1},{8,10},{9,11},{10,... | collective-permute-start | bytes 491528 | tf_op jit(solution)/shard_map/ppermute | solution.py:25
  44.8 1.7 %collective-permute-start.19 = (bf16[32,5120]{1,0:T(8,128)(2,1)S(1)}, bf16[32,5120]{1,0:T(8,128)(2,1)S(1)}, u32[]{:S(2)}, u32[]{:S(2)}) collective-permute-start(bf16[32,5120]{1,0:T(8,128)(2,1)S(1)} %get-tuple-element.48), channel_id=1, source_target_pairs={{0,4},{1,5},{2,6},{3,7},{4,0},{5,1},{6,2},{7,3},{8,12},{9,13},{10,... | collective-permute-start | bytes 983048 | tf_op jit(solution)/shard_map/ppermute | solution.py:25
  46.6 2.3 %shard_map.96 = (bf16[32,5120]{1,0:T(8,128)(2,1)S(1)}, bf16[32,5120]{1,0:T(8,128)(2,1)S(1)}, bf16[32,5120]{1,0:T(8,128)(2,1)S(1)}, bf16[32,5120]{1,0:T(8,128)(2,1)S(1)}) custom-call(bf16[2,128,256]{2,1,0:T(8,128)(2,1)S(1)} %get-tuple-element.31.q_ref, bf16[4,512,256]{2,1,0:T(8,128)(2,1)S(1)} %get-tuple-element.39.kv_ref, bf16[256,5120]{1,0:T(8,128)(2,1)S(1)} %copy-done, ...), custom_call_target="tpu_custom_call" | custom-call | flops 805306368 | bytes 5242880 | tf_op jit(solution)/shard_map/pallas_call | solution.py:253
  48.9 2.4 %collective-permute-done.13 = bf16[32,5120]{1,0:T(8,128)(2,1)S(1)} collective-permute-done((bf16[32,5120]{1,0:T(8,128)(2,1)S(1)}, bf16[32,5120]{1,0:T(8,128)(2,1)S(1)}, u32[]{:S(2)}, u32[]{:S(2)}) %collective-permute-start.13) | collective-permute-done | bytes 327712 | tf_op jit(solution)/shard_map/ppermute | solution.py:25
  51.3 0.0 copy-start.1
  51.4 0.1 convert_add_fusion.1
  51.4 0.0 collective-permute-done.14
  51.5 0.0 copy-start.3
  51.5 1.2 %collective-permute-start.15 = (bf16[32,5120]{1,0:T(8,128)(2,1)S(1)}, bf16[32,5120]{1,0:T(8,128)(2,1)S(1)}, u32[]{:S(2)}, u32[]{:S(2)}) collective-permute-start(bf16[32,5120]{1,0:T(8,128)(2,1)S(1)} %pad_maximum_fusion), channel_id=1, source_target_pairs={{0,6},{1,7},{2,0},{3,1},{4,2},{5,3},{6,4},{7,5},{8,14},{9,15},{10,... | collective-permute-start | bytes 983048 | tf_op jit(solution)/shard_map/ppermute | solution.py:25
  52.8 4.8 %collective-permute-done.16 = bf16[32,5120]{1,0:T(8,128)(2,1)S(1)} collective-permute-done((bf16[32,5120]{1,0:T(8,128)(2,1)S(1)}, bf16[32,5120]{1,0:T(8,128)(2,1)S(1)}, u32[]{:S(2)}, u32[]{:S(2)}) %collective-permute-start.16) | collective-permute-done | bytes 327712 | tf_op jit(solution)/shard_map/ppermute | solution.py:25
  57.6 0.1 convert_add_fusion
  57.7 0.0 collective-permute-done.17
  57.8 0.7 collective-permute-start.18
  58.4 0.0 collective-permute-done.19
  58.4 0.1 add_convert_fusion.1
  58.5 0.6 collective-permute-start.20
  59.8 1.9 %collective-permute-done.15 = bf16[32,5120]{1,0:T(8,128)(2,1)S(1)} collective-permute-done((bf16[32,5120]{1,0:T(8,128)(2,1)S(1)}, bf16[32,5120]{1,0:T(8,128)(2,1)S(1)}, u32[]{:S(2)}, u32[]{:S(2)}) %collective-permute-start.15) | collective-permute-done | bytes 327712 | tf_op jit(solution)/shard_map/ppermute | solution.py:25
  61.7 6.3 %collective-permute-done.18 = bf16[32,5120]{1,0:T(8,128)(2,1)S(1)} collective-permute-done((bf16[32,5120]{1,0:T(8,128)(2,1)S(1)}, bf16[32,5120]{1,0:T(8,128)(2,1)S(1)}, u32[]{:S(2)}, u32[]{:S(2)}) %collective-permute-start.18) | collective-permute-done | bytes 327712 | tf_op jit(solution)/shard_map/ppermute | solution.py:25
  68.0 0.8 %collective-permute-done.20 = bf16[32,5120]{1,0:T(8,128)(2,1)S(1)} collective-permute-done((bf16[32,5120]{1,0:T(8,128)(2,1)S(1)}, bf16[32,5120]{1,0:T(8,128)(2,1)S(1)}, u32[]{:S(2)}, u32[]{:S(2)}) %collective-permute-start.20) | collective-permute-done | bytes 327712 | tf_op jit(solution)/shard_map/ppermute | solution.py:25
  68.7 0.0 copy-done.1
  68.7 0.2 add_convert_fusion
  69.0 0.0 copy-start.2
  69.0 1.6 %collective-permute-start.21 = (bf16[8,5120]{1,0:T(8,128)(2,1)S(1)}, bf16[8,5120]{1,0:T(8,128)(2,1)S(1)}, u32[]{:S(2)}, u32[]{:S(2)}) collective-permute-start(bf16[8,5120]{1,0:T(8,128)(2,1)S(1)} %dynamic-slice_bitcast_fusion), channel_id=1, source_target_pairs={{0,16},{16,32},{32,48},{48,64},{64,80},{80,96},{96,112},{112,0},{1... | collective-permute-start | bytes 245768 | tf_op jit(solution)/shard_map/ppermute | solution.py:31
  70.7 5.0 %collective-permute-done.21 = bf16[8,5120]{1,0:T(8,128)(2,1)S(1)} collective-permute-done((bf16[8,5120]{1,0:T(8,128)(2,1)S(1)}, bf16[8,5120]{1,0:T(8,128)(2,1)S(1)}, u32[]{:S(2)}, u32[]{:S(2)}) %collective-permute-start.21) | collective-permute-done | bytes 81952 | tf_op jit(solution)/shard_map/ppermute | solution.py:31
  75.6 0.0 copy-done.2
  75.6 0.0 copy-done.3
  75.6 0.7 bitcast_dynamic-update-slice_fusion
  (7 shorter events, 0.2 us)
Async XLA Ops:
  0.0 21.4 %copy-start = (bf16[256,5120]{1,0:T(8,128)(2,1)S(1)}, bf16[256,5120]{1,0:T(8,128)(2,1)}, u32[]{:S(2)}) copy-start(bf16[256,5120]{1,0:T(8,128)(2,1)} %w_mine.3) | copy-start | bytes 7864324
  0.0 2.8 %collective-permute-start.3 = (f32[1,256]{1,0:T(1,128)}, f32[1,256]{1,0:T(1,128)S(1)}, u32[]{:S(2)}, u32[]{:S(2)}) collective-permute-start(f32[1,256]{1,0:T(1,128)} %bitcast.20), channel_id=1, source_target_pairs={{0,1},{1,0},{2,3},{3,2},{4,5},{5,4},{6,7},{7,6},{8,9},{9,8},{10,11... | collective-permute-start | bytes 3080 | tf_op jit(solution)/shard_map/ppermute | solution.py:25
  0.0 2.8 %collective-permute-start.4 = (f32[1,256]{1,0:T(1,128)}, f32[1,256]{1,0:T(1,128)S(1)}, u32[]{:S(2)}, u32[]{:S(2)}) collective-permute-start(f32[1,256]{1,0:T(1,128)} %bitcast.22), channel_id=1, source_target_pairs={{0,1},{1,0},{2,3},{3,2},{4,5},{5,4},{6,7},{7,6},{8,9},{9,8},{10,11... | collective-permute-start | bytes 3080 | tf_op jit(solution)/shard_map/ppermute | solution.py:25
  2.9 16.8 %collective-permute-start.5 = (bf16[3,5120,256]{2,1,0:T(8,128)(2,1)}, bf16[3,5120,256]{2,1,0:T(8,128)(2,1)S(1)}, u32[]{:S(2)}, u32[]{:S(2)}) collective-permute-start(bf16[3,5120,256]{2,1,0:T(8,128)(2,1)} %bitcast.24), channel_id=1, source_target_pairs={{0,1},{1,0},{2,3},{3,2},{4,5},{5,4},{6,7},{7,6},{8,9},{9,8},{10,11... | collective-permute-start | bytes 23592968 | tf_op jit(solution)/shard_map/ppermute | solution.py:25
  2.9 11.3 %collective-permute-start = (bf16[32,5120]{1,0:T(8,128)(2,1)S(1)}, bf16[32,5120]{1,0:T(8,128)(2,1)S(1)}, u32[]{:S(2)}, u32[]{:S(2)}) collective-permute-start(bf16[32,5120]{1,0:T(8,128)(2,1)S(1)} %get-tuple-element.33.refs_0_), channel_id=1, source_target_pairs={{0,2},{1,3},{2,4},{3,5},{4,6},{5,7},{6,0},{7,1},{8,10},{9,11},{10,... | collective-permute-start | bytes 983048 | tf_op jit(solution)/shard_map/ppermute | solution.py:25
  4.5 12.1 %collective-permute-start.1 = (bf16[32,5120]{1,0:T(8,128)(2,1)S(1)}, bf16[32,5120]{1,0:T(8,128)(2,1)S(1)}, u32[]{:S(2)}, u32[]{:S(2)}) collective-permute-start(bf16[32,5120]{1,0:T(8,128)(2,1)S(1)} %get-tuple-element.33.refs_0_), channel_id=1, source_target_pairs={{0,6},{1,7},{2,0},{3,1},{4,2},{5,3},{6,4},{7,5},{8,14},{9,15},{10,... | collective-permute-start | bytes 983048 | tf_op jit(solution)/shard_map/ppermute | solution.py:25
  6.3 13.4 %collective-permute-start.2 = (bf16[32,5120]{1,0:T(8,128)(2,1)S(1)}, bf16[32,5120]{1,0:T(8,128)(2,1)S(1)}, u32[]{:S(2)}, u32[]{:S(2)}) collective-permute-start(bf16[32,5120]{1,0:T(8,128)(2,1)S(1)} %get-tuple-element.33.refs_0_), channel_id=1, source_target_pairs={{0,8},{1,9},{2,10},{3,11},{4,12},{5,13},{6,14},{7,15},{8,0},{9,1},... | collective-permute-start | bytes 983048 | tf_op jit(solution)/shard_map/ppermute | solution.py:25
  14.3 12.1 %collective-permute-start.9 = (bf16[32,5120]{1,0:T(8,128)(2,1)S(1)}, bf16[32,5120]{1,0:T(8,128)(2,1)S(1)}, u32[]{:S(2)}, u32[]{:S(2)}) collective-permute-start(bf16[32,5120]{1,0:T(8,128)(2,1)S(1)} %get-tuple-element.33.refs_0_), channel_id=1, source_target_pairs={{0,4},{1,5},{2,6},{3,7},{4,0},{5,1},{6,2},{7,3},{8,12},{9,13},{10,... | collective-permute-start | bytes 983048 | tf_op jit(solution)/shard_map/ppermute | solution.py:25
  16.1 12.2 %collective-permute-start.6 = (bf16[32,5120]{1,0:T(8,128)(2,1)S(1)}, bf16[32,5120]{1,0:T(8,128)(2,1)S(1)}, u32[]{:S(2)}, u32[]{:S(2)}) collective-permute-start(bf16[32,5120]{1,0:T(8,128)(2,1)S(1)} %collective-permute-done.refs_1_), channel_id=1, source_target_pairs={{0,8},{1,9},{2,10},{3,11},{4,12},{5,13},{6,14},{7,15},{8,0},{9,1},... | collective-permute-start | bytes 983048 | tf_op jit(solution)/shard_map/ppermute | solution.py:25
  16.7 17.0 %collective-permute-start.7 = (bf16[32,5120]{1,0:T(8,128)(2,1)S(1)}, bf16[32,5120]{1,0:T(8,128)(2,1)S(1)}, u32[]{:S(2)}, u32[]{:S(2)}) collective-permute-start(bf16[32,5120]{1,0:T(8,128)(2,1)S(1)} %collective-permute-done.1.refs_2_), channel_id=1, source_target_pairs={{0,8},{1,9},{2,10},{3,11},{4,12},{5,13},{6,14},{7,15},{8,0},{9,1},... | collective-permute-start | bytes 983048 | tf_op jit(solution)/shard_map/ppermute | solution.py:25
  19.6 14.0 %collective-permute-start.8 = (bf16[32,5120]{1,0:T(8,128)(2,1)S(1)}, bf16[32,5120]{1,0:T(8,128)(2,1)S(1)}, u32[]{:S(2)}, u32[]{:S(2)}) collective-permute-start(bf16[32,5120]{1,0:T(8,128)(2,1)S(1)} %collective-permute-done.2.refs_3_), channel_id=1, source_target_pairs={{0,4},{1,5},{2,6},{3,7},{4,0},{5,1},{6,2},{7,3},{8,12},{9,13},{10,... | collective-permute-start | bytes 983048 | tf_op jit(solution)/shard_map/ppermute | solution.py:25
  21.4 15.5 %collective-permute-start.12 = (bf16[256,5120]{1,0:T(8,128)(2,1)S(1)}, bf16[256,5120]{1,0:T(8,128)(2,1)S(1)}, u32[]{:S(2)}, u32[]{:S(2)}) collective-permute-start(bf16[256,5120]{1,0:T(8,128)(2,1)S(1)} %copy-done), channel_id=1, source_target_pairs={{0,1},{1,0},{2,3},{3,2},{4,5},{5,4},{6,7},{7,6},{8,9},{9,8},{10,11... | collective-permute-start | bytes 7864328 | tf_op jit(solution)/shard_map/ppermute | solution.py:25
  26.4 9.9 %collective-permute-start.10 = (bf16[4,128,256]{2,1,0:T(8,128)(2,1)S(1)}, bf16[4,128,256]{2,1,0:T(8,128)(2,1)S(1)}, u32[]{:S(2)}, u32[]{:S(2)}) collective-permute-start(bf16[4,128,256]{2,1,0:T(8,128)(2,1)S(1)} %get-tuple-element.36.kv_a), channel_id=1, source_target_pairs={{0,1},{1,0},{2,3},{3,2},{4,5},{5,4},{6,7},{7,6},{8,9},{9,8},{10,11... | collective-permute-start | bytes 786440 | tf_op jit(solution)/shard_map/ppermute | solution.py:25
  35.2 1.6 %collective-permute-start.11 = (bf16[4,128,256]{2,1,0:T(8,128)(2,1)S(1)}, bf16[4,128,256]{2,1,0:T(8,128)(2,1)S(1)}, u32[]{:S(2)}, u32[]{:S(2)}) collective-permute-start(bf16[4,128,256]{2,1,0:T(8,128)(2,1)S(1)} %get-tuple-element.37.kv_b), channel_id=1, source_target_pairs={{0,1},{1,0},{2,3},{3,2},{4,5},{5,4},{6,7},{7,6},{8,9},{9,8},{10,11... | collective-permute-start | bytes 786440 | tf_op jit(solution)/shard_map/ppermute | solution.py:25
  39.2 12.1 %collective-permute-start.13 = (bf16[32,5120]{1,0:T(8,128)(2,1)S(1)}, bf16[32,5120]{1,0:T(8,128)(2,1)S(1)}, u32[]{:S(2)}, u32[]{:S(2)}) collective-permute-start(bf16[32,5120]{1,0:T(8,128)(2,1)S(1)} %get-tuple-element.42), channel_id=1, source_target_pairs={{0,8},{1,9},{2,10},{3,11},{4,12},{5,13},{6,14},{7,15},{8,0},{9,1},... | collective-permute-start | bytes 983048 | tf_op jit(solution)/shard_map/ppermute | solution.py:25
  39.8 11.6 %collective-permute-start.14 = (bf16[16,5120]{1,0:T(8,128)(2,1)S(1)}, bf16[16,5120]{1,0:T(8,128)(2,1)S(1)}, u32[]{:S(2)}, u32[]{:S(2)}) collective-permute-start(bf16[16,5120]{1,0:T(8,128)(2,1)S(1)} %get-tuple-element.43), channel_id=1, source_target_pairs={{0,6},{1,7},{2,0},{3,1},{4,2},{5,3},{6,4},{7,5},{8,14},{9,15},{10,... | collective-permute-start | bytes 491528 | tf_op jit(solution)/shard_map/ppermute | solution.py:25
  41.0 16.6 %collective-permute-start.16 = (bf16[32,5120]{1,0:T(8,128)(2,1)S(1)}, bf16[32,5120]{1,0:T(8,128)(2,1)S(1)}, u32[]{:S(2)}, u32[]{:S(2)}) collective-permute-start(bf16[32,5120]{1,0:T(8,128)(2,1)S(1)} %get-tuple-element.45), channel_id=1, source_target_pairs={{0,8},{1,9},{2,10},{3,11},{4,12},{5,13},{6,14},{7,15},{8,0},{9,1},... | collective-permute-start | bytes 983048 | tf_op jit(solution)/shard_map/ppermute | solution.py:25
  44.0 13.7 %collective-permute-start.17 = (bf16[16,5120]{1,0:T(8,128)(2,1)S(1)}, bf16[16,5120]{1,0:T(8,128)(2,1)S(1)}, u32[]{:S(2)}, u32[]{:S(2)}) collective-permute-start(bf16[16,5120]{1,0:T(8,128)(2,1)S(1)} %get-tuple-element.46), channel_id=1, source_target_pairs={{0,2},{1,3},{2,4},{3,5},{4,6},{5,7},{6,0},{7,1},{8,10},{9,11},{10,... | collective-permute-start | bytes 491528 | tf_op jit(solution)/shard_map/ppermute | solution.py:25
  44.8 13.6 %collective-permute-start.19 = (bf16[32,5120]{1,0:T(8,128)(2,1)S(1)}, bf16[32,5120]{1,0:T(8,128)(2,1)S(1)}, u32[]{:S(2)}, u32[]{:S(2)}) collective-permute-start(bf16[32,5120]{1,0:T(8,128)(2,1)S(1)} %get-tuple-element.48), channel_id=1, source_target_pairs={{0,4},{1,5},{2,6},{3,7},{4,0},{5,1},{6,2},{7,3},{8,12},{9,13},{10,... | collective-permute-start | bytes 983048 | tf_op jit(solution)/shard_map/ppermute | solution.py:25
  51.3 17.4 %copy-start.1 = (bf16[1,4,8,5120]{3,2,1,0:T(8,128)(2,1)S(1)}, bf16[1,4,8,5120]{3,2,1,0:T(8,128)(2,1)}, u32[]{:S(2)}) copy-start(bf16[1,4,8,5120]{3,2,1,0:T(8,128)(2,1)} %param.9) | copy-start | bytes 983044
  51.5 24.1 %copy-start.3 = (bf16[8,5120]{1,0:T(8,128)(2,1)S(1)}, bf16[8,5120]{1,0:T(8,128)(2,1)}, u32[]{:S(2)}) copy-start(bf16[8,5120]{1,0:T(8,128)(2,1)} %param.12) | copy-start | bytes 245764
  51.5 10.1 %collective-permute-start.15 = (bf16[32,5120]{1,0:T(8,128)(2,1)S(1)}, bf16[32,5120]{1,0:T(8,128)(2,1)S(1)}, u32[]{:S(2)}, u32[]{:S(2)}) collective-permute-start(bf16[32,5120]{1,0:T(8,128)(2,1)S(1)} %pad_maximum_fusion), channel_id=1, source_target_pairs={{0,6},{1,7},{2,0},{3,1},{4,2},{5,3},{6,4},{7,5},{8,14},{9,15},{10,... | collective-permute-start | bytes 983048 | tf_op jit(solution)/shard_map/ppermute | solution.py:25
  57.8 10.2 %collective-permute-start.18 = (bf16[32,5120]{1,0:T(8,128)(2,1)S(1)}, bf16[32,5120]{1,0:T(8,128)(2,1)S(1)}, u32[]{:S(2)}, u32[]{:S(2)}) collective-permute-start(bf16[32,5120]{1,0:T(8,128)(2,1)S(1)} %pad_maximum_fusion.1), channel_id=1, source_target_pairs={{0,2},{1,3},{2,4},{3,5},{4,6},{5,7},{6,0},{7,1},{8,10},{9,11},{10,... | collective-permute-start | bytes 983048 | tf_op jit(solution)/shard_map/ppermute | solution.py:25
  58.5 10.2 %collective-permute-start.20 = (bf16[32,5120]{1,0:T(8,128)(2,1)S(1)}, bf16[32,5120]{1,0:T(8,128)(2,1)S(1)}, u32[]{:S(2)}, u32[]{:S(2)}) collective-permute-start(bf16[32,5120]{1,0:T(8,128)(2,1)S(1)} %add_convert_fusion.1), channel_id=1, source_target_pairs={{0,8},{1,9},{2,10},{3,11},{4,12},{5,13},{6,14},{7,15},{8,0},{9,1},... | collective-permute-start | bytes 983048 | tf_op jit(solution)/shard_map/ppermute | solution.py:25
  69.0 6.7 %copy-start.2 = (bf16[32,5120]{1,0:T(8,128)(2,1)}, bf16[32,5120]{1,0:T(8,128)(2,1)S(1)}, u32[]{:S(2)}) copy-start(bf16[32,5120]{1,0:T(8,128)(2,1)S(1)} %add_convert_fusion) | copy-start | bytes 983044
  69.0 6.6 %collective-permute-start.21 = (bf16[8,5120]{1,0:T(8,128)(2,1)S(1)}, bf16[8,5120]{1,0:T(8,128)(2,1)S(1)}, u32[]{:S(2)}, u32[]{:S(2)}) collective-permute-start(bf16[8,5120]{1,0:T(8,128)(2,1)S(1)} %dynamic-slice_bitcast_fusion), channel_id=1, source_target_pairs={{0,16},{16,32},{32,48},{48,64},{64,80},{80,96},{96,112},{112,0},{1... | collective-permute-start | bytes 245768 | tf_op jit(solution)/shard_map/ppermute | solution.py:31

commit v8 on v7

--- a/solution.py
+++ b/solution.py
@@ -8,6 +8,7 @@
 from jax.sharding import PartitionSpec as P
 
 HEAD_DIM = 128
+EXP2_SCALE = HEAD_DIM**-0.5 * 1.4426950408889634
 Z_CHIPS, X_CHIPS, CORES = 2, 4, 2
 MIB = 1 << 20
 ANY = pl.BlockSpec(memory_space=pl.ANY)
@@ -191,21 +192,35 @@
     return q, kv
 
 
-def attend(q_ref, kv_ref, attn_ref):
+def attend(q_ref, near_refs, far_refs, attn_ref):
     cols = q_ref.shape[2]
     contract = (((1,), (1,)), ((), ()))
     for owner in range(2):
+        parts = [(ref, 2 * owner) for ref in near_refs] + [(ref, 2 * (1 - owner)) for ref in far_refs]
         for at in range(0, cols, HEAD_DIM):
             span = slice(at, at + HEAD_DIM)
-            scores = lax.dot_general(
-                q_ref[owner, :, span], kv_ref[2 * owner, :, span], contract, preferred_element_type=jnp.float32
-            ) * HEAD_DIM ** (-0.5)
+            query = q_ref[owner, :, span]
+            scores = jnp.concatenate(
+                [
+                    lax.dot_general(query, ref[i, :, span], contract, preferred_element_type=jnp.float32)
+                    for ref, i in parts
+                ],
+                axis=1,
+            )
             top = jnp.max(scores, axis=-1, keepdims=True)
-            expo = jnp.exp(scores - top)
+            expo = jnp.exp2((scores - top) * EXP2_SCALE)
             total = jnp.sum(expo, axis=-1, keepdims=True)
-            prob = (expo * (1.0 / total)).astype(jnp.bfloat16)
-            value = jnp.dot(prob, kv_ref[2 * owner + 1, :, span], preferred_element_type=jnp.float32)
-            attn_ref[:, owner * cols + at : owner * cols + at + HEAD_DIM] = value.astype(jnp.bfloat16)
+            expo = expo.astype(jnp.bfloat16)
+            value, start = 0.0, 0
+            for ref, i in parts:
+                rows = ref.shape[1]
+                value += jnp.dot(
+                    expo[:, start : start + rows], ref[i + 1, :, span], preferred_element_type=jnp.float32
+                )
+                start += rows
+            attn_ref[:, owner * cols + at : owner * cols + at + HEAD_DIM] = (value * (1.0 / total)).astype(
+                jnp.bfloat16
+            )
 
 
 def out_project(attn_ref, w_mine, w_other, outs):
@@ -222,36 +237,19 @@
             at += out.shape[0]
 
 
-def far_kernel(pieces, q_b, kv_a, kv_b, far_a, far_b, w_mine, w_other, *refs):
-    outs, (kv_ref, attn_ref) = refs[:pieces], refs[pieces:]
-    cut, most = kv_a.shape[1], kv_b.shape[1]
-    half = cut + most
-    for owner in range(2):
-        for kind in range(2):
-            near, far = 2 * owner + kind, 2 * (1 - owner) + kind
-            kv_ref[near, :cut, :] = kv_a[near]
-            kv_ref[near, cut:half, :] = kv_b[near]
-            kv_ref[near, half : half + cut, :] = far_a[far]
-            kv_ref[near, half + cut :, :] = far_b[far]
-    attend(q_b, kv_ref, attn_ref)
+def attend_kernel(q_ref, kv_a, kv_b, far_a, far_b, w_mine, w_other, *refs):
+    outs, attn_ref = refs[:-1], refs[-1]
+    attend(q_ref, (kv_a, kv_b), (far_a, far_b), attn_ref)
     out_project(attn_ref, w_mine, w_other, outs)
 
 
-def near_kernel(pieces, q_ref, kv_ref, w_mine, w_other, *refs):
-    outs, attn_ref = refs[:pieces], refs[pieces]
-    attend(q_ref, kv_ref, attn_ref)
-    out_project(attn_ref, w_mine, w_other, outs)
-
-
-def attend_call(kernel, operands, w_mine, w_other, sizes, length, keys=None):
+def attend_call(operands, w_mine, w_other, sizes, length):
     cols, width = w_mine.shape
     total = sum(sizes)
     out_shape = [jax.ShapeDtypeStruct((rows, width), jnp.bfloat16) for rows in sizes]
-    if keys is not None:
-        out_shape = out_shape + [jax.ShapeDtypeStruct(keys, jnp.bfloat16)]
     in_vmem = lambda array: pltpu.with_memory_space_constraint(array, pltpu.VMEM)
     return pl.pallas_call(
-        functools.partial(kernel, len(sizes)),
+        attend_kernel,
         in_specs=[VMEM] * (len(operands) + 2),
         out_specs=[VMEM] * len(out_shape),
         out_shape=out_shape,
@@ -293,12 +291,12 @@
     far_a = hop(kv_a, dc=1)
     q_b, kv_b = rest_call([far_left, far_right, far_across, *across], gains, held, w_other)
     far_b = hop(kv_b, dc=1)
-    keys = (4, 16 * rows, kv_a.shape[2])
-    half = rows // 2
-    p_far_left, p_far_right, p_far_across, p_before, p_after, kv = attend_call(
-        far_kernel, (q_b, kv_a, kv_b, far_a, far_b), w_out, out_other, [rows] * 3 + [half] * 2, keys[1], keys
+    half, length = rows // 2, 16 * rows
+    keys = (kv_a, kv_b, far_a, far_b)
+    p_far_left, p_far_right, p_far_across, p_before, p_after = attend_call(
+        (q_b, *keys), w_out, out_other, [rows] * 3 + [half] * 2, length
     )
-    p_own, p_left, p_right, p_far = attend_call(near_kernel, (q_a, kv), w_out, out_other, [rows] * 4, keys[1])
+    p_own, p_left, p_right, p_far = attend_call((q_a, *keys), w_out, out_other, [rows] * 4, length)
 
     def add(a, b):
         return (a.astype(jnp.float32) + b.astype(jnp.float32)).astype(jnp.bfloat16)

time: 77.2 us -> 76.3 us (0.988)
  waiting for transfers between devices: 37 us -> 34.8 us
  starting transfers between devices: 23.1 us -> 24.4 us
    ppermute x21, waiting for transfers between devices: 32 us -> 29.8 us  [hop(): return lax.ppermute(value, 'seq', pairs)]
    ppermute x21, starting transfers between devices: 21.4 us -> 22.8 us  [hop(): return lax.ppermute(value, 'seq', pairs)]
where the time goes in v8:
time: 76.3 us; the launch traced here: 75.5 us
  waiting for transfers between devices  34.8 us (46%)
  starting transfers between devices  24.4 us (32%)
  Pallas kernels  13.2 us (17%)
  between operations  1.75 us (2%)
  other arithmetic  1.24 us (2%)
    ppermute x21, waiting for transfers between devices, hop(): return lax.ppermute(value, 'seq', pairs)  29.8 us
    ppermute x21, starting transfers between devices, hop(): return lax.ppermute(value, 'seq', pairs)  22.8 us
    ppermute x1, waiting for transfers between devices, from_behind(): return lax.ppermute(x, axis, pairs)  4.97 us
    pallas_call x2, Pallas kernels, attend_call(): pl.pallas_call(attend_kernel, in_specs=[VMEM] * (len(operands) + 2), out_...  4.8 us
    pallas_call x1, Pallas kernels, first_call(): pl.pallas_call(functools.partial(first_kernel, pieces), in_specs=[VMEM] *...  4.44 us
    ppermute x1, starting transfers between devices, from_behind(): return lax.ppermute(x, axis, pairs)  1.65 us
    pallas_call x1, Pallas kernels, rest_call(): pl.pallas_call(functools.partial(rest_keys_kernel, pieces), in_specs=[VME...  1.61 us
  transfers between devices with their start and end apart: 22, of which 11 were waited for; matrix products, arithmetic and copies ran while one was open for 1% of the time, Pallas kernels for 14%

profile of v8, /device:TPU:96, one launch (start us, length us, event | category | flops | bytes accessed | tf_op | source)
XLA Modules:
  0.0 75.5 jit_solution(12311036659226238056)
XLA Ops:
  0.0 0.0 copy-start
  0.0 0.0 collective-permute-start.3
  0.0 0.5 collective-permute-start.4
  1.4 1.4 %shard_map.91 = (bf16[32,5120]{1,0:T(8,128)(2,1)S(1)}, f32[1,5120]{1,0:T(1,128)S(1)}, f32[2,256]{1,0:T(2,128)S(1)}) custom-call(s32[1]{0:T(128)S(6)} %copy.11.step, bf16[32,5120]{1,0:T(8,128)(2,1)} %bitcast.17, f32[50,15360]{1,0:T(8,128)} %table.1, f32[1,256]{1,0:T(1,128)} %bitcast.21, f32[1,256]{1,0:T(1,128)} %bitcast.23), custom_call_target="tpu_custom_call" | custom-call | flops 1638400 | bytes 655360 | tf_op jit(solution)/shard_map/pallas_call | solution.py:60
  2.8 0.0 collective-permute-done.3.refs_5_.refs_1_
  2.8 0.0 collective-permute-done.4.refs_6_.refs_2_
  2.9 0.1 collective-permute-start.5
  2.9 1.6 %collective-permute-start = (bf16[32,5120]{1,0:T(8,128)(2,1)S(1)}, bf16[32,5120]{1,0:T(8,128)(2,1)S(1)}, u32[]{:S(2)}, u32[]{:S(2)}) collective-permute-start(bf16[32,5120]{1,0:T(8,128)(2,1)S(1)} %get-tuple-element.33.refs_0_), channel_id=1, source_target_pairs={{0,2},{1,3},{2,4},{3,5},{4,6},{5,7},{6,0},{7,1},{8,10},{9,11},{10,... | collective-permute-start | bytes 983048 | tf_op jit(solution)/shard_map/ppermute | solution.py:26
  4.5 1.7 %collective-permute-start.1 = (bf16[32,5120]{1,0:T(8,128)(2,1)S(1)}, bf16[32,5120]{1,0:T(8,128)(2,1)S(1)}, u32[]{:S(2)}, u32[]{:S(2)}) collective-permute-start(bf16[32,5120]{1,0:T(8,128)(2,1)S(1)} %get-tuple-element.33.refs_0_), channel_id=1, source_target_pairs={{0,6},{1,7},{2,0},{3,1},{4,2},{5,3},{6,4},{7,5},{8,14},{9,15},{10,... | collective-permute-start | bytes 983048 | tf_op jit(solution)/shard_map/ppermute | solution.py:26
  6.3 0.6 collective-permute-start.2
  6.8 7.5 %collective-permute-done.refs_1_ = bf16[32,5120]{1,0:T(8,128)(2,1)S(1)} collective-permute-done((bf16[32,5120]{1,0:T(8,128)(2,1)S(1)}, bf16[32,5120]{1,0:T(8,128)(2,1)S(1)}, u32[]{:S(2)}, u32[]{:S(2)}) %collective-permute-start) | collective-permute-done | bytes 327712 | tf_op jit(solution)/shard_map/ppermute | solution.py:26
  14.3 1.8 %collective-permute-start.9 = (bf16[32,5120]{1,0:T(8,128)(2,1)S(1)}, bf16[32,5120]{1,0:T(8,128)(2,1)S(1)}, u32[]{:S(2)}, u32[]{:S(2)}) collective-permute-start(bf16[32,5120]{1,0:T(8,128)(2,1)S(1)} %get-tuple-element.33.refs_0_), channel_id=1, source_target_pairs={{0,4},{1,5},{2,6},{3,7},{4,0},{5,1},{6,2},{7,3},{8,12},{9,13},{10,... | collective-permute-start | bytes 983048 | tf_op jit(solution)/shard_map/ppermute | solution.py:26
  16.1 0.6 collective-permute-start.6
  16.7 0.0 collective-permute-done.1.refs_2_
  16.7 3.0 %collective-permute-start.7 = (bf16[32,5120]{1,0:T(8,128)(2,1)S(1)}, bf16[32,5120]{1,0:T(8,128)(2,1)S(1)}, u32[]{:S(2)}, u32[]{:S(2)}) collective-permute-start(bf16[32,5120]{1,0:T(8,128)(2,1)S(1)} %collective-permute-done.1.refs_2_), channel_id=1, source_target_pairs={{0,8},{1,9},{2,10},{3,11},{4,12},{5,13},{6,14},{7,15},{8,0},{9,1},... | collective-permute-start | bytes 983048 | tf_op jit(solution)/shard_map/ppermute | solution.py:26
  19.6 0.0 collective-permute-done.2.refs_3_
  19.6 0.0 collective-permute-done.5.refs_8_.refs_4_
  19.6 1.7 %collective-permute-start.8 = (bf16[32,5120]{1,0:T(8,128)(2,1)S(1)}, bf16[32,5120]{1,0:T(8,128)(2,1)S(1)}, u32[]{:S(2)}, u32[]{:S(2)}) collective-permute-start(bf16[32,5120]{1,0:T(8,128)(2,1)S(1)} %collective-permute-done.2.refs_3_), channel_id=1, source_target_pairs={{0,4},{1,5},{2,6},{3,7},{4,0},{5,1},{6,2},{7,3},{8,12},{9,13},{10,... | collective-permute-start | bytes 983048 | tf_op jit(solution)/shard_map/ppermute | solution.py:26
  21.4 0.0 copy-done
  21.4 0.0 collective-permute-start.12
  21.4 4.4 %shard_map.92 = (bf16[2,128,256]{2,1,0:T(8,128)(2,1)S(1)}, bf16[4,128,256]{2,1,0:T(8,128)(2,1)S(1)}, bf16[3,5120,256]{2,1,0:T(8,128)(2,1)S(1)}) custom-call(bf16[32,5120]{1,0:T(8,128)(2,1)S(1)} %get-tuple-element.33.refs_0_, bf16[32,5120]{1,0:T(8,128)(2,1)S(1)} %collective-permute-done.refs_1_, bf16[32,5120]{1,0:T(8,128)(2,1)S(1)} %collective-permute-done.1.refs_2_, ...), custom_call_target="tpu_custom_call" | custom-call | flops 80530636800 | bytes 15728640 | tf_op jit(solution)/shard_map/pallas_call | solution.py:148
  25.8 2.4 %collective-permute-done.6.refs_0_ = bf16[32,5120]{1,0:T(8,128)(2,1)S(1)} collective-permute-done((bf16[32,5120]{1,0:T(8,128)(2,1)S(1)}, bf16[32,5120]{1,0:T(8,128)(2,1)S(1)}, u32[]{:S(2)}, u32[]{:S(2)}) %collective-permute-start.6) | collective-permute-done | bytes 327712 | tf_op jit(solution)/shard_map/ppermute | solution.py:26
  28.3 0.0 collective-permute-start.10
  28.3 5.4 %collective-permute-done.7.refs_1_ = bf16[32,5120]{1,0:T(8,128)(2,1)S(1)} collective-permute-done((bf16[32,5120]{1,0:T(8,128)(2,1)S(1)}, bf16[32,5120]{1,0:T(8,128)(2,1)S(1)}, u32[]{:S(2)}, u32[]{:S(2)}) %collective-permute-start.7) | collective-permute-done | bytes 327712 | tf_op jit(solution)/shard_map/ppermute | solution.py:26
  33.6 0.0 collective-permute-done.9.refs_3_
  33.6 0.0 collective-permute-done.8.refs_2_
  33.6 1.6 %shard_map.93 = (bf16[4,128,256]{2,1,0:T(8,128)(2,1)S(1)}, bf16[128,5120]{1,0:T(8,128)(2,1)S(1)}) custom-call(bf16[32,5120]{1,0:T(8,128)(2,1)S(1)} %collective-permute-done.6.refs_0_, bf16[32,5120]{1,0:T(8,128)(2,1)S(1)} %collective-permute-done.7.refs_1_, bf16[32,5120]{1,0:T(8,128)(2,1)S(1)} %collective-permute-done.8.refs_2_, ...), custom_call_target="tpu_custom_call" | custom-call | flops 1342177280 | bytes 10485760 | tf_op jit(solution)/shard_map/pallas_call | solution.py:176
  35.2 0.1 collective-permute-start.11
  35.3 1.0 %shard_map.95.q_ref = bf16[2,128,256]{2,1,0:T(8,128)(2,1)S(1)} custom-call(bf16[128,5120]{1,0:T(8,128)(2,1)S(1)} %get-tuple-element.39.rows_ref, f32[2,256]{1,0:T(2,128)S(1)} %get-tuple-element.28.refs_4_.refs_0_, f32[1,256]{1,0:T(1,128)S(1)} %collective-permute-done.3.refs_5_.refs_1_, f32[1,256]{1,0:T(1,128)S(1)} %collective-permute-done.4.refs_6_.refs_2_, ...), custom_call_target="tpu_custom_call" | custom-call | flops 671088640 | bytes 5242880 | tf_op jit(solution)/shard_map/pallas_call | solution.py:184
  36.3 0.0 collective-permute-done.10.far_a
  36.3 0.5 collective-permute-done.11.far_b
  36.8 0.0 collective-permute-done.12.w_other
  36.9 2.4 %shard_map.96 = (bf16[32,5120]{1,0:T(8,128)(2,1)S(1)}, bf16[32,5120]{1,0:T(8,128)(2,1)S(1)}, bf16[32,5120]{1,0:T(8,128)(2,1)S(1)}, bf16[16,5120]{1,0:T(8,128)(2,1)S(1)}, bf16[16,5120]{1,0:T(8,128)(2,1)S(1)}) custom-call(bf16[2,128,256]{2,1,0:T(8,128)(2,1)S(1)} %shard_map.95.q_ref, bf16[4,128,256]{2,1,0:T(8,128)(2,1)S(1)} %get-tuple-element.31.kv_a, ...), custom_call_target="tpu_custom_call" | custom-call | flops 805306368 | bytes 5242880 | tf_op jit(solution)/shard_map/pallas_call | solution.py:251
  39.3 1.8 %collective-permute-start.19 = (bf16[32,5120]{1,0:T(8,128)(2,1)S(1)}, bf16[32,5120]{1,0:T(8,128)(2,1)S(1)}, u32[]{:S(2)}, u32[]{:S(2)}) collective-permute-start(bf16[32,5120]{1,0:T(8,128)(2,1)S(1)} %get-tuple-element.46), channel_id=1, source_target_pairs={{0,4},{1,5},{2,6},{3,7},{4,0},{5,1},{6,2},{7,3},{8,12},{9,13},{10,... | collective-permute-start | bytes 983048 | tf_op jit(solution)/shard_map/ppermute | solution.py:26
  41.1 0.6 collective-permute-start.16
  41.6 0.3 collective-permute-start.17
  41.9 3.0 %collective-permute-start.13 = (bf16[32,5120]{1,0:T(8,128)(2,1)S(1)}, bf16[32,5120]{1,0:T(8,128)(2,1)S(1)}, u32[]{:S(2)}, u32[]{:S(2)}) collective-permute-start(bf16[32,5120]{1,0:T(8,128)(2,1)S(1)} %get-tuple-element.40), channel_id=1, source_target_pairs={{0,8},{1,9},{2,10},{3,11},{4,12},{5,13},{6,14},{7,15},{8,0},{9,1},... | collective-permute-start | bytes 983048 | tf_op jit(solution)/shard_map/ppermute | solution.py:26
  44.9 3.0 %collective-permute-start.14 = (bf16[16,5120]{1,0:T(8,128)(2,1)S(1)}, bf16[16,5120]{1,0:T(8,128)(2,1)S(1)}, u32[]{:S(2)}, u32[]{:S(2)}) collective-permute-start(bf16[16,5120]{1,0:T(8,128)(2,1)S(1)} %get-tuple-element.41), channel_id=1, source_target_pairs={{0,6},{1,7},{2,0},{3,1},{4,2},{5,3},{6,4},{7,5},{8,14},{9,15},{10,... | collective-permute-start | bytes 491528 | tf_op jit(solution)/shard_map/ppermute | solution.py:26
  47.8 2.4 %shard_map.94 = (bf16[32,5120]{1,0:T(8,128)(2,1)S(1)}, bf16[32,5120]{1,0:T(8,128)(2,1)S(1)}, bf16[32,5120]{1,0:T(8,128)(2,1)S(1)}, bf16[32,5120]{1,0:T(8,128)(2,1)S(1)}) custom-call(bf16[2,128,256]{2,1,0:T(8,128)(2,1)S(1)} %get-tuple-element.30.q_ref, bf16[4,128,256]{2,1,0:T(8,128)(2,1)S(1)} %get-tuple-element.31.kv_a, ...), custom_call_target="tpu_custom_call" | custom-call | flops 805306368 | bytes 5242880 | tf_op jit(solution)/shard_map/pallas_call | solution.py:251
  50.2 1.2 %collective-permute-done.19 = bf16[32,5120]{1,0:T(8,128)(2,1)S(1)} collective-permute-done((bf16[32,5120]{1,0:T(8,128)(2,1)S(1)}, bf16[32,5120]{1,0:T(8,128)(2,1)S(1)}, u32[]{:S(2)}, u32[]{:S(2)}) %collective-permute-start.19) | collective-permute-done | bytes 327712 | tf_op jit(solution)/shard_map/ppermute | solution.py:26
  51.4 0.0 copy-start.1
  51.4 0.1 add_convert_fusion.1
  51.5 0.6 collective-permute-start.20
  52.2 1.0 %collective-permute-done.16 = bf16[32,5120]{1,0:T(8,128)(2,1)S(1)} collective-permute-done((bf16[32,5120]{1,0:T(8,128)(2,1)S(1)}, bf16[32,5120]{1,0:T(8,128)(2,1)S(1)}, u32[]{:S(2)}, u32[]{:S(2)}) %collective-permute-start.16) | collective-permute-done | bytes 327712 | tf_op jit(solution)/shard_map/ppermute | solution.py:26
  53.1 0.1 convert_add_fusion
  53.2 0.0 copy-start.3
  53.3 0.8 %collective-permute-done.17 = bf16[16,5120]{1,0:T(8,128)(2,1)S(1)} collective-permute-done((bf16[16,5120]{1,0:T(8,128)(2,1)S(1)}, bf16[16,5120]{1,0:T(8,128)(2,1)S(1)}, u32[]{:S(2)}, u32[]{:S(2)}) %collective-permute-start.17) | collective-permute-done | bytes 163872 | tf_op jit(solution)/shard_map/ppermute | solution.py:26
  54.2 0.3 collective-permute-start.18
  54.5 5.7 %collective-permute-done.13 = bf16[32,5120]{1,0:T(8,128)(2,1)S(1)} collective-permute-done((bf16[32,5120]{1,0:T(8,128)(2,1)S(1)}, bf16[32,5120]{1,0:T(8,128)(2,1)S(1)}, u32[]{:S(2)}, u32[]{:S(2)}) %collective-permute-start.13) | collective-permute-done | bytes 327712 | tf_op jit(solution)/shard_map/ppermute | solution.py:26
  60.2 0.1 convert_add_fusion.1
  60.3 0.0 collective-permute-done.14
  60.4 1.6 %collective-permute-start.15 = (bf16[32,5120]{1,0:T(8,128)(2,1)S(1)}, bf16[32,5120]{1,0:T(8,128)(2,1)S(1)}, u32[]{:S(2)}, u32[]{:S(2)}) collective-permute-start(bf16[32,5120]{1,0:T(8,128)(2,1)S(1)} %pad_maximum_fusion), channel_id=1, source_target_pairs={{0,6},{1,7},{2,0},{3,1},{4,2},{5,3},{6,4},{7,5},{8,14},{9,15},{10,... | collective-permute-start | bytes 983048 | tf_op jit(solution)/shard_map/ppermute | solution.py:26
  62.6 3.4 %collective-permute-done.20 = bf16[32,5120]{1,0:T(8,128)(2,1)S(1)} collective-permute-done((bf16[32,5120]{1,0:T(8,128)(2,1)S(1)}, bf16[32,5120]{1,0:T(8,128)(2,1)S(1)}, u32[]{:S(2)}, u32[]{:S(2)}) %collective-permute-start.20) | collective-permute-done | bytes 327712 | tf_op jit(solution)/shard_map/ppermute | solution.py:26
  66.1 0.0 collective-permute-done.18
  66.1 1.8 %collective-permute-done.15 = bf16[32,5120]{1,0:T(8,128)(2,1)S(1)} collective-permute-done((bf16[32,5120]{1,0:T(8,128)(2,1)S(1)}, bf16[32,5120]{1,0:T(8,128)(2,1)S(1)}, u32[]{:S(2)}, u32[]{:S(2)}) %collective-permute-start.15) | collective-permute-done | bytes 327712 | tf_op jit(solution)/shard_map/ppermute | solution.py:26
  67.9 0.0 copy-done.1
  67.9 0.2 add_convert_fusion
  68.1 0.0 copy-start.2
  68.2 1.6 %collective-permute-start.21 = (bf16[8,5120]{1,0:T(8,128)(2,1)S(1)}, bf16[8,5120]{1,0:T(8,128)(2,1)S(1)}, u32[]{:S(2)}, u32[]{:S(2)}) collective-permute-start(bf16[8,5120]{1,0:T(8,128)(2,1)S(1)} %dynamic-slice_bitcast_fusion), channel_id=1, source_target_pairs={{0,16},{16,32},{32,48},{48,64},{64,80},{80,96},{96,112},{112,0},{1... | collective-permute-start | bytes 245768 | tf_op jit(solution)/shard_map/ppermute | solution.py:32
  69.8 5.0 %collective-permute-done.21 = bf16[8,5120]{1,0:T(8,128)(2,1)S(1)} collective-permute-done((bf16[8,5120]{1,0:T(8,128)(2,1)S(1)}, bf16[8,5120]{1,0:T(8,128)(2,1)S(1)}, u32[]{:S(2)}, u32[]{:S(2)}) %collective-permute-start.21) | collective-permute-done | bytes 81952 | tf_op jit(solution)/shard_map/ppermute | solution.py:32
  74.8 0.0 copy-done.2
  74.8 0.0 copy-done.3
  74.8 0.7 bitcast_dynamic-update-slice_fusion
  (7 shorter events, 0.2 us)
Async XLA Ops:
  0.0 21.4 %copy-start = (bf16[256,5120]{1,0:T(8,128)(2,1)S(1)}, bf16[256,5120]{1,0:T(8,128)(2,1)}, u32[]{:S(2)}) copy-start(bf16[256,5120]{1,0:T(8,128)(2,1)} %w_mine.3) | copy-start | bytes 7864324
  0.0 2.8 %collective-permute-start.3 = (f32[1,256]{1,0:T(1,128)}, f32[1,256]{1,0:T(1,128)S(1)}, u32[]{:S(2)}, u32[]{:S(2)}) collective-permute-start(f32[1,256]{1,0:T(1,128)} %bitcast.20), channel_id=1, source_target_pairs={{0,1},{1,0},{2,3},{3,2},{4,5},{5,4},{6,7},{7,6},{8,9},{9,8},{10,11... | collective-permute-start | bytes 3080 | tf_op jit(solution)/shard_map/ppermute | solution.py:26
  0.0 2.8 %collective-permute-start.4 = (f32[1,256]{1,0:T(1,128)}, f32[1,256]{1,0:T(1,128)S(1)}, u32[]{:S(2)}, u32[]{:S(2)}) collective-permute-start(f32[1,256]{1,0:T(1,128)} %bitcast.22), channel_id=1, source_target_pairs={{0,1},{1,0},{2,3},{3,2},{4,5},{5,4},{6,7},{7,6},{8,9},{9,8},{10,11... | collective-permute-start | bytes 3080 | tf_op jit(solution)/shard_map/ppermute | solution.py:26
  2.9 16.8 %collective-permute-start.5 = (bf16[3,5120,256]{2,1,0:T(8,128)(2,1)}, bf16[3,5120,256]{2,1,0:T(8,128)(2,1)S(1)}, u32[]{:S(2)}, u32[]{:S(2)}) collective-permute-start(bf16[3,5120,256]{2,1,0:T(8,128)(2,1)} %bitcast.24), channel_id=1, source_target_pairs={{0,1},{1,0},{2,3},{3,2},{4,5},{5,4},{6,7},{7,6},{8,9},{9,8},{10,11... | collective-permute-start | bytes 23592968 | tf_op jit(solution)/shard_map/ppermute | solution.py:26
  2.9 11.3 %collective-permute-start = (bf16[32,5120]{1,0:T(8,128)(2,1)S(1)}, bf16[32,5120]{1,0:T(8,128)(2,1)S(1)}, u32[]{:S(2)}, u32[]{:S(2)}) collective-permute-start(bf16[32,5120]{1,0:T(8,128)(2,1)S(1)} %get-tuple-element.33.refs_0_), channel_id=1, source_target_pairs={{0,2},{1,3},{2,4},{3,5},{4,6},{5,7},{6,0},{7,1},{8,10},{9,11},{10,... | collective-permute-start | bytes 983048 | tf_op jit(solution)/shard_map/ppermute | solution.py:26
  4.5 12.1 %collective-permute-start.1 = (bf16[32,5120]{1,0:T(8,128)(2,1)S(1)}, bf16[32,5120]{1,0:T(8,128)(2,1)S(1)}, u32[]{:S(2)}, u32[]{:S(2)}) collective-permute-start(bf16[32,5120]{1,0:T(8,128)(2,1)S(1)} %get-tuple-element.33.refs_0_), channel_id=1, source_target_pairs={{0,6},{1,7},{2,0},{3,1},{4,2},{5,3},{6,4},{7,5},{8,14},{9,15},{10,... | collective-permute-start | bytes 983048 | tf_op jit(solution)/shard_map/ppermute | solution.py:26
  6.3 13.4 %collective-permute-start.2 = (bf16[32,5120]{1,0:T(8,128)(2,1)S(1)}, bf16[32,5120]{1,0:T(8,128)(2,1)S(1)}, u32[]{:S(2)}, u32[]{:S(2)}) collective-permute-start(bf16[32,5120]{1,0:T(8,128)(2,1)S(1)} %get-tuple-element.33.refs_0_), channel_id=1, source_target_pairs={{0,8},{1,9},{2,10},{3,11},{4,12},{5,13},{6,14},{7,15},{8,0},{9,1},... | collective-permute-start | bytes 983048 | tf_op jit(solution)/shard_map/ppermute | solution.py:26
  14.3 19.3 %collective-permute-start.9 = (bf16[32,5120]{1,0:T(8,128)(2,1)S(1)}, bf16[32,5120]{1,0:T(8,128)(2,1)S(1)}, u32[]{:S(2)}, u32[]{:S(2)}) collective-permute-start(bf16[32,5120]{1,0:T(8,128)(2,1)S(1)} %get-tuple-element.33.refs_0_), channel_id=1, source_target_pairs={{0,4},{1,5},{2,6},{3,7},{4,0},{5,1},{6,2},{7,3},{8,12},{9,13},{10,... | collective-permute-start | bytes 983048 | tf_op jit(solution)/shard_map/ppermute | solution.py:26
  16.1 12.2 %collective-permute-start.6 = (bf16[32,5120]{1,0:T(8,128)(2,1)S(1)}, bf16[32,5120]{1,0:T(8,128)(2,1)S(1)}, u32[]{:S(2)}, u32[]{:S(2)}) collective-permute-start(bf16[32,5120]{1,0:T(8,128)(2,1)S(1)} %collective-permute-done.refs_1_), channel_id=1, source_target_pairs={{0,8},{1,9},{2,10},{3,11},{4,12},{5,13},{6,14},{7,15},{8,0},{9,1},... | collective-permute-start | bytes 983048 | tf_op jit(solution)/shard_map/ppermute | solution.py:26
  16.7 17.0 %collective-permute-start.7 = (bf16[32,5120]{1,0:T(8,128)(2,1)S(1)}, bf16[32,5120]{1,0:T(8,128)(2,1)S(1)}, u32[]{:S(2)}, u32[]{:S(2)}) collective-permute-start(bf16[32,5120]{1,0:T(8,128)(2,1)S(1)} %collective-permute-done.1.refs_2_), channel_id=1, source_target_pairs={{0,8},{1,9},{2,10},{3,11},{4,12},{5,13},{6,14},{7,15},{8,0},{9,1},... | collective-permute-start | bytes 983048 | tf_op jit(solution)/shard_map/ppermute | solution.py:26
  19.6 14.0 %collective-permute-start.8 = (bf16[32,5120]{1,0:T(8,128)(2,1)S(1)}, bf16[32,5120]{1,0:T(8,128)(2,1)S(1)}, u32[]{:S(2)}, u32[]{:S(2)}) collective-permute-start(bf16[32,5120]{1,0:T(8,128)(2,1)S(1)} %collective-permute-done.2.refs_3_), channel_id=1, source_target_pairs={{0,4},{1,5},{2,6},{3,7},{4,0},{5,1},{6,2},{7,3},{8,12},{9,13},{10,... | collective-permute-start | bytes 983048 | tf_op jit(solution)/shard_map/ppermute | solution.py:26
  21.4 15.5 %collective-permute-start.12 = (bf16[256,5120]{1,0:T(8,128)(2,1)S(1)}, bf16[256,5120]{1,0:T(8,128)(2,1)S(1)}, u32[]{:S(2)}, u32[]{:S(2)}) collective-permute-start(bf16[256,5120]{1,0:T(8,128)(2,1)S(1)} %copy-done), channel_id=1, source_target_pairs={{0,1},{1,0},{2,3},{3,2},{4,5},{5,4},{6,7},{7,6},{8,9},{9,8},{10,11... | collective-permute-start | bytes 7864328 | tf_op jit(solution)/shard_map/ppermute | solution.py:26
  28.3 8.1 %collective-permute-start.10 = (bf16[4,128,256]{2,1,0:T(8,128)(2,1)S(1)}, bf16[4,128,256]{2,1,0:T(8,128)(2,1)S(1)}, u32[]{:S(2)}, u32[]{:S(2)}) collective-permute-start(bf16[4,128,256]{2,1,0:T(8,128)(2,1)S(1)} %get-tuple-element.31.kv_a), channel_id=1, source_target_pairs={{0,1},{1,0},{2,3},{3,2},{4,5},{5,4},{6,7},{7,6},{8,9},{9,8},{10,11... | collective-permute-start | bytes 786440 | tf_op jit(solution)/shard_map/ppermute | solution.py:26
  35.2 1.6 %collective-permute-start.11 = (bf16[4,128,256]{2,1,0:T(8,128)(2,1)S(1)}, bf16[4,128,256]{2,1,0:T(8,128)(2,1)S(1)}, u32[]{:S(2)}, u32[]{:S(2)}) collective-permute-start(bf16[4,128,256]{2,1,0:T(8,128)(2,1)S(1)} %get-tuple-element.35.kv_b), channel_id=1, source_target_pairs={{0,1},{1,0},{2,3},{3,2},{4,5},{5,4},{6,7},{7,6},{8,9},{9,8},{10,11... | collective-permute-start | bytes 786440 | tf_op jit(solution)/shard_map/ppermute | solution.py:26
  39.3 12.2 %collective-permute-start.19 = (bf16[32,5120]{1,0:T(8,128)(2,1)S(1)}, bf16[32,5120]{1,0:T(8,128)(2,1)S(1)}, u32[]{:S(2)}, u32[]{:S(2)}) collective-permute-start(bf16[32,5120]{1,0:T(8,128)(2,1)S(1)} %get-tuple-element.46), channel_id=1, source_target_pairs={{0,4},{1,5},{2,6},{3,7},{4,0},{5,1},{6,2},{7,3},{8,12},{9,13},{10,... | collective-permute-start | bytes 983048 | tf_op jit(solution)/shard_map/ppermute | solution.py:26
  41.1 12.1 %collective-permute-start.16 = (bf16[32,5120]{1,0:T(8,128)(2,1)S(1)}, bf16[32,5120]{1,0:T(8,128)(2,1)S(1)}, u32[]{:S(2)}, u32[]{:S(2)}) collective-permute-start(bf16[32,5120]{1,0:T(8,128)(2,1)S(1)} %get-tuple-element.43), channel_id=1, source_target_pairs={{0,8},{1,9},{2,10},{3,11},{4,12},{5,13},{6,14},{7,15},{8,0},{9,1},... | collective-permute-start | bytes 983048 | tf_op jit(solution)/shard_map/ppermute | solution.py:26
  41.6 12.5 %collective-permute-start.17 = (bf16[16,5120]{1,0:T(8,128)(2,1)S(1)}, bf16[16,5120]{1,0:T(8,128)(2,1)S(1)}, u32[]{:S(2)}, u32[]{:S(2)}) collective-permute-start(bf16[16,5120]{1,0:T(8,128)(2,1)S(1)} %get-tuple-element.44), channel_id=1, source_target_pairs={{0,2},{1,3},{2,4},{3,5},{4,6},{5,7},{6,0},{7,1},{8,10},{9,11},{10,... | collective-permute-start | bytes 491528 | tf_op jit(solution)/shard_map/ppermute | solution.py:26
  41.9 18.3 %collective-permute-start.13 = (bf16[32,5120]{1,0:T(8,128)(2,1)S(1)}, bf16[32,5120]{1,0:T(8,128)(2,1)S(1)}, u32[]{:S(2)}, u32[]{:S(2)}) collective-permute-start(bf16[32,5120]{1,0:T(8,128)(2,1)S(1)} %get-tuple-element.40), channel_id=1, source_target_pairs={{0,8},{1,9},{2,10},{3,11},{4,12},{5,13},{6,14},{7,15},{8,0},{9,1},... | collective-permute-start | bytes 983048 | tf_op jit(solution)/shard_map/ppermute | solution.py:26
  44.9 15.4 %collective-permute-start.14 = (bf16[16,5120]{1,0:T(8,128)(2,1)S(1)}, bf16[16,5120]{1,0:T(8,128)(2,1)S(1)}, u32[]{:S(2)}, u32[]{:S(2)}) collective-permute-start(bf16[16,5120]{1,0:T(8,128)(2,1)S(1)} %get-tuple-element.41), channel_id=1, source_target_pairs={{0,6},{1,7},{2,0},{3,1},{4,2},{5,3},{6,4},{7,5},{8,14},{9,15},{10,... | collective-permute-start | bytes 491528 | tf_op jit(solution)/shard_map/ppermute | solution.py:26
  51.4 16.5 %copy-start.1 = (bf16[1,4,8,5120]{3,2,1,0:T(8,128)(2,1)S(1)}, bf16[1,4,8,5120]{3,2,1,0:T(8,128)(2,1)}, u32[]{:S(2)}) copy-start(bf16[1,4,8,5120]{3,2,1,0:T(8,128)(2,1)} %param.9) | copy-start | bytes 983044
  51.5 14.6 %collective-permute-start.20 = (bf16[32,5120]{1,0:T(8,128)(2,1)S(1)}, bf16[32,5120]{1,0:T(8,128)(2,1)S(1)}, u32[]{:S(2)}, u32[]{:S(2)}) collective-permute-start(bf16[32,5120]{1,0:T(8,128)(2,1)S(1)} %add_convert_fusion.1), channel_id=1, source_target_pairs={{0,8},{1,9},{2,10},{3,11},{4,12},{5,13},{6,14},{7,15},{8,0},{9,1},... | collective-permute-start | bytes 983048 | tf_op jit(solution)/shard_map/ppermute | solution.py:26
  53.2 21.6 %copy-start.3 = (bf16[8,5120]{1,0:T(8,128)(2,1)S(1)}, bf16[8,5120]{1,0:T(8,128)(2,1)}, u32[]{:S(2)}) copy-start(bf16[8,5120]{1,0:T(8,128)(2,1)} %param.12) | copy-start | bytes 245764
  54.2 11.9 %collective-permute-start.18 = (bf16[32,5120]{1,0:T(8,128)(2,1)S(1)}, bf16[32,5120]{1,0:T(8,128)(2,1)S(1)}, u32[]{:S(2)}, u32[]{:S(2)}) collective-permute-start(bf16[32,5120]{1,0:T(8,128)(2,1)S(1)} %pad_maximum_fusion.1), channel_id=1, source_target_pairs={{0,2},{1,3},{2,4},{3,5},{4,6},{5,7},{6,0},{7,1},{8,10},{9,11},{10,... | collective-permute-start | bytes 983048 | tf_op jit(solution)/shard_map/ppermute | solution.py:26
  60.4 7.6 %collective-permute-start.15 = (bf16[32,5120]{1,0:T(8,128)(2,1)S(1)}, bf16[32,5120]{1,0:T(8,128)(2,1)S(1)}, u32[]{:S(2)}, u32[]{:S(2)}) collective-permute-start(bf16[32,5120]{1,0:T(8,128)(2,1)S(1)} %pad_maximum_fusion), channel_id=1, source_target_pairs={{0,6},{1,7},{2,0},{3,1},{4,2},{5,3},{6,4},{7,5},{8,14},{9,15},{10,... | collective-permute-start | bytes 983048 | tf_op jit(solution)/shard_map/ppermute | solution.py:26
  68.1 6.7 %copy-start.2 = (bf16[32,5120]{1,0:T(8,128)(2,1)}, bf16[32,5120]{1,0:T(8,128)(2,1)S(1)}, u32[]{:S(2)}) copy-start(bf16[32,5120]{1,0:T(8,128)(2,1)S(1)} %add_convert_fusion) | copy-start | bytes 983044
  68.2 6.6 %collective-permute-start.21 = (bf16[8,5120]{1,0:T(8,128)(2,1)S(1)}, bf16[8,5120]{1,0:T(8,128)(2,1)S(1)}, u32[]{:S(2)}, u32[]{:S(2)}) collective-permute-start(bf16[8,5120]{1,0:T(8,128)(2,1)S(1)} %dynamic-slice_bitcast_fusion), channel_id=1, source_target_pairs={{0,16},{16,32},{32,48},{48,64},{64,80},{80,96},{96,112},{112,0},{1... | collective-permute-start | bytes 245768 | tf_op jit(solution)/shard_map/ppermute | solution.py:32
